TPU v7x, 256 devices: a whole 4x4x8 slice. The times are simulated.
256 devices in a mesh: slab: 128 (over y, x_lo, z, core), deg: 2 (over x_hi).
Axes of the slice: x: 4 (x_hi: 2, x_lo: 2; x = x_hi * 2 + x_lo), y: 4, z: 8, core: 2. Of those that a mesh axis runs over, the one named last changes fastest.
Arguments:
- harmonic: bfloat16 [131072, 52, 128], P('slab', 'deg'), may hold values from -6 to 6
- shell: int32 [131072], P('slab'), may hold values from 0 to 63
- atom_type: int32 [131072], P('slab'), may hold values from 0 to 7
- domain: int32 [131072], P('slab'), may hold values from 0 to 1
- form: float32 [8, 256], replicated, may hold values from 0.5 to 4
- bessel: float32 [64, 52, 256], P(None, 'deg'), may hold values from -1 to 1
- wigner: bfloat16 [512, 52, 128, 128], P('slab', 'deg'), may hold values from -0.5 to 0.5
Outputs:
- intensity: float32 [512, 256], P('slab')
All inputs are finite; a program needn't handle non-finite values.
Results may differ from a plain program's by a relative error of at most 0.004.
Values may be sent and summed in bfloat16 or wider, within the bound.
No kernel may reach another device: no remote copies, remote signals or barrier semaphores. Data moves between devices by JAX's collectives and lax.ppermute only.
A program may use at most 128 MiB of HBM per device.

v0:
```python
import jax
import jax.numpy as jnp
from jax import lax
from jax.sharding import PartitionSpec as P

L_DEG = 52
SHELLS = 64
TYPES = 8


def per_device(harmonic, shell, atom_type, domain, form, bessel, wigner):
    atom_rows = harmonic.shape[0]
    local_deg = harmonic.shape[1]
    width = harmonic.shape[2]
    qcount = form.shape[1]
    nkeys = 2 * SHELLS * TYPES
    total_atoms = atom_rows * lax.axis_size("slab")
    keys = (domain * SHELLS + shell) * TYPES + atom_type
    onehot = (keys[:, None] == jnp.arange(nkeys, dtype=jnp.int32)[None, :]).astype(jnp.bfloat16)
    binned = lax.dot_general(
        onehot,
        harmonic.reshape(atom_rows, local_deg * width),
        (((0,), (0,)), ((), ())),
        preferred_element_type=jnp.float32,
    )
    binned = binned.reshape(2, SHELLS * TYPES, local_deg, width)
    radial = (bessel[:, None, :, :] * form[None, :, None, :]).reshape(
        SHELLS * TYPES, local_deg, qcount
    )
    degree = lax.axis_index("deg") * local_deg + jnp.arange(local_deg, dtype=jnp.int32)
    mask = (jnp.arange(width, dtype=jnp.int32)[None, :] < 2 * degree[:, None] + 1).astype(
        jnp.float32
    )
    factor = mask[None, None] / jnp.sqrt(jnp.float32(total_atoms))
    term = jnp.einsum("dklm,klq->qdlm", binned, radial, precision=lax.Precision.HIGHEST)
    amplitude = lax.psum(term * factor, "slab").astype(jnp.bfloat16)
    first = amplitude[:, 0].astype(jnp.float32)
    turned = jnp.einsum(
        "qlk,rlmk->rqlm", amplitude[:, 1], wigner, preferred_element_type=jnp.float32
    )
    partial_int = jnp.sum(first[None] * turned, axis=(2, 3))
    intensity = lax.psum(partial_int, "deg")
    return intensity / L_DEG


def solution(mesh):
    in_specs = (
        P("slab", "deg", None),
        P("slab"),
        P("slab"),
        P("slab"),
        P(),
        P(None, "deg", None),
        P("slab", "deg", None, None),
    )
    out_specs = P("slab", None)
    return jax.shard_map(
        per_device, mesh=mesh, in_specs=in_specs, out_specs=out_specs, check_vma=False
    )
```

profile of v0, /device:TPU:1, one launch (start us, length us, event | category | flops | bytes accessed | tf_op | source)
XLA Modules:
  0.0 693.2 jit_solution(1720487432440025898)
XLA Ops:
  0.0 0.0 copy-start
  0.0 0.0 copy-start.4
  0.0 0.0 copy-start.3
  0.0 0.0 copy-start.2
  0.0 10.1 %copy.12 = bf16[1024,26,128]{0,2,1:T(8,128)(2,1)} copy(bf16[1024,26,128]{2,0,1:T(8,128)(2,1)} %param.7) | data formatting | bytes 13631488 | tf_op args[0]
  10.1 0.0 copy-done.4
  10.1 0.0 copy-done.3
  10.1 0.0 copy-done.2
  10.1 0.0 copy-start.1
  10.1 12.9 %fusion.3 = f32[2,512,26,128]{3,1,0,2:T(8,128)} fusion(bf16[1024,26,128]{0,2,1:T(8,128)(2,1)} %copy.12, s32[2,512]{1,0:T(2,128)S(1)} %multiply_add_fusion, s32[1024]{0:T(1024)S(1)} %multiply_add_fusion.1), kind=kOutput, calls=%fused_computation.5 | convolution fusion | flops 6980370432 | bytes 20455424 | tf_op jit(solution)/shard_map/dot_general | solution.py:20
  23.1 0.0 copy-done.1
  23.1 0.8 broadcast_bitcast_fusion
  23.9 0.1 fusion.15
  24.0 27.1 %multiply_bitcast_fusion = f32[256,2,26,128]{3,0,1,2:T(8,128)} fusion(f32[26,128]{1,0:T(8,128)S(1)} %fusion.15, f32[2,512,26,128]{3,1,0,2:T(8,128)} %fusion.3, f32[512,256]{1,0:T(8,128)} %broadcast_bitcast_fusion, f32[64,26,256]{2,0,1:T(8,128)} %param.12), kind=kOutput, calls=%fused_computation.7 | convolution fusion | flops 10474094592 | bytes 22688768 | tf_op jit(solution)/shard_map/dklm,klq->qdlm/dot_general | solution.py:35
  51.1 623.2 %all-reduce.1 = bf16[256,2,26,128]{3,0,1,2:T(8,128)(2,1)} all-reduce(f32[256,2,26,128]{3,0,1,2:T(8,128)} %multiply_bitcast_fusion), channel_id=1, replica_groups=mesh['slab'=128,'deg'=2] {'slab'}, use_global_device_ids=true, to_apply=%region_0.0 | all-reduce | flops 1703936 | bytes 10223616 | tf_op jit(solution)/shard_map/psum | solution.py:36
  674.2 3.6 fusion.14
  677.9 5.0 copy.14
  682.9 0.0 copy-done
  682.9 4.4 fusion.2
  687.3 5.3 psum.15
  692.6 0.6 broadcast_multiply_fusion
  (3 shorter events, 0.0 us)
Async XLA Ops:
  0.0 682.9 %copy-start = (bf16[4,26,128,128]{3,2,1,0:T(8,128)(2,1)S(1)}, bf16[4,26,128,128]{3,2,1,0:T(8,128)(2,1)}, u32[]{:S(2)}) copy-start(bf16[4,26,128,128]{3,2,1,0:T(8,128)(2,1)} %param.13) | copy-start | bytes 10223620
  0.0 10.1 %copy-start.4 = (s32[1024]{0:T(1024)S(1)}, s32[1024]{0:T(1024)}, u32[]{:S(2)}) copy-start(s32[1024]{0:T(1024)} %param.10) | copy-start | bytes 12292
  0.0 10.1 %copy-start.3 = (s32[1024]{0:T(1024)S(1)}, s32[1024]{0:T(1024)}, u32[]{:S(2)}) copy-start(s32[1024]{0:T(1024)} %param.8) | copy-start | bytes 12292
  0.0 10.1 %copy-start.2 = (s32[1024]{0:T(1024)S(1)}, s32[1024]{0:T(1024)}, u32[]{:S(2)}) copy-start(s32[1024]{0:T(1024)} %param.9) | copy-start | bytes 12292
  10.1 13.0 %copy-start.1 = (f32[8,256]{1,0:T(8,128)S(1)}, f32[8,256]{1,0:T(8,128)}, u32[]{:S(2)}) copy-start(f32[8,256]{1,0:T(8,128)} %param.11) | copy-start | bytes 24580
where the time goes:
time: 700 us; the launch traced here: 693 us
  blocking collectives  628 us (90%)
  matrix products  44.4 us (6%)
  local copies, waits for them, and re-layouts  16 us (2%)
    psum x1, blocking collectives, per_device(): amplitude = lax.psum(term * factor, 'slab').astype(jnp.bfloat16)  623 us
    dot_general x1, matrix products, per_device(): jnp.einsum('dklm,klq->qdlm', binned, radial, precision=lax.Precision.HIGH...  27.1 us

commit v1 on v0

v1 whole, which is shorter than its diff:
```python
import jax
import jax.numpy as jnp
from jax import lax
from jax.sharding import Mesh, PartitionSpec as P

SHELLS = 64
TYPES = 8
NEAR = ("y", "xl")
FAR = "z"


def widths(local_deg):
    rows = []
    for j in range(local_deg):
        live = 2 * (local_deg + j) + 1
        rows.append(-(-live // 16) * 16)
    return rows


def exchange(x, axis, parts):
    return lax.all_to_all(x.reshape(parts, x.shape[0] // parts, x.shape[1]), axis, 0, 0)


def spread(x, axis, parts):
    y = lax.all_to_all(jnp.broadcast_to(x[None], (parts,) + x.shape), axis, 0, 0)
    return y.reshape(parts * x.shape[0], x.shape[1])


def per_device(harmonic, shell, atom_type, domain, form, bessel, wigner):
    atom_rows, local_deg, width = harmonic.shape
    qcount = form.shape[1]
    total_atoms = atom_rows * 128
    nkeys = 2 * SHELLS * TYPES
    keys = (domain * SHELLS + shell) * TYPES + atom_type
    onehot = (keys[:, None] == jnp.arange(nkeys, dtype=jnp.int32)[None, :]).astype(jnp.bfloat16)
    binned = lax.dot_general(
        onehot,
        harmonic.reshape(atom_rows, local_deg * width),
        (((0,), (0,)), ((), ())),
        preferred_element_type=jnp.float32,
    )
    binned = binned.reshape(2, SHELLS * TYPES, local_deg, width)
    radial = (bessel[:, None, :, :] * form[None, :, None, :]).reshape(
        SHELLS * TYPES, local_deg, qcount
    )
    degree = lax.axis_index("deg") * local_deg + jnp.arange(local_deg, dtype=jnp.int32)
    mask = (jnp.arange(width, dtype=jnp.int32)[None, :] < 2 * degree[:, None] + 1).astype(
        jnp.float32
    )
    factor = mask[:, :, None, None] / jnp.sqrt(jnp.float32(total_atoms))
    term = jnp.einsum("dklm,klq->lmdq", binned, radial, precision=lax.Precision.HIGHEST)
    term = term * factor
    rows = widths(local_deg)
    live = sum(rows)
    total = -(-live // 256) * 256
    packed = jnp.concatenate(
        [term[j, :w] for j, w in enumerate(rows)]
        + [jnp.zeros((total - live, 2, qcount), jnp.float32)],
        axis=0,
    )
    core = lax.axis_index("c")
    swap = [(0, 1), (1, 0)]
    keep = jnp.where(core == 0, packed[:, 0], packed[:, 1])
    give = jnp.where(core == 0, packed[:, 1], packed[:, 0])
    part = keep + lax.ppermute(give, "c", swap)
    part = jnp.sum(exchange(part, NEAR, 8), axis=0)
    half = qcount // 2
    part = jnp.concatenate([part[:, :half], part[:, half:]], axis=0)
    part = jnp.sum(exchange(part, FAR, 8), axis=0)
    part = part.astype(jnp.bfloat16)
    part = spread(part, FAR, 8)
    deep = part.shape[0] // 2
    part = jnp.concatenate([part[:deep], part[deep:]], axis=1)
    mine = spread(part, NEAR, 8)
    other = lax.ppermute(mine, "c", swap)
    first = jnp.where(core == 0, mine, other)
    second = jnp.where(core == 0, other, mine)
    out = jnp.zeros((wigner.shape[0], qcount), jnp.float32)
    start = 0
    for j, w in enumerate(rows):
        a0 = first[start : start + w].astype(jnp.float32)
        a1 = second[start : start + w]
        turned = jnp.einsum(
            "rmk,kq->rmq", wigner[:, j, :w, :w], a1, preferred_element_type=jnp.float32
        )
        out = out + jnp.sum(a0[None] * turned, axis=1)
        start += w
    return lax.psum(out, "deg") / (2 * local_deg)


def solution(mesh):
    grid = Mesh(mesh.devices.reshape(4, 2, 8, 2, 2), ("y", "xl", "z", "c", "deg"))
    slab = ("y", "xl", "z", "c")
    in_specs = (
        P(slab, "deg", None),
        P(slab),
        P(slab),
        P(slab),
        P(),
        P(None, "deg", None),
        P(slab, "deg", None, None),
    )
    return jax.shard_map(
        per_device, mesh=grid, in_specs=in_specs, out_specs=P(slab, None), check_vma=False
    )
```

time: 700 us -> 172 us (0.25)
  blocking collectives: 628 us -> 83.4 us
  local copies, waits for them, and re-layouts: 16 us -> 28.5 us
  starting transfers between devices: 0 us -> 8.06 us
  matrix products: 44.4 us -> 37.2 us
    psum x2 -> x1, blocking collectives: 628 us -> 5.3 us  [per_device(): return lax.psum(out, 'deg') / (2 * local_deg)]
    all_to_all x0 -> x4, blocking collectives: none -> 78.1 us  [the longest x2 49.4 us: exchange(): lax.all_to_all(x.reshape(parts, x.shape[0] // parts, x.shape[1]), axis, 0...]
    dot_general x2 -> x26, matrix products: 31.5 us -> 5.15 us  [per_device(): jnp.einsum('rmk,kq->rmq', wigner[:, j, :w, :w], a1, preferred_element_typ...]
    unnamed x0 -> x1, matrix products: none -> 18.3 us
    unnamed x11 -> x41, local copies, waits for them, and re-layouts: 10.1 us -> 27.7 us
    ppermute x0 -> x2, starting transfers between devices: none -> 8.06 us  [the longest x1 4.74 us: per_device(): other = lax.ppermute(mine, 'c', swap)]
  transfers between devices with their start and end apart: 0 -> 2, of which waited for: 0 -> 2; matrix products, arithmetic and copies ran while one was open for 0% -> 0% of each run, Pallas kernels for 0% -> 0%
where the time goes in v1:
time: 172 us
  blocking collectives  83.4 us (48%)
  matrix products  37.2 us (22%)
  local copies, waits for them, and re-layouts  28.5 us (17%)
  starting transfers between devices  8.06 us (5%)
  other arithmetic  7.84 us (5%)
  waiting for transfers between devices  6.64 us (4%)
    all_to_all x2, blocking collectives, exchange(): lax.all_to_all(x.reshape(parts, x.shape[0] // parts, x.shape[1]), axis, 0...  49.4 us
    all_to_all x2, blocking collectives, spread(): lax.all_to_all(jnp.broadcast_to(x[None], (parts,) + x.shape), axis, 0, 0)  28.7 us
    unnamed x41, local copies, waits for them, and re-layouts  27.7 us
    unnamed x1, matrix products  18.3 us
    dot_general x1, matrix products, per_device(): lax.dot_general(onehot, harmonic.reshape(atom_rows, local_deg * width), (...  13.7 us
    psum x1, blocking collectives, per_device(): return lax.psum(out, 'deg') / (2 * local_deg)  5.3 us
    dot_general x26, matrix products, per_device(): jnp.einsum('rmk,kq->rmq', wigner[:, j, :w, :w], a1, preferred_element_typ...  5.15 us
    ppermute x1, starting transfers between devices, per_device(): other = lax.ppermute(mine, 'c', swap)  4.74 us
  transfers between devices with their start and end apart: 2, of which 2 were waited for; matrix products, arithmetic and copies ran while one was open for 0% of the time, Pallas kernels for 0%

profile of v1, /device:TPU:1, one launch (start us, length us, event | category | flops | bytes accessed | tf_op | source)
XLA Modules:
  0.0 171.9 jit_solution(12809660087568240827)
XLA Ops:
  0.1 9.9 %copy.61 = bf16[1024,26,128]{0,2,1:T(8,128)(2,1)} copy(bf16[1024,26,128]{2,0,1:T(8,128)(2,1)} %param.7) | data formatting | bytes 13631488 | tf_op args[0]
  10.1 13.7 %fusion.1 = f32[2,512,26,128]{1,3,0,2:T(8,128)} fusion(bf16[1024,26,128]{0,2,1:T(8,128)(2,1)} %copy.61, s32[2,512]{1,0:T(2,128)S(1)} %multiply_add_fusion, s32[1024]{0:T(1024)S(1)} %multiply_add_fusion.1), kind=kOutput, calls=%fused_computation.2 | convolution fusion | flops 6980370432 | bytes 20455424 | tf_op jit(solution)/shard_map/dot_general | solution.py:36
  23.9 18.3 %fusion = f32[26,256,256]{1,2,0:S(1)} fusion(f32[26,512,256]{1,2,0:T(8,128)} %bitcast.506, f32[512,256]{1,0:T(8,128)S(1)} %broadcast_bitcast_fusion, f32[64,26,256]{2,0,1:T(8,128)S(1)} %copy-done.2), kind=kOutput, calls=%fused_computation.1 | convolution fusion | flops 10472390656 | bytes 22675456
  42.2 0.8 multiply_bitcast_fusion
  43.0 0.7 fusion.34
  43.7 0.7 fusion.33
  44.4 0.7 fusion.32
  45.0 0.7 fusion.31
  45.7 0.6 fusion.30
  46.3 0.7 fusion.29
  47.0 0.7 fusion.28
  47.6 0.7 fusion.27
  48.3 0.7 fusion.26
  49.0 0.7 fusion.25
  49.7 0.7 fusion.24
  50.4 0.7 fusion.23
  51.1 0.7 fusion.22
  51.7 0.7 fusion.21
  52.4 0.7 fusion.20
  53.1 0.7 fusion.19
  53.8 0.7 fusion.18
  54.5 0.7 fusion.17
  55.2 0.7 fusion.16
  55.9 0.7 fusion.15
  56.5 0.7 fusion.14
  57.3 0.7 fusion.13
  58.0 0.7 fusion.12
  58.7 0.7 fusion.11
  59.4 0.7 fusion.10
  60.0 0.7 fusion.9
  60.8 0.7 broadcast_dynamic-update-slice_fusion
  61.4 2.7 %select_bitcast_fusion = f32[2304,256]{1,0:T(8,128)S(1)} fusion(f32[2304,2,256]{2,0,1:T(8,128)} %broadcast_dynamic-update-slice_fusion, pred[]{:T(512)S(6)} %eq.35), kind=kLoop, calls=%fused_computation.10 | loop fusion | flops 589824 | bytes 7077889 | tf_op jit(solution)/shard_map/jit(_where)/select_n | solution.py:64
  64.1 3.3 %collective-permute-start = (f32[2304,256]{1,0:T(8,128)S(1)}, f32[2304,256]{1,0:T(8,128)S(1)}, u32[]{:S(2)}, u32[]{:S(2)}) collective-permute-start(f32[2304,256]{1,0:T(8,128)S(1)} %select_bitcast_fusion), channel_id=1, source_target_pairs={{0,2},{2,0},{1,3},{3,1},{4,6},{6,4},{5,7},{7,5},{8,10},{10,8},{9,1... | collective-permute-start | bytes 7077896 | tf_op jit(solution)/shard_map/ppermute | solution.py:65
  67.4 4.2 %collective-permute-done = f32[2304,256]{1,0:T(8,128)S(1)} collective-permute-done((f32[2304,256]{1,0:T(8,128)S(1)}, f32[2304,256]{1,0:T(8,128)S(1)}, u32[]{:S(2)}, u32[]{:S(2)}) %collective-permute-start) | collective-permute-done | bytes 2359328 | tf_op jit(solution)/shard_map/ppermute | solution.py:65
  71.6 3.0 %bitcast_add_fusion = f32[2304,256]{1,0:T(8,128)S(1)} fusion(f32[2304,256]{1,0:T(8,128)S(1)} %collective-permute-done, f32[2304,2,256]{2,0,1:T(8,128)} %broadcast_dynamic-update-slice_fusion, pred[]{:T(512)S(6)} %eq.35), kind=kLoop, calls=%fused_computation.9 | loop fusion | flops 1179648 | bytes 9437185 | tf_op jit(solution)/shard_map/add | solution.py:65
  74.6 32.1 %all_to_all.20 = f32[8,288,256]{2,1,0:T(8,128)S(1)} all-to-all(f32[8,288,256]{2,1,0:T(8,128)S(1)} %bitcast.507), channel_id=1, replica_groups=mesh['y'=4,'xl'=2,'z'=8,'c'=2,'deg'=2] {'y','xl'}, dimensions={0} | all-to-all | bytes 4718592 | tf_op jit(solution)/shard_map/all_to_all | solution.py:21
  106.9 17.3 %all_to_all.21 = f32[8,72,128]{2,1,0:T(8,128)S(1)} all-to-all(f32[8,72,128]{2,1,0:T(8,128)S(1)} %bitcast.509), channel_id=1, replica_groups=mesh['y'=4,'xl'=2,'z'=8,'c'=2,'deg'=2] {'z'}, dimensions={0} | all-to-all | bytes 589824 | tf_op jit(solution)/shard_map/all_to_all | solution.py:21
  124.2 11.7 %all_to_all.22 = bf16[8,72,128]{2,1,0:T(8,128)(2,1)S(1)} all-to-all(bf16[8,72,128]{2,1,0:T(8,128)(2,1)S(1)} %broadcast_in_dim.7), channel_id=1, replica_groups=mesh['y'=4,'xl'=2,'z'=8,'c'=2,'deg'=2] {'z'}, dimensions={0} | all-to-all | bytes 294912 | tf_op jit(solution)/shard_map/all_to_all | solution.py:25
  136.0 17.0 %all_to_all.23 = bf16[8,288,256]{2,1,0:T(8,128)(2,1)S(1)} all-to-all(bf16[8,288,256]{2,1,0:T(8,128)(2,1)S(1)} %broadcast_in_dim.8), channel_id=1, replica_groups=mesh['y'=4,'xl'=2,'z'=8,'c'=2,'deg'=2] {'y','xl'}, dimensions={0} | all-to-all | bytes 2359296 | tf_op jit(solution)/shard_map/all_to_all | solution.py:25
  153.1 4.7 %collective-permute-start.1 = (bf16[2304,256]{1,0:T(8,128)(2,1)S(1)}, bf16[2304,256]{1,0:T(8,128)(2,1)S(1)}, u32[]{:S(2)}, u32[]{:S(2)}) collective-permute-start(bf16[2304,256]{1,0:T(8,128)(2,1)S(1)} %bitcast.508), channel_id=1, source_target_pairs={{0,2},{2,0},{1,3},{3,1},{4,6},{6,4},{5,7},{7,5},{8,10},{10,8},{9,1... | collective-permute-start | bytes 3538952 | tf_op jit(solution)/shard_map/ppermute | solution.py:75
  157.8 2.5 %collective-permute-done.1 = bf16[2304,256]{1,0:T(8,128)(2,1)S(1)} collective-permute-done((bf16[2304,256]{1,0:T(8,128)(2,1)S(1)}, bf16[2304,256]{1,0:T(8,128)(2,1)S(1)}, u32[]{:S(2)}, u32[]{:S(2)}) %collective-permute-start.1) | collective-permute-done | bytes 1179680 | tf_op jit(solution)/shard_map/ppermute | solution.py:75
  160.3 0.2 broadcast_select_fusion
  160.7 0.2 multiply_reduce_fusion
  161.0 0.2 multiply_reduce_fusion.1
  161.2 0.2 multiply_reduce_fusion.2
  161.4 0.2 multiply_reduce_fusion.3
  166.0 5.3 %psum.7 = f32[4,256]{1,0:T(4,128)S(1)} all-reduce(f32[4,256]{1,0:T(4,128)S(1)} %add_add_fusion), channel_id=1, replica_groups=mesh['y'=4,'xl'=2,'z'=8,'c'=2,'deg'=2] {'deg'}, use_global_device_ids=true, to_apply=%region_28.29 | all-reduce | flops 1024 | bytes 8192 | tf_op jit(solution)/shard_map/psum | solution.py:88
  171.3 0.6 broadcast_multiply_fusion
  (54 shorter events, 5.0 us)
Async XLA Ops:
  0.0 10.0 %copy-start = (f32[8,256]{1,0:T(8,128)S(1)}, f32[8,256]{1,0:T(8,128)}, u32[]{:S(2)}) copy-start(f32[8,256]{1,0:T(8,128)} %param.11) | copy-start | bytes 24580
  0.0 10.1 %copy-start.3 = (s32[1024]{0:T(1024)S(1)}, s32[1024]{0:T(1024)}, u32[]{:S(2)}) copy-start(s32[1024]{0:T(1024)} %param.9) | copy-start | bytes 12292
  0.0 10.1 %copy-start.4 = (s32[1024]{0:T(1024)S(1)}, s32[1024]{0:T(1024)}, u32[]{:S(2)}) copy-start(s32[1024]{0:T(1024)} %param.8) | copy-start | bytes 12292
  0.0 10.1 %copy-start.5 = (s32[1024]{0:T(1024)S(1)}, s32[1024]{0:T(1024)}, u32[]{:S(2)}) copy-start(s32[1024]{0:T(1024)} %param.10) | copy-start | bytes 12292
  10.1 13.8 %copy-start.2 = (f32[64,26,256]{2,0,1:T(8,128)S(1)}, f32[64,26,256]{2,0,1:T(8,128)}, u32[]{:S(2)}) copy-start(f32[64,26,256]{2,0,1:T(8,128)} %param.12) | copy-start | bytes 5111812
  64.1 7.5 %collective-permute-start = (f32[2304,256]{1,0:T(8,128)S(1)}, f32[2304,256]{1,0:T(8,128)S(1)}, u32[]{:S(2)}, u32[]{:S(2)}) collective-permute-start(f32[2304,256]{1,0:T(8,128)S(1)} %select_bitcast_fusion), channel_id=1, source_target_pairs={{0,2},{2,0},{1,3},{3,1},{4,6},{6,4},{5,7},{7,5},{8,10},{10,8},{9,1... | collective-permute-start | bytes 7077896 | tf_op jit(solution)/shard_map/ppermute | solution.py:65
  153.1 7.7 %copy-start.6 = (bf16[4,26,128,128]{3,2,1,0:T(8,128)(2,1)S(1)}, bf16[4,26,128,128]{3,2,1,0:T(8,128)(2,1)}, u32[]{:S(2)}) copy-start(bf16[4,26,128,128]{3,2,1,0:T(8,128)(2,1)} %param.13) | copy-start | bytes 10223620
  153.1 7.2 %collective-permute-start.1 = (bf16[2304,256]{1,0:T(8,128)(2,1)S(1)}, bf16[2304,256]{1,0:T(8,128)(2,1)S(1)}, u32[]{:S(2)}, u32[]{:S(2)}) collective-permute-start(bf16[2304,256]{1,0:T(8,128)(2,1)S(1)} %bitcast.508), channel_id=1, source_target_pairs={{0,2},{2,0},{1,3},{3,1},{4,6},{6,4},{5,7},{7,5},{8,10},{10,8},{9,1... | collective-permute-start | bytes 3538952 | tf_op jit(solution)/shard_map/ppermute | solution.py:75
  161.4 10.5 %copy-start.1 = (f32[8,256]{1,0:T(8,128)S(1)}, f32[8,256]{1,0:T(8,128)}, u32[]{:S(2)}) copy-start(f32[8,256]{1,0:T(8,128)} %param.11) | copy-start | bytes 24580

commit v2 on v1

v2 whole, which is shorter than its diff:
```python
import functools
import jax
import jax.numpy as jnp
from jax import lax
from jax.experimental import pallas as pl
from jax.experimental.pallas import tpu as pltpu
from jax.sharding import Mesh, PartitionSpec as P

SHELLS = 64
TYPES = 8
BINS = SHELLS * TYPES
NEAR = ("y", "xl")
FAR = "z"


def widths(local_deg):
    return [-(-(2 * (local_deg + j) + 1) // 16) * 16 for j in range(local_deg)]


def start_of(local, rows):
    return sum(jnp.where(local > j, w, 0) for j, w in enumerate(rows[:-1]))


def wide_of(local, rows):
    cuts = [j for j in range(1, len(rows)) if rows[j] != rows[j - 1]]
    return rows[0] + sum(jnp.where(local >= j, rows[j] - rows[j - 1], 0) for j in cuts)


def contract_first(a, b):
    return lax.dot_general(a, b, (((0,), (0,)), ((), ())), preferred_element_type=jnp.float32)


def amplitude_kernel(pair, scale, rows, place, keys, harmonic, bessel, form, keep, give, onehot):
    step = pl.program_id(0)

    @pl.when(step == 0)
    def _():
        slots = lax.broadcasted_iota(jnp.int32, onehot.shape, 0)
        onehot[...] = jnp.where(slots == keys[...], 1.0, 0.0).astype(jnp.bfloat16)
        keep[...] = jnp.zeros_like(keep)
        give[...] = jnp.zeros_like(give)

    both = jnp.concatenate([harmonic[i] for i in range(pair)], axis=1)
    binned = jnp.dot(onehot[...], both, preferred_element_type=jnp.float32)
    width = harmonic.shape[2]
    for i in range(pair):
        mine = binned[:, i * width : (i + 1) * width]
        cols = jnp.concatenate([mine[:BINS], mine[BINS:]], axis=1)
        cols_hi = cols.astype(jnp.bfloat16)
        cols_lo = (cols - cols_hi.astype(jnp.float32)).astype(jnp.bfloat16)
        radial = (bessel[i][:, None, :] * form[...][None]).reshape(BINS, form.shape[1])
        radial_hi = radial.astype(jnp.bfloat16)
        radial_lo = (radial - radial_hi.astype(jnp.float32)).astype(jnp.bfloat16)
        out = contract_first(cols_hi, radial_hi)
        out = out + contract_first(cols_lo, radial_hi)
        out = out + contract_first(cols_hi, radial_lo)
        local = step * pair + i
        live = 2 * (place[0] + local) + 1
        order = lax.broadcasted_iota(jnp.int32, (width, out.shape[1]), 0)
        at = pl.ds(pl.multiple_of(start_of(local, rows), 16), width)
        keep[at, :] = jnp.where(order < live, out[:width] * scale, 0.0)
        give[at, :] = jnp.where(order < live, out[width:] * scale, 0.0)


def local_amplitude(place, keys, harmonic, bessel, form, total, pair, scale, rows):
    degs, atoms, width = harmonic.shape
    qcount = form.shape[1]
    out = jax.ShapeDtypeStruct((total, qcount), jnp.float32)
    grid_spec = pltpu.PrefetchScalarGridSpec(
        num_scalar_prefetch=1,
        grid=(degs // pair,),
        in_specs=[
            pl.BlockSpec((1, atoms), lambda s, *_: (0, 0)),
            pl.BlockSpec((pair, atoms, width), lambda s, *_: (s, 0, 0)),
            pl.BlockSpec((pair, SHELLS, qcount), lambda s, *_: (s, 0, 0)),
            pl.BlockSpec((TYPES, qcount), lambda s, *_: (0, 0)),
        ],
        out_specs=[pl.BlockSpec((total, qcount), lambda s, *_: (0, 0))] * 2,
        scratch_shapes=[pltpu.VMEM((2 * BINS, atoms), jnp.bfloat16)],
    )
    return pl.pallas_call(
        functools.partial(amplitude_kernel, pair, scale, rows),
        grid_spec=grid_spec,
        out_shape=[out, out],
        compiler_params=pltpu.CompilerParams(vmem_limit_bytes=40 * 2**20),
        cost_estimate=pl.CostEstimate(
            flops=2 * degs * width * (2 * BINS * atoms + 6 * BINS * qcount),
            bytes_accessed=harmonic.size * 2 + bessel.size * 4,
            transcendentals=0,
        ),
    )(place, keys, harmonic, bessel, form)


def turn_kernel(group, steps, rows, place, mine, other, wigner, out, acc):
    step = pl.program_id(0)
    rots, width = wigner.shape[0], wigner.shape[2]
    qcount = mine.shape[1]

    @pl.when(step == 0)
    def _():
        acc[...] = jnp.zeros_like(acc)

    order = lax.broadcasted_iota(jnp.int32, (width, qcount), 0)
    swap = jnp.broadcast_to(place[1], (width, qcount)) == 1
    for i in range(group):
        local = step * group + i
        at = pl.ds(pl.multiple_of(start_of(local, rows), 16), width)
        inside = order < wide_of(local, rows)
        here = jnp.where(inside, mine[at, :].astype(jnp.float32), 0.0)
        there = jnp.where(inside, other[at, :].astype(jnp.float32), 0.0)
        first = jnp.where(swap, there, here)
        second = jnp.where(swap, here, there).astype(jnp.bfloat16)
        blocks = wigner[:, i].reshape(rots * width, width)
        turned = jnp.dot(blocks, second, preferred_element_type=jnp.float32)
        for r in range(rots):
            prod = turned[r * width : (r + 1) * width] * first
            acc[r] += jnp.sum(prod.reshape(width // 8, 8, qcount), axis=0)

    @pl.when(step == steps - 1)
    def _():
        out[...] = jnp.sum(acc[...], axis=1) * (0.5 / (steps * group))


def local_intensity(place, mine, other, wigner, group, rows):
    rots, degs, width, _ = wigner.shape
    total, qcount = mine.shape
    grid_spec = pltpu.PrefetchScalarGridSpec(
        num_scalar_prefetch=1,
        grid=(degs // group,),
        in_specs=[
            pl.BlockSpec((total, qcount), lambda s, *_: (0, 0)),
            pl.BlockSpec((total, qcount), lambda s, *_: (0, 0)),
            pl.BlockSpec((rots, group, width, width), lambda s, *_: (0, s, 0, 0)),
        ],
        out_specs=pl.BlockSpec((rots, qcount), lambda s, *_: (0, 0)),
        scratch_shapes=[pltpu.VMEM((rots, 8, qcount), jnp.float32)],
    )
    return pl.pallas_call(
        functools.partial(turn_kernel, group, degs // group, rows),
        grid_spec=grid_spec,
        out_shape=jax.ShapeDtypeStruct((rots, qcount), jnp.float32),
        compiler_params=pltpu.CompilerParams(vmem_limit_bytes=40 * 2**20),
        cost_estimate=pl.CostEstimate(
            flops=2 * wigner.size * qcount,
            bytes_accessed=wigner.size * 2 + mine.size * 4,
            transcendentals=0,
        ),
    )(place, mine, other, wigner)


def coded(x, spare):
    top = jnp.maximum(jnp.max(jnp.abs(x), axis=0, keepdims=True), 1e-30)
    power = jnp.floor(jnp.log2(top)) + 1.0
    steps = jnp.clip(jnp.round(x * jnp.exp2(15.0 - power)), -32767.0, 32767.0)
    tail = jnp.broadcast_to(power, (spare, x.shape[1]))
    return jnp.concatenate([steps, tail], axis=0).astype(jnp.int32).astype(jnp.int16)


def decoded(block, rows):
    wide = block.astype(jnp.int32).astype(jnp.float32)
    return wide[:rows] * jnp.exp2(wide[rows : rows + 1] - 15.0)


def near_kernel(keep, recv, out):
    out[0] = coded(keep[...] + recv[...], out.shape[1] - keep.shape[0])


def far_kernel(parts, rows, near, out):
    total = decoded(near[0], rows)
    for i in range(1, near.shape[0]):
        total = total + decoded(near[i], rows)
    half = total.shape[1] // 2
    piece = rows * 2 // parts
    for i in range(parts):
        side, row = divmod(i * piece, rows)
        block = total[row : row + piece, side * half : (side + 1) * half]
        out[i] = coded(block, out.shape[1] - piece)


def last_kernel(far, out):
    total = decoded(far[0], out.shape[0])
    for i in range(1, far.shape[0]):
        total = total + decoded(far[i], out.shape[0])
    out[...] = total


def near_parts(keep, recv, parts):
    total, lanes = keep.shape
    rows = total // parts
    spare = 32 - rows % 16 if rows % 16 else 16
    return pl.pallas_call(
        near_kernel,
        grid=(parts,),
        in_specs=[pl.BlockSpec((rows, lanes), lambda s: (s, 0))] * 2,
        out_specs=pl.BlockSpec((1, rows + spare, lanes), lambda s: (s, 0, 0)),
        out_shape=jax.ShapeDtypeStruct((parts, rows + spare, lanes), jnp.int16),
    )(keep, recv), rows


def far_parts(near, rows, parts):
    piece = rows * 2 // parts
    return pl.pallas_call(
        functools.partial(far_kernel, parts, rows),
        out_shape=jax.ShapeDtypeStruct((parts, piece + 8, near.shape[2] // 2), jnp.int16),
        compiler_params=pltpu.CompilerParams(vmem_limit_bytes=40 * 2**20),
    )(near), piece


def last_sum(far, piece):
    return pl.pallas_call(
        last_kernel,
        out_shape=jax.ShapeDtypeStruct((piece, far.shape[2]), jnp.float32),
    )(far)


def exchange(x, axis):
    return lax.all_to_all(x, axis, 0, 0)


def spread(x, axis, parts):
    y = lax.all_to_all(jnp.broadcast_to(x[None], (parts,) + x.shape), axis, 0, 0)
    return y.reshape(parts * x.shape[0], x.shape[1])


def per_device(harmonic, shell, atom_type, domain, form, bessel, wigner):
    atom_rows, local_deg, width = harmonic.shape
    rows = widths(local_deg)
    total = -(-sum(rows) // 256) * 256
    core = lax.axis_index("c")
    swap = [(0, 1), (1, 0)]
    place = jnp.stack([lax.axis_index("deg") * local_deg, core]).astype(jnp.int32)
    side = jnp.where(core == 0, domain, 1 - domain)
    keys = ((side * SHELLS + shell) * TYPES + atom_type)[None]
    keep, give = local_amplitude(
        place,
        keys,
        harmonic.transpose(1, 0, 2),
        bessel.transpose(1, 0, 2),
        form,
        total,
        2,
        (atom_rows * 128) ** -0.5,
        rows,
    )
    near, height = near_parts(keep, lax.ppermute(give, "c", swap), 8)
    far, piece = far_parts(exchange(near, NEAR), height, 8)
    part = last_sum(exchange(far, FAR), piece).astype(jnp.bfloat16)
    part = spread(part, FAR, 8)
    deep = part.shape[0] // 2
    part = jnp.concatenate([part[:deep], part[deep:]], axis=1)
    mine = spread(part, NEAR, 8)
    other = lax.ppermute(mine, "c", swap)
    out = local_intensity(place, mine, other, wigner, 2, rows)
    return out + lax.ppermute(out, "deg", swap)


def solution(mesh):
    grid = Mesh(mesh.devices.reshape(4, 2, 8, 2, 2), ("y", "xl", "z", "c", "deg"))
    slab = ("y", "xl", "z", "c")
    in_specs = (
        P(slab, "deg", None),
        P(slab),
        P(slab),
        P(slab),
        P(),
        P(None, "deg", None),
        P(slab, "deg", None, None),
    )
    return jax.shard_map(
        per_device, mesh=grid, in_specs=in_specs, out_specs=P(slab, None), check_vma=False
    )
```

time: 172 us -> 134 us (0.78)
  Pallas kernels: 0 us -> 40.8 us
  matrix products: 37.2 us -> 0 us
  blocking collectives: 83.4 us -> 62.9 us
  local copies, waits for them, and re-layouts: 28.5 us -> 8.01 us
  other arithmetic: 7.84 us -> 2.19 us
  starting transfers between devices: 8.06 us -> 11.2 us
    pallas_call x0 -> x5, Pallas kernels: none -> 40.8 us  [the longest x1 27 us: local_amplitude(): pl.pallas_call(functools.partial(amplitude_kernel, pair, scale, rows), gr...]
    unnamed x41 -> x12, local copies, waits for them, and re-layouts: 27.7 us -> 7.9 us
    dot_general x27 -> x0, matrix products: 18.9 us -> none  [the longest x1 13.7 us: per_device(): lax.dot_general(onehot, harmonic.reshape(atom_rows, local_deg * width), (...]
    unnamed x1 -> x0, matrix products: 18.3 us -> none
    all_to_all x2, blocking collectives: 49.4 us -> 37.1 us  [exchange(): return lax.all_to_all(x, axis, 0, 0)]
    psum x1 -> x0, blocking collectives: 5.3 us -> none  [per_device(): return lax.psum(out, 'deg') / (2 * local_deg)]
    select_n x2 -> x0, other arithmetic: 2.91 us -> none  [the longest x1 2.68 us: per_device(): give = jnp.where(core == 0, packed[:, 1], packed[:, 0])]
    all_to_all x2, blocking collectives: 28.7 us -> 25.9 us  [spread(): lax.all_to_all(jnp.broadcast_to(x[None], (parts,) + x.shape), axis, 0, 0)]
  transfers between devices with their start and end apart: 2 -> 3, of which waited for: 2 -> 3; matrix products, arithmetic and copies ran while one was open for 0% -> 0% of each run, Pallas kernels for 0% -> 0%
where the time goes in v2:
time: 134 us; the launch traced here: 133 us
  blocking collectives  62.9 us (47%)
  Pallas kernels  40.8 us (30%)
  starting transfers between devices  11.2 us (8%)
  waiting for transfers between devices  8.15 us (6%)
  local copies, waits for them, and re-layouts  8.01 us (6%)
  other arithmetic  2.19 us (2%)
    all_to_all x2, blocking collectives, exchange(): return lax.all_to_all(x, axis, 0, 0)  37.1 us
    pallas_call x1, Pallas kernels, local_amplitude(): pl.pallas_call(functools.partial(amplitude_kernel, pair, scale, rows), gr...  27 us
    all_to_all x2, blocking collectives, spread(): lax.all_to_all(jnp.broadcast_to(x[None], (parts,) + x.shape), axis, 0, 0)  25.9 us
    unnamed x12, local copies, waits for them, and re-layouts  7.9 us
    pallas_call x1, Pallas kernels, near_parts(): pl.pallas_call(near_kernel, grid=(parts,), in_specs=[pl.BlockSpec((rows,...  6.21 us
    pallas_call x1, Pallas kernels, local_intensity(): pl.pallas_call(functools.partial(turn_kernel, group, degs // group, rows)...  5.55 us
    ppermute x1, starting transfers between devices, per_device(): other = lax.ppermute(mine, 'c', swap)  5.47 us
    ppermute x1, waiting for transfers between devices, per_device(): near, height = near_parts(keep, lax.ppermute(give, 'c', swap), 8)  4.16 us
  transfers between devices with their start and end apart: 3, of which 3 were waited for; matrix products, arithmetic and copies ran while one was open for 0% of the time, Pallas kernels for 0%

profile of v2, /device:TPU:1, one launch (start us, length us, event | category | flops | bytes accessed | tf_op | source)
XLA Modules:
  0.0 133.4 jit_solution(1564014430095826354)
XLA Ops:
  0.0 0.1 pad_add_fusion.place
  0.1 0.7 fusion.3
  0.8 0.0 copy-start.2
  0.8 2.9 %copy-done.2 = bf16[1024,26,128]{2,0,1:T(8,128)(2,1)S(1)} copy-done((bf16[1024,26,128]{2,0,1:T(8,128)(2,1)S(1)}, bf16[1024,26,128]{2,0,1:T(8,128)(2,1)}, u32[]{:S(2)}) %copy-start.2) | copy-done | bytes 6815768
  3.7 0.0 copy-start.3
  3.7 1.5 %copy-done.3 = f32[64,26,256]{2,0,1:T(8,128)S(1)} copy-done((f32[64,26,256]{2,0,1:T(8,128)S(1)}, f32[64,26,256]{2,0,1:T(8,128)}, u32[]{:S(2)}) %copy-start.3) | copy-done | bytes 1703960
  5.2 0.0 copy-start.4
  5.2 0.7 copy-done.4
  5.9 27.0 %shard_map.73 = (f32[2304,256]{1,0:T(8,128)S(1)}, f32[2304,256]{1,0:T(8,128)S(1)}) custom-call(s32[2]{0:T(128)S(1)} %pad_add_fusion.place, s32[1,1024]{1,0:T(1,128)S(1)} %bitcast.10, bf16[26,1024,128]{2,1,0:T(8,128)(2,1)S(1)} %bitcast.11, f32[26,64,256]{2,1,0:T(8,128)S(1)} %bitcast.12, f32[8,256]{1,0:T(8,128)S(1)} %copy-done.4), custom_call_target="tpu_custom_call" | custom-call | flops 12213813248 | bytes 8519680 | tf_op jit(solution)/shard_map/pallas_call | solution.py:81
  32.9 0.0 copy-start.1
  32.9 1.4 %copy-done.1 = f32[2304,256]{1,0:T(8,128)} copy-done((f32[2304,256]{1,0:T(8,128)}, f32[2304,256]{1,0:T(8,128)S(1)}, u32[]{:S(2)}) %copy-start.1) | copy-done | bytes 2359320
  34.3 3.2 %collective-permute-start = (f32[2304,256]{1,0:T(8,128)S(1)}, f32[2304,256]{1,0:T(8,128)S(1)}, u32[]{:S(2)}, u32[]{:S(2)}) collective-permute-start(f32[2304,256]{1,0:T(8,128)S(1)} %get-tuple-element.8), channel_id=1, source_target_pairs={{0,2},{2,0},{1,3},{3,1},{4,6},{6,4},{5,7},{7,5},{8,10},{10,8},{9,1... | collective-permute-start | bytes 7077896 | tf_op jit(solution)/shard_map/ppermute | solution.py:245
  37.5 4.2 %collective-permute-done.recv = f32[2304,256]{1,0:T(8,128)S(1)} collective-permute-done((f32[2304,256]{1,0:T(8,128)S(1)}, f32[2304,256]{1,0:T(8,128)S(1)}, u32[]{:S(2)}, u32[]{:S(2)}) %collective-permute-start) | collective-permute-done | bytes 2359328 | tf_op jit(solution)/shard_map/ppermute | solution.py:245
  41.7 0.0 copy-start.5
  41.7 1.4 %copy-done.5 = f32[2304,256]{1,0:T(8,128)} copy-done((f32[2304,256]{1,0:T(8,128)}, f32[2304,256]{1,0:T(8,128)S(1)}, u32[]{:S(2)}) %copy-start.5) | copy-done | bytes 2359320
  43.1 6.2 %shard_map.74 = s16[8,304,256]{2,1,0:T(8,128)(2,1)} custom-call(f32[2304,256]{1,0:T(8,128)} %copy-done.1, f32[2304,256]{1,0:T(8,128)} %copy-done.5), custom_call_target="tpu_custom_call" | custom-call | tf_op jit(solution)/shard_map/pallas_call | solution.py:191
  49.3 20.7 %all_to_all.20.near = s16[8,304,256]{2,1,0:T(8,128)(2,1)S(1)} all-to-all(s16[8,304,256]{2,1,0:T(8,128)(2,1)} %shard_map.74), channel_id=1, replica_groups=mesh['y'=4,'xl'=2,'z'=8,'c'=2,'deg'=2] {'y','xl'}, dimensions={0} | all-to-all | bytes 2490368 | tf_op jit(solution)/shard_map/all_to_all | solution.py:217
  70.0 0.5 shard_map.75
  70.6 16.3 %all_to_all.21.far = s16[8,80,128]{2,1,0:T(8,128)(2,1)} all-to-all(s16[8,80,128]{2,1,0:T(8,128)(2,1)S(1)} %shard_map.75), channel_id=1, replica_groups=mesh['y'=4,'xl'=2,'z'=8,'c'=2,'deg'=2] {'z'}, dimensions={0} | all-to-all | bytes 327680 | tf_op jit(solution)/shard_map/all_to_all | solution.py:217
  86.9 1.6 %shard_map.76 = f32[72,128]{1,0:T(8,128)} custom-call(s16[8,80,128]{2,1,0:T(8,128)(2,1)} %all_to_all.21.far), custom_call_target="tpu_custom_call" | custom-call | tf_op jit(solution)/shard_map/pallas_call | solution.py:210
  88.5 0.8 convert_element_type.3
  89.3 10.5 %all_to_all.22 = bf16[8,72,128]{2,1,0:T(8,128)(2,1)S(1)} all-to-all(bf16[8,72,128]{2,1,0:T(8,128)(2,1)S(1)} %broadcast_in_dim.7), channel_id=1, replica_groups=mesh['y'=4,'xl'=2,'z'=8,'c'=2,'deg'=2] {'z'}, dimensions={0} | all-to-all | bytes 294912 | tf_op jit(solution)/shard_map/all_to_all | solution.py:221
  99.8 0.0 copy-start
  99.8 0.1 broadcast_in_dim.8
  99.9 15.4 %all_to_all.23 = bf16[8,288,256]{2,1,0:T(8,128)(2,1)S(1)} all-to-all(bf16[8,288,256]{2,1,0:T(8,128)(2,1)S(1)} %broadcast_in_dim.8), channel_id=1, replica_groups=mesh['y'=4,'xl'=2,'z'=8,'c'=2,'deg'=2] {'y','xl'}, dimensions={0} | all-to-all | bytes 2359296 | tf_op jit(solution)/shard_map/all_to_all | solution.py:221
  115.3 5.5 %collective-permute-start.1 = (bf16[2304,256]{1,0:T(8,128)(2,1)S(1)}, bf16[2304,256]{1,0:T(8,128)(2,1)S(1)}, u32[]{:S(2)}, u32[]{:S(2)}) collective-permute-start(bf16[2304,256]{1,0:T(8,128)(2,1)S(1)} %bitcast.8), channel_id=1, source_target_pairs={{0,2},{2,0},{1,3},{3,1},{4,6},{6,4},{5,7},{7,5},{8,10},{10,8},{9,1... | collective-permute-start | bytes 3538952 | tf_op jit(solution)/shard_map/ppermute | solution.py:252
  120.7 2.5 %collective-permute-done.1.other = bf16[2304,256]{1,0:T(8,128)(2,1)S(1)} collective-permute-done((bf16[2304,256]{1,0:T(8,128)(2,1)S(1)}, bf16[2304,256]{1,0:T(8,128)(2,1)S(1)}, u32[]{:S(2)}, u32[]{:S(2)}) %collective-permute-start.1) | collective-permute-done | bytes 1179680 | tf_op jit(solution)/shard_map/ppermute | solution.py:252
  123.2 0.0 copy-done
  123.2 5.6 %shard_map.77 = f32[4,256]{1,0:T(4,128)S(1)} custom-call(s32[2]{0:T(128)S(1)} %pad_add_fusion.place, bf16[2304,256]{1,0:T(8,128)(2,1)S(1)} %bitcast.9, bf16[2304,256]{1,0:T(8,128)(2,1)S(1)} %collective-permute-done.1.other, bf16[4,26,128,128]{3,2,1,0:T(8,128)(2,1)S(1)} %copy-done), custom_call_target="tpu_custom_call" | custom-call | flops 872415232 | bytes 5767168 | tf_op jit(solution)/shard_map/pallas_call | solution.py:138
  128.8 2.5 %collective-permute-start.2 = (f32[4,256]{1,0:T(4,128)S(1)}, f32[4,256]{1,0:T(4,128)S(1)}, u32[]{:S(2)}, u32[]{:S(2)}) collective-permute-start(f32[4,256]{1,0:T(4,128)S(1)} %shard_map.77), channel_id=1, source_target_pairs={{0,1},{1,0},{2,3},{3,2},{4,5},{5,4},{6,7},{7,6},{8,9},{9,8},{10,11... | collective-permute-start | bytes 12296 | tf_op jit(solution)/shard_map/ppermute | solution.py:254
  131.3 1.5 %collective-permute-done.2 = f32[4,256]{1,0:T(4,128)S(1)} collective-permute-done((f32[4,256]{1,0:T(4,128)S(1)}, f32[4,256]{1,0:T(4,128)S(1)}, u32[]{:S(2)}, u32[]{:S(2)}) %collective-permute-start.2) | collective-permute-done | bytes 4128 | tf_op jit(solution)/shard_map/ppermute | solution.py:254
  132.8 0.6 add.11
  (3 shorter events, 0.1 us)
Async XLA Ops:
  0.8 2.9 %copy-start.2 = (bf16[1024,26,128]{2,0,1:T(8,128)(2,1)S(1)}, bf16[1024,26,128]{2,0,1:T(8,128)(2,1)}, u32[]{:S(2)}) copy-start(bf16[1024,26,128]{2,0,1:T(8,128)(2,1)} %param.7) | copy-start | bytes 20447236
  3.7 1.5 %copy-start.3 = (f32[64,26,256]{2,0,1:T(8,128)S(1)}, f32[64,26,256]{2,0,1:T(8,128)}, u32[]{:S(2)}) copy-start(f32[64,26,256]{2,0,1:T(8,128)} %param.12) | copy-start | bytes 5111812
  5.2 0.7 copy-start.4
  32.9 1.4 %copy-start.1 = (f32[2304,256]{1,0:T(8,128)}, f32[2304,256]{1,0:T(8,128)S(1)}, u32[]{:S(2)}) copy-start(f32[2304,256]{1,0:T(8,128)S(1)} %get-tuple-element.7.keep) | copy-start | bytes 7077892
  34.3 7.4 %collective-permute-start = (f32[2304,256]{1,0:T(8,128)S(1)}, f32[2304,256]{1,0:T(8,128)S(1)}, u32[]{:S(2)}, u32[]{:S(2)}) collective-permute-start(f32[2304,256]{1,0:T(8,128)S(1)} %get-tuple-element.8), channel_id=1, source_target_pairs={{0,2},{2,0},{1,3},{3,1},{4,6},{6,4},{5,7},{7,5},{8,10},{10,8},{9,1... | collective-permute-start | bytes 7077896 | tf_op jit(solution)/shard_map/ppermute | solution.py:245
  41.7 1.4 %copy-start.5 = (f32[2304,256]{1,0:T(8,128)}, f32[2304,256]{1,0:T(8,128)S(1)}, u32[]{:S(2)}) copy-start(f32[2304,256]{1,0:T(8,128)S(1)} %collective-permute-done.recv) | copy-start | bytes 7077892
  99.8 23.4 %copy-start = (bf16[4,26,128,128]{3,2,1,0:T(8,128)(2,1)S(1)}, bf16[4,26,128,128]{3,2,1,0:T(8,128)(2,1)}, u32[]{:S(2)}) copy-start(bf16[4,26,128,128]{3,2,1,0:T(8,128)(2,1)} %wigner.1) | copy-start | bytes 10223620
  115.3 7.9 %collective-permute-start.1 = (bf16[2304,256]{1,0:T(8,128)(2,1)S(1)}, bf16[2304,256]{1,0:T(8,128)(2,1)S(1)}, u32[]{:S(2)}, u32[]{:S(2)}) collective-permute-start(bf16[2304,256]{1,0:T(8,128)(2,1)S(1)} %bitcast.8), channel_id=1, source_target_pairs={{0,2},{2,0},{1,3},{3,1},{4,6},{6,4},{5,7},{7,5},{8,10},{10,8},{9,1... | collective-permute-start | bytes 3538952 | tf_op jit(solution)/shard_map/ppermute | solution.py:252
  128.8 4.0 %collective-permute-start.2 = (f32[4,256]{1,0:T(4,128)S(1)}, f32[4,256]{1,0:T(4,128)S(1)}, u32[]{:S(2)}, u32[]{:S(2)}) collective-permute-start(f32[4,256]{1,0:T(4,128)S(1)} %shard_map.77), channel_id=1, source_target_pairs={{0,1},{1,0},{2,3},{3,2},{4,5},{5,4},{6,7},{7,6},{8,9},{9,8},{10,11... | collective-permute-start | bytes 12296 | tf_op jit(solution)/shard_map/ppermute | solution.py:254

commit v3 on v2

--- a/solution.py
+++ b/solution.py
@@ -9,8 +9,10 @@
 SHELLS = 64
 TYPES = 8
 BINS = SHELLS * TYPES
-NEAR = ("y", "xl")
-FAR = "z"
+NEAR = ("y", "xl", "zl")
+FAR = "zh"
+PLANE = 16
+LIMIT = 8
 
 
 def widths(local_deg):
@@ -75,14 +77,14 @@
             pl.BlockSpec((pair, SHELLS, qcount), lambda s, *_: (s, 0, 0)),
             pl.BlockSpec((TYPES, qcount), lambda s, *_: (0, 0)),
         ],
-        out_specs=[pl.BlockSpec((total, qcount), lambda s, *_: (0, 0))] * 2,
+        out_specs=[pl.BlockSpec(memory_space=pltpu.VMEM)] * 2,
         scratch_shapes=[pltpu.VMEM((2 * BINS, atoms), jnp.bfloat16)],
     )
     return pl.pallas_call(
         functools.partial(amplitude_kernel, pair, scale, rows),
         grid_spec=grid_spec,
         out_shape=[out, out],
-        compiler_params=pltpu.CompilerParams(vmem_limit_bytes=40 * 2**20),
+        compiler_params=pltpu.CompilerParams(vmem_limit_bytes=56 * 2**20),
         cost_estimate=pl.CostEstimate(
             flops=2 * degs * width * (2 * BINS * atoms + 6 * BINS * qcount),
             bytes_accessed=harmonic.size * 2 + bessel.size * 4,
@@ -161,69 +163,43 @@
     return wide[:rows] * jnp.exp2(wide[rows : rows + 1] - 15.0)
 
 
-def near_kernel(keep, recv, out):
-    out[0] = coded(keep[...] + recv[...], out.shape[1] - keep.shape[0])
-
-
-def far_kernel(parts, rows, near, out):
-    total = decoded(near[0], rows)
+def near_kernel(rows, keep, recv, out):
+    for i in range(out.shape[0]):
+        at = pl.ds(i * rows, rows)
+        out[i] = coded(keep[at, :] + recv[at, :], out.shape[1] - rows)
+
+
+def plane_kernel(rows, near, total, code):
+    acc = decoded(near[0], rows)
     for i in range(1, near.shape[0]):
-        total = total + decoded(near[i], rows)
-    half = total.shape[1] // 2
-    piece = rows * 2 // parts
-    for i in range(parts):
-        side, row = divmod(i * piece, rows)
-        block = total[row : row + piece, side * half : (side + 1) * half]
-        out[i] = coded(block, out.shape[1] - piece)
-
-
-def last_kernel(far, out):
-    total = decoded(far[0], out.shape[0])
-    for i in range(1, far.shape[0]):
-        total = total + decoded(far[i], out.shape[0])
-    out[...] = total
-
-
-def near_parts(keep, recv, parts):
-    total, lanes = keep.shape
-    rows = total // parts
-    spare = 32 - rows % 16 if rows % 16 else 16
+        acc = acc + decoded(near[i], rows)
+    total[...] = acc
+    code[...] = coded(acc, code.shape[0] - rows)
+
+
+def whole_kernel(total, after, before, across, out):
+    rows = total.shape[0]
+    acc = total[...] + decoded(across[...], rows)
+    acc = acc + (decoded(after[...], rows) + decoded(before[...], rows))
+    block = acc.astype(jnp.bfloat16)
+    for i in range(out.shape[0]):
+        out[i] = block
+
+
+def whole_call(body, out_shape, limit, *args):
+    spec = pl.BlockSpec(memory_space=pltpu.VMEM)
     return pl.pallas_call(
-        near_kernel,
-        grid=(parts,),
-        in_specs=[pl.BlockSpec((rows, lanes), lambda s: (s, 0))] * 2,
-        out_specs=pl.BlockSpec((1, rows + spare, lanes), lambda s: (s, 0, 0)),
-        out_shape=jax.ShapeDtypeStruct((parts, rows + spare, lanes), jnp.int16),
-    )(keep, recv), rows
-
-
-def far_parts(near, rows, parts):
-    piece = rows * 2 // parts
-    return pl.pallas_call(
-        functools.partial(far_kernel, parts, rows),
-        out_shape=jax.ShapeDtypeStruct((parts, piece + 8, near.shape[2] // 2), jnp.int16),
-        compiler_params=pltpu.CompilerParams(vmem_limit_bytes=40 * 2**20),
-    )(near), piece
-
-
-def last_sum(far, piece):
-    return pl.pallas_call(
-        last_kernel,
-        out_shape=jax.ShapeDtypeStruct((piece, far.shape[2]), jnp.float32),
-    )(far)
-
-
-def exchange(x, axis):
-    return lax.all_to_all(x, axis, 0, 0)
-
-
-def spread(x, axis, parts):
-    y = lax.all_to_all(jnp.broadcast_to(x[None], (parts,) + x.shape), axis, 0, 0)
-    return y.reshape(parts * x.shape[0], x.shape[1])
+        body,
+        in_specs=[spec] * len(args),
+        out_specs=jax.tree.map(lambda _: spec, out_shape),
+        out_shape=out_shape,
+        compiler_params=pltpu.CompilerParams(vmem_limit_bytes=limit * 2**20),
+    )(*args)
 
 
 def per_device(harmonic, shell, atom_type, domain, form, bessel, wigner):
     atom_rows, local_deg, width = harmonic.shape
+    qcount = form.shape[1]
     rows = widths(local_deg)
     total = -(-sum(rows) // 256) * 256
     core = lax.axis_index("c")
@@ -242,21 +218,43 @@
         (atom_rows * 128) ** -0.5,
         rows,
     )
-    near, height = near_parts(keep, lax.ppermute(give, "c", swap), 8)
-    far, piece = far_parts(exchange(near, NEAR), height, 8)
-    part = last_sum(exchange(far, FAR), piece).astype(jnp.bfloat16)
-    part = spread(part, FAR, 8)
-    deep = part.shape[0] // 2
-    part = jnp.concatenate([part[:deep], part[deep:]], axis=1)
-    mine = spread(part, NEAR, 8)
+    recv = lax.ppermute(give, "c", swap)
+    height = total // PLANE
+    coded_shape = (height + 16, qcount)
+    near = whole_call(
+        functools.partial(near_kernel, height),
+        jax.ShapeDtypeStruct((PLANE,) + coded_shape, jnp.int16),
+        LIMIT,
+        keep,
+        recv,
+    )
+    near = lax.all_to_all(near, NEAR, 0, 0)
+    part, code = whole_call(
+        functools.partial(plane_kernel, height),
+        [
+            jax.ShapeDtypeStruct((height, qcount), jnp.float32),
+            jax.ShapeDtypeStruct(coded_shape, jnp.int16),
+        ],
+        LIMIT,
+        near,
+    )
+    turns = [lax.ppermute(code, FAR, [(i, (i + k) % 4) for i in range(4)]) for k in (1, 3, 2)]
+    spread = whole_call(
+        whole_kernel,
+        jax.ShapeDtypeStruct((PLANE, height, qcount), jnp.bfloat16),
+        LIMIT,
+        part,
+        *turns,
+    )
+    mine = lax.all_to_all(spread, NEAR, 0, 0).reshape(total, qcount)
     other = lax.ppermute(mine, "c", swap)
     out = local_intensity(place, mine, other, wigner, 2, rows)
     return out + lax.ppermute(out, "deg", swap)
 
 
 def solution(mesh):
-    grid = Mesh(mesh.devices.reshape(4, 2, 8, 2, 2), ("y", "xl", "z", "c", "deg"))
-    slab = ("y", "xl", "z", "c")
+    grid = Mesh(mesh.devices.reshape(4, 2, 4, 2, 2, 2), ("y", "xl", "zh", "zl", "c", "deg"))
+    slab = ("y", "xl", "zh", "zl", "c")
     in_specs = (
         P(slab, "deg", None),
         P(slab),

time: 134 us -> 115 us (0.86)
  blocking collectives: 62.9 us -> 42.9 us
  local copies, waits for them, and re-layouts: 8.01 us -> 1.67 us
  starting transfers between devices: 11.2 us -> 17.4 us
  waiting for transfers between devices: 8.15 us -> 12.8 us
  Pallas kernels: 40.8 us -> 37 us
    all_to_all x4 -> x2, blocking collectives: 62.9 us -> 42.9 us  [the longest x1 21.6 us: per_device(): near = lax.all_to_all(near, NEAR, 0, 0)]
    ppermute x1 -> x4, starting transfers between devices: 3.24 us -> 11.7 us  [the longest x3 8.46 us: per_device(): lax.ppermute(code, FAR, [(i, (i + k) % 4) for i in range(4)])]
    pallas_call x3, Pallas kernels: 8.32 us -> 1.01 us  [whole_call(): pl.pallas_call(body, in_specs=[spec] * len(args), out_specs=jax.tree.map(...]
    unnamed x12 -> x6, local copies, waits for them, and re-layouts: 7.9 us -> 1.67 us
    ppermute x1 -> x4, waiting for transfers between devices: 4.16 us -> 8.86 us  [the longest x3 4.49 us: per_device(): lax.ppermute(code, FAR, [(i, (i + k) % 4) for i in range(4)])]
    pallas_call x1, Pallas kernels: 27 us -> 30.4 us  [local_amplitude(): pl.pallas_call(functools.partial(amplitude_kernel, pair, scale, rows), gr...]
    ppermute x1, starting transfers between devices: 5.47 us -> 3.16 us  [per_device(): other = lax.ppermute(mine, 'c', swap)]
  transfers between devices with their start and end apart: 3 -> 6, of which waited for: 3 -> 4; matrix products, arithmetic and copies ran while one was open for 0% -> 0% of each run, Pallas kernels for 0% -> 0%
where the time goes in v3:
time: 115 us; the launch traced here: 114 us
  blocking collectives  42.9 us (37%)
  Pallas kernels  37 us (32%)
  starting transfers between devices  17.4 us (15%)
  waiting for transfers between devices  12.8 us (11%)
  other arithmetic  2.56 us (2%)
  local copies, waits for them, and re-layouts  1.67 us (1%)
    pallas_call x1, Pallas kernels, local_amplitude(): pl.pallas_call(functools.partial(amplitude_kernel, pair, scale, rows), gr...  30.4 us
    all_to_all x1, blocking collectives, per_device(): near = lax.all_to_all(near, NEAR, 0, 0)  21.6 us
    all_to_all x1, blocking collectives, per_device(): mine = lax.all_to_all(spread, NEAR, 0, 0).reshape(total, qcount)  21.3 us
    ppermute x3, starting transfers between devices, per_device(): lax.ppermute(code, FAR, [(i, (i + k) % 4) for i in range(4)])  8.46 us
    pallas_call x1, Pallas kernels, local_intensity(): pl.pallas_call(functools.partial(turn_kernel, group, degs // group, rows)...  5.57 us
    ppermute x3, waiting for transfers between devices, per_device(): lax.ppermute(code, FAR, [(i, (i + k) % 4) for i in range(4)])  4.49 us
    ppermute x1, waiting for transfers between devices, per_device(): recv = lax.ppermute(give, 'c', swap)  4.37 us
    ppermute x1, starting transfers between devices, per_device(): recv = lax.ppermute(give, 'c', swap)  3.24 us
  transfers between devices with their start and end apart: 6, of which 4 were waited for; matrix products, arithmetic and copies ran while one was open for 0% of the time, Pallas kernels for 0%

profile of v3, /device:TPU:1, one launch (start us, length us, event | category | flops | bytes accessed | tf_op | source)
XLA Modules:
  0.0 114.4 jit_solution(5293073066443382285)
XLA Ops:
  0.0 0.6 pad_add_fusion.place
  0.6 1.3 %fusion.3 = s32[1024]{0:T(1024)} fusion(s32[1024]{0:T(1024)} %param.9, s32[1024]{0:T(1024)} %param.8, s32[1024]{0:T(1024)} %param.10, pred[]{:T(512)S(6)} %eq.3), kind=kLoop, calls=%fused_computation.4 | loop fusion | flops 6144 | bytes 16385 | tf_op jit(solution)/shard_map/add | solution.py:209
  2.0 30.4 %shard_map.73 = (f32[2304,256]{1,0:T(8,128)}, f32[2304,256]{1,0:T(8,128)}) custom-call(s32[2]{0:T(128)} %pad_add_fusion.place, s32[1,1024]{1,0:T(1,128)} %bitcast.8, bf16[26,1024,128]{2,1,0:T(8,128)(2,1)} %bitcast.9, f32[26,64,256]{2,1,0:T(8,128)} %bitcast.10, f32[8,256]{1,0:T(8,128)} %form.1), custom_call_target="tpu_custom_call" | custom-call | flops 12213813248 | bytes 8519680 | tf_op jit(solution)/shard_map/pallas_call | solution.py:83
  32.4 3.2 %collective-permute-start = (f32[2304,256]{1,0:T(8,128)}, f32[2304,256]{1,0:T(8,128)S(1)}, u32[]{:S(2)}, u32[]{:S(2)}) collective-permute-start(f32[2304,256]{1,0:T(8,128)} %get-tuple-element.10), channel_id=1, source_target_pairs={{0,2},{2,0},{1,3},{3,1},{4,6},{6,4},{5,7},{7,5},{8,10},{10,8},{9,1... | collective-permute-start | bytes 7077896 | tf_op jit(solution)/shard_map/ppermute | solution.py:221
  35.6 4.4 %collective-permute-done.recv = f32[2304,256]{1,0:T(8,128)S(1)} collective-permute-done((f32[2304,256]{1,0:T(8,128)}, f32[2304,256]{1,0:T(8,128)S(1)}, u32[]{:S(2)}, u32[]{:S(2)}) %collective-permute-start) | collective-permute-done | bytes 2359328 | tf_op jit(solution)/shard_map/ppermute | solution.py:221
  40.0 0.0 copy-start.1
  40.0 1.7 %copy-done.1 = f32[2304,256]{1,0:T(8,128)S(1)} copy-done((f32[2304,256]{1,0:T(8,128)S(1)}, f32[2304,256]{1,0:T(8,128)}, u32[]{:S(2)}) %copy-start.1) | copy-done | bytes 2359320
  41.7 0.5 shard_map.74
  42.2 21.6 %all_to_all.10.near = s16[16,160,256]{2,1,0:T(8,128)(2,1)S(1)} all-to-all(s16[16,160,256]{2,1,0:T(8,128)(2,1)S(1)} %shard_map.74), channel_id=1, replica_groups=mesh['y'=4,'xl'=2,'zh'=4,'zl'=2,'c'=2,'deg'=2] {'y','xl','zl'}, dimensions={0} | all-to-all | bytes 2621440 | tf_op jit(solution)/shard_map/all_to_all | solution.py:231
  63.8 0.4 shard_map.75
  64.2 6.1 %collective-permute-start.3 = (s16[160,256]{1,0:T(8,128)(2,1)S(1)}, s16[160,256]{1,0:T(8,128)(2,1)S(1)}, u32[]{:S(2)}, u32[]{:S(2)}) collective-permute-start(s16[160,256]{1,0:T(8,128)(2,1)S(1)} %get-tuple-element.12), channel_id=1, source_target_pairs={{0,16},{8,24},{16,0},{24,8},{1,17},{9,25},{17,1},{25,9},{2,18},{10... | collective-permute-start | bytes 245768 | tf_op jit(solution)/shard_map/ppermute | solution.py:241
  70.3 0.3 collective-permute-start.2
  70.6 2.1 %collective-permute-start.1 = (s16[160,256]{1,0:T(8,128)(2,1)S(1)}, s16[160,256]{1,0:T(8,128)(2,1)S(1)}, u32[]{:S(2)}, u32[]{:S(2)}) collective-permute-start(s16[160,256]{1,0:T(8,128)(2,1)S(1)} %get-tuple-element.12), channel_id=1, source_target_pairs={{0,8},{8,16},{16,24},{24,0},{1,9},{9,17},{17,25},{25,1},{2,10},{10... | collective-permute-start | bytes 245768 | tf_op jit(solution)/shard_map/ppermute | solution.py:241
  72.7 0.0 collective-permute-done.3.across
  72.7 4.5 %collective-permute-done.2.before = s16[160,256]{1,0:T(8,128)(2,1)S(1)} collective-permute-done((s16[160,256]{1,0:T(8,128)(2,1)S(1)}, s16[160,256]{1,0:T(8,128)(2,1)S(1)}, u32[]{:S(2)}, u32[]{:S(2)}) %collective-permute-start.2) | collective-permute-done | bytes 81952 | tf_op jit(solution)/shard_map/ppermute | solution.py:241
  77.2 0.0 collective-permute-done.1.after
  77.2 0.0 copy-start
  77.2 0.0 copy-start.2
  77.2 0.1 shard_map.76
  77.3 21.3 %all_to_all.11 = bf16[16,144,256]{2,1,0:T(8,128)(2,1)S(1)} all-to-all(bf16[16,144,256]{2,1,0:T(8,128)(2,1)S(1)} %shard_map.76), channel_id=1, replica_groups=mesh['y'=4,'xl'=2,'zh'=4,'zl'=2,'c'=2,'deg'=2] {'y','xl','zl'}, dimensions={0} | all-to-all | bytes 2359296 | tf_op jit(solution)/shard_map/all_to_all | solution.py:249
  98.5 3.2 %collective-permute-start.4 = (bf16[2304,256]{1,0:T(8,128)(2,1)S(1)}, bf16[2304,256]{1,0:T(8,128)(2,1)S(1)}, u32[]{:S(2)}, u32[]{:S(2)}) collective-permute-start(bf16[2304,256]{1,0:T(8,128)(2,1)S(1)} %bitcast.6), channel_id=1, source_target_pairs={{0,2},{2,0},{1,3},{3,1},{4,6},{6,4},{5,7},{7,5},{8,10},{10,8},{9,1... | collective-permute-start | bytes 3538952 | tf_op jit(solution)/shard_map/ppermute | solution.py:250
  101.7 2.5 %collective-permute-done.4.other = bf16[2304,256]{1,0:T(8,128)(2,1)S(1)} collective-permute-done((bf16[2304,256]{1,0:T(8,128)(2,1)S(1)}, bf16[2304,256]{1,0:T(8,128)(2,1)S(1)}, u32[]{:S(2)}, u32[]{:S(2)}) %collective-permute-start.4) | collective-permute-done | bytes 1179680 | tf_op jit(solution)/shard_map/ppermute | solution.py:250
  104.2 0.0 copy-done
  104.2 0.0 copy-done.2
  104.2 5.6 %shard_map.77 = f32[4,256]{1,0:T(4,128)S(1)} custom-call(s32[2]{0:T(128)S(1)} %copy-done.2, bf16[2304,256]{1,0:T(8,128)(2,1)S(1)} %bitcast.7, bf16[2304,256]{1,0:T(8,128)(2,1)S(1)} %collective-permute-done.4.other, bf16[4,26,128,128]{3,2,1,0:T(8,128)(2,1)S(1)} %copy-done), custom_call_target="tpu_custom_call" | custom-call | flops 872415232 | bytes 5767168 | tf_op jit(solution)/shard_map/pallas_call | solution.py:140
  109.7 2.5 %collective-permute-start.5 = (f32[4,256]{1,0:T(4,128)S(1)}, f32[4,256]{1,0:T(4,128)S(1)}, u32[]{:S(2)}, u32[]{:S(2)}) collective-permute-start(f32[4,256]{1,0:T(4,128)S(1)} %shard_map.77), channel_id=1, source_target_pairs={{0,1},{1,0},{2,3},{3,2},{4,5},{5,4},{6,7},{7,6},{8,9},{9,8},{10,11... | collective-permute-start | bytes 12296 | tf_op jit(solution)/shard_map/ppermute | solution.py:252
  112.3 1.5 %collective-permute-done.5 = f32[4,256]{1,0:T(4,128)S(1)} collective-permute-done((f32[4,256]{1,0:T(4,128)S(1)}, f32[4,256]{1,0:T(4,128)S(1)}, u32[]{:S(2)}, u32[]{:S(2)}) %collective-permute-start.5) | collective-permute-done | bytes 4128 | tf_op jit(solution)/shard_map/ppermute | solution.py:252
  113.8 0.6 add.11
Async XLA Ops:
  32.4 7.6 %collective-permute-start = (f32[2304,256]{1,0:T(8,128)}, f32[2304,256]{1,0:T(8,128)S(1)}, u32[]{:S(2)}, u32[]{:S(2)}) collective-permute-start(f32[2304,256]{1,0:T(8,128)} %get-tuple-element.10), channel_id=1, source_target_pairs={{0,2},{2,0},{1,3},{3,1},{4,6},{6,4},{5,7},{7,5},{8,10},{10,8},{9,1... | collective-permute-start | bytes 7077896 | tf_op jit(solution)/shard_map/ppermute | solution.py:221
  40.0 1.7 %copy-start.1 = (f32[2304,256]{1,0:T(8,128)S(1)}, f32[2304,256]{1,0:T(8,128)}, u32[]{:S(2)}) copy-start(f32[2304,256]{1,0:T(8,128)} %get-tuple-element.9.keep) | copy-start | bytes 7077892
  64.2 8.5 %collective-permute-start.3 = (s16[160,256]{1,0:T(8,128)(2,1)S(1)}, s16[160,256]{1,0:T(8,128)(2,1)S(1)}, u32[]{:S(2)}, u32[]{:S(2)}) collective-permute-start(s16[160,256]{1,0:T(8,128)(2,1)S(1)} %get-tuple-element.12), channel_id=1, source_target_pairs={{0,16},{8,24},{16,0},{24,8},{1,17},{9,25},{17,1},{25,9},{2,18},{10... | collective-permute-start | bytes 245768 | tf_op jit(solution)/shard_map/ppermute | solution.py:241
  70.3 6.9 %collective-permute-start.2 = (s16[160,256]{1,0:T(8,128)(2,1)S(1)}, s16[160,256]{1,0:T(8,128)(2,1)S(1)}, u32[]{:S(2)}, u32[]{:S(2)}) collective-permute-start(s16[160,256]{1,0:T(8,128)(2,1)S(1)} %get-tuple-element.12), channel_id=1, source_target_pairs={{0,24},{8,0},{16,8},{24,16},{1,25},{9,1},{17,9},{25,17},{2,26},{10... | collective-permute-start | bytes 245768 | tf_op jit(solution)/shard_map/ppermute | solution.py:241
  70.6 6.6 %collective-permute-start.1 = (s16[160,256]{1,0:T(8,128)(2,1)S(1)}, s16[160,256]{1,0:T(8,128)(2,1)S(1)}, u32[]{:S(2)}, u32[]{:S(2)}) collective-permute-start(s16[160,256]{1,0:T(8,128)(2,1)S(1)} %get-tuple-element.12), channel_id=1, source_target_pairs={{0,8},{8,16},{16,24},{24,0},{1,9},{9,17},{17,25},{25,1},{2,10},{10... | collective-permute-start | bytes 245768 | tf_op jit(solution)/shard_map/ppermute | solution.py:241
  77.2 27.0 %copy-start = (bf16[4,26,128,128]{3,2,1,0:T(8,128)(2,1)S(1)}, bf16[4,26,128,128]{3,2,1,0:T(8,128)(2,1)}, u32[]{:S(2)}) copy-start(bf16[4,26,128,128]{3,2,1,0:T(8,128)(2,1)} %wigner.1) | copy-start | bytes 10223620
  77.2 27.0 %copy-start.2 = (s32[2]{0:T(128)S(1)}, s32[2]{0:T(128)}, u32[]{:S(2)}) copy-start(s32[2]{0:T(128)} %pad_add_fusion.place) | copy-start | bytes 28
  98.5 5.6 %collective-permute-start.4 = (bf16[2304,256]{1,0:T(8,128)(2,1)S(1)}, bf16[2304,256]{1,0:T(8,128)(2,1)S(1)}, u32[]{:S(2)}, u32[]{:S(2)}) collective-permute-start(bf16[2304,256]{1,0:T(8,128)(2,1)S(1)} %bitcast.6), channel_id=1, source_target_pairs={{0,2},{2,0},{1,3},{3,1},{4,6},{6,4},{5,7},{7,5},{8,10},{10,8},{9,1... | collective-permute-start | bytes 3538952 | tf_op jit(solution)/shard_map/ppermute | solution.py:250
  109.7 4.0 %collective-permute-start.5 = (f32[4,256]{1,0:T(4,128)S(1)}, f32[4,256]{1,0:T(4,128)S(1)}, u32[]{:S(2)}, u32[]{:S(2)}) collective-permute-start(f32[4,256]{1,0:T(4,128)S(1)} %shard_map.77), channel_id=1, source_target_pairs={{0,1},{1,0},{2,3},{3,2},{4,5},{5,4},{6,7},{7,6},{8,9},{9,8},{10,11... | collective-permute-start | bytes 12296 | tf_op jit(solution)/shard_map/ppermute | solution.py:252

commit v4 on v3

--- a/solution.py
+++ b/solution.py
@@ -13,6 +13,7 @@
 FAR = "zh"
 PLANE = 16
 LIMIT = 8
+CHUNK = 1120
 
 
 def widths(local_deg):
@@ -28,65 +29,125 @@
     return rows[0] + sum(jnp.where(local >= j, rows[j] - rows[j - 1], 0) for j in cuts)
 
 
-def contract_first(a, b):
-    return lax.dot_general(a, b, (((0,), (0,)), ((), ())), preferred_element_type=jnp.float32)
-
-
-def amplitude_kernel(pair, scale, rows, place, keys, harmonic, bessel, form, keep, give, onehot):
-    step = pl.program_id(0)
-
-    @pl.when(step == 0)
-    def _():
-        slots = lax.broadcasted_iota(jnp.int32, onehot.shape, 0)
-        onehot[...] = jnp.where(slots == keys[...], 1.0, 0.0).astype(jnp.bfloat16)
-        keep[...] = jnp.zeros_like(keep)
-        give[...] = jnp.zeros_like(give)
-
-    both = jnp.concatenate([harmonic[i] for i in range(pair)], axis=1)
-    binned = jnp.dot(onehot[...], both, preferred_element_type=jnp.float32)
+def runs_of(rows):
+    runs, at = [], 0
+    for j, w in enumerate(rows):
+        if runs and runs[-1][2] == w:
+            runs[-1][1] += 1
+        else:
+            runs.append([j, 1, w, at])
+        at += w
+    return runs
+
+
+def amplitude_kernel(
+    scale, rows, place, keys, harmonic, bessel, form, keep, give,
+    atoms, waves, onehot, turned, high, low, atom_sems, wave_sem,
+):
+    live_rows = sum(rows)
     width = harmonic.shape[2]
-    for i in range(pair):
-        mine = binned[:, i * width : (i + 1) * width]
-        cols = jnp.concatenate([mine[:BINS], mine[BINS:]], axis=1)
-        cols_hi = cols.astype(jnp.bfloat16)
-        cols_lo = (cols - cols_hi.astype(jnp.float32)).astype(jnp.bfloat16)
-        radial = (bessel[i][:, None, :] * form[...][None]).reshape(BINS, form.shape[1])
-        radial_hi = radial.astype(jnp.bfloat16)
-        radial_lo = (radial - radial_hi.astype(jnp.float32)).astype(jnp.bfloat16)
-        out = contract_first(cols_hi, radial_hi)
-        out = out + contract_first(cols_lo, radial_hi)
-        out = out + contract_first(cols_hi, radial_lo)
-        local = step * pair + i
-        live = 2 * (place[0] + local) + 1
-        order = lax.broadcasted_iota(jnp.int32, (width, out.shape[1]), 0)
-        at = pl.ds(pl.multiple_of(start_of(local, rows), 16), width)
-        keep[at, :] = jnp.where(order < live, out[:width] * scale, 0.0)
-        give[at, :] = jnp.where(order < live, out[width:] * scale, 0.0)
-
-
-def local_amplitude(place, keys, harmonic, bessel, form, total, pair, scale, rows):
+    qcount = form.shape[1]
+    fetch = [
+        pltpu.make_async_copy(harmonic.at[j], atoms.at[j], atom_sems.at[j])
+        for j in range(len(rows))
+    ]
+    for copy in fetch:
+        copy.start()
+    wave_copy = pltpu.make_async_copy(bessel, waves, wave_sem)
+    wave_copy.start()
+
+    slots = lax.broadcasted_iota(jnp.int32, (width, 2 * BINS), 1).astype(jnp.float32)
+    for i in range(atoms.shape[1] // width):
+        line = keys[:, i * width : (i + 1) * width].astype(jnp.float32)
+        tall = jnp.transpose(jnp.broadcast_to(line, (width, width)))
+        same = slots == jnp.concatenate([tall] * (2 * BINS // width), axis=1)
+        onehot[i * width : (i + 1) * width, :] = jnp.where(same, 1.0, 0.0).astype(jnp.bfloat16)
+    tail = keep.shape[0] - live_rows
+    keep[live_rows:, :] = jnp.zeros((tail, qcount), jnp.float32)
+    give[live_rows:, :] = jnp.zeros((tail, qcount), jnp.float32)
+
+    for first, count, wide, at in runs_of(rows):
+
+        def turn(j, carry):
+            pltpu.make_async_copy(
+                harmonic.at[first + j], atoms.at[first + j], atom_sems.at[first + j]
+            ).wait()
+            there = pl.ds(pl.multiple_of(at + j * wide, 16), wide)
+            turned[there, :] = jnp.transpose(atoms[first + j])[:wide]
+            return carry
+
+        lax.fori_loop(0, count, turn, 0)
+
+    chunk = CHUNK
+
+    def bin_rows(i, carry):
+        there = pl.ds(pl.multiple_of(i * chunk, 16), chunk)
+        binned = jnp.dot(turned[there, :], onehot[...], preferred_element_type=jnp.float32)
+        top = binned.astype(jnp.bfloat16)
+        high[there, :] = top
+        low[there, :] = (binned - top.astype(jnp.float32)).astype(jnp.bfloat16)
+        return carry
+
+    lax.fori_loop(0, live_rows // chunk, bin_rows, 0)
+    wave_copy.wait()
+
+    for first, count, wide, at in runs_of(rows):
+
+        def mix(j, carry):
+            radial = (waves[first + j][:, None, :] * form[...][None]).reshape(BINS, qcount)
+            radial_hi = radial.astype(jnp.bfloat16)
+            radial_lo = (radial - radial_hi.astype(jnp.float32)).astype(jnp.bfloat16)
+            there = pl.ds(pl.multiple_of(at + j * wide, 16), wide)
+            tops = [high[there, :BINS], high[there, BINS:]]
+            lows = [low[there, :BINS], low[there, BINS:]]
+            main = jnp.dot(
+                jnp.concatenate(tops + lows, axis=0),
+                radial_hi,
+                preferred_element_type=jnp.float32,
+            )
+            rest = jnp.dot(
+                jnp.concatenate(tops, axis=0), radial_lo, preferred_element_type=jnp.float32
+            )
+            out = (main[: 2 * wide] + (main[2 * wide :] + rest)) * scale
+            live = 2 * (place[0] + first + j) + 1
+            order = lax.broadcasted_iota(jnp.int32, (wide, qcount), 0)
+            keep[there, :] = jnp.where(order < live, out[:wide], 0.0)
+            give[there, :] = jnp.where(order < live, out[wide:], 0.0)
+            return carry
+
+        for j in range(count):
+            mix(j, 0)
+
+
+def local_amplitude(place, keys, harmonic, bessel, form, total, scale, rows):
     degs, atoms, width = harmonic.shape
     qcount = form.shape[1]
+    live_rows = sum(rows)
     out = jax.ShapeDtypeStruct((total, qcount), jnp.float32)
-    grid_spec = pltpu.PrefetchScalarGridSpec(
-        num_scalar_prefetch=1,
-        grid=(degs // pair,),
+    return pl.pallas_call(
+        functools.partial(amplitude_kernel, scale, rows),
         in_specs=[
-            pl.BlockSpec((1, atoms), lambda s, *_: (0, 0)),
-            pl.BlockSpec((pair, atoms, width), lambda s, *_: (s, 0, 0)),
-            pl.BlockSpec((pair, SHELLS, qcount), lambda s, *_: (s, 0, 0)),
-            pl.BlockSpec((TYPES, qcount), lambda s, *_: (0, 0)),
+            pl.BlockSpec(memory_space=pltpu.SMEM),
+            pl.BlockSpec(memory_space=pltpu.VMEM),
+            pl.BlockSpec(memory_space=pltpu.HBM),
+            pl.BlockSpec(memory_space=pltpu.HBM),
+            pl.BlockSpec(memory_space=pltpu.VMEM),
         ],
         out_specs=[pl.BlockSpec(memory_space=pltpu.VMEM)] * 2,
-        scratch_shapes=[pltpu.VMEM((2 * BINS, atoms), jnp.bfloat16)],
-    )
-    return pl.pallas_call(
-        functools.partial(amplitude_kernel, pair, scale, rows),
-        grid_spec=grid_spec,
         out_shape=[out, out],
-        compiler_params=pltpu.CompilerParams(vmem_limit_bytes=56 * 2**20),
+        scratch_shapes=[
+            pltpu.VMEM((degs, atoms, width), jnp.bfloat16),
+            pltpu.VMEM(bessel.shape, jnp.float32),
+            pltpu.VMEM((atoms, 2 * BINS), jnp.bfloat16),
+            pltpu.VMEM((live_rows, atoms), jnp.bfloat16),
+            pltpu.VMEM((live_rows, 2 * BINS), jnp.bfloat16),
+            pltpu.VMEM((live_rows, 2 * BINS), jnp.bfloat16),
+            pltpu.SemaphoreType.DMA((degs,)),
+            pltpu.SemaphoreType.DMA,
+        ],
+        compiler_params=pltpu.CompilerParams(vmem_limit_bytes=52 * 2**20),
         cost_estimate=pl.CostEstimate(
-            flops=2 * degs * width * (2 * BINS * atoms + 6 * BINS * qcount),
+            flops=2 * live_rows * (2 * BINS * atoms + 6 * BINS * qcount),
             bytes_accessed=harmonic.size * 2 + bessel.size * 4,
             transcendentals=0,
         ),
@@ -214,7 +275,6 @@
         bessel.transpose(1, 0, 2),
         form,
         total,
-        2,
         (atom_rows * 128) ** -0.5,
         rows,
     )

time: 115 us -> 102 us (0.89)
  Pallas kernels: 37 us -> 22.9 us
  local copies, waits for them, and re-layouts: 1.67 us -> 3.82 us
  other arithmetic: 2.56 us -> 1.4 us
    pallas_call x1, Pallas kernels: 30.4 us -> 16.3 us  [local_amplitude(): pl.pallas_call(functools.partial(amplitude_kernel, scale, rows), in_specs...]
    unnamed x6 -> x8, local copies, waits for them, and re-layouts: 1.67 us -> 3.82 us
where the time goes in v4:
time: 102 us; the launch traced here: 101 us
  blocking collectives  43 us (42%)
  Pallas kernels  22.9 us (22%)
  starting transfers between devices  17.4 us (17%)
  waiting for transfers between devices  12.9 us (13%)
  local copies, waits for them, and re-layouts  3.82 us (4%)
  other arithmetic  1.4 us (1%)
    all_to_all x1, blocking collectives, per_device(): near = lax.all_to_all(near, NEAR, 0, 0)  21.6 us
    all_to_all x1, blocking collectives, per_device(): mine = lax.all_to_all(spread, NEAR, 0, 0).reshape(total, qcount)  21.3 us
    pallas_call x1, Pallas kernels, local_amplitude(): pl.pallas_call(functools.partial(amplitude_kernel, scale, rows), in_specs...  16.3 us
    ppermute x3, starting transfers between devices, per_device(): lax.ppermute(code, FAR, [(i, (i + k) % 4) for i in range(4)])  8.46 us
    pallas_call x1, Pallas kernels, local_intensity(): pl.pallas_call(functools.partial(turn_kernel, group, degs // group, rows)...  5.57 us
    ppermute x3, waiting for transfers between devices, per_device(): lax.ppermute(code, FAR, [(i, (i + k) % 4) for i in range(4)])  4.5 us
    ppermute x1, waiting for transfers between devices, per_device(): recv = lax.ppermute(give, 'c', swap)  4.37 us
    unnamed x8, local copies, waits for them, and re-layouts  3.82 us
  transfers between devices with their start and end apart: 6, of which 4 were waited for; matrix products, arithmetic and copies ran while one was open for 0% of the time, Pallas kernels for 0%

profile of v4, /device:TPU:1, one launch (start us, length us, event | category | flops | bytes accessed | tf_op | source)
XLA Modules:
  0.0 101.4 jit_solution(6947141450179203270)
XLA Ops:
  0.0 0.1 pad_add_fusion.place
  0.1 0.7 fusion.3
  0.8 0.0 copy-start.2
  0.8 1.5 %copy-done.2 = f32[64,26,256]{2,0,1:T(8,128)S(1)} copy-done((f32[64,26,256]{2,0,1:T(8,128)S(1)}, f32[64,26,256]{2,0,1:T(8,128)}, u32[]{:S(2)}) %copy-start.2) | copy-done | bytes 1703960
  2.3 0.0 copy-start.3
  2.3 0.7 copy-done.3
  3.0 16.3 %shard_map.73 = (f32[2304,256]{1,0:T(8,128)}, f32[2304,256]{1,0:T(8,128)}) custom-call(s32[2]{0:T(128)S(1)} %pad_add_fusion.place, s32[1,1024]{1,0:T(1,128)S(1)} %bitcast.8, bf16[26,1024,128]{2,1,0:T(8,128)(2,1)} %bitcast.10, f32[26,64,256]{2,1,0:T(8,128)S(1)} %bitcast.9, f32[8,256]{1,0:T(8,128)S(1)} %copy-done.3), custom_call_target="tpu_custom_call" | custom-call | flops 8220835840 | bytes 8519680 | tf_op jit(solution)/shard_map/pallas_call | solution.py:127
  19.3 3.3 %collective-permute-start = (f32[2304,256]{1,0:T(8,128)}, f32[2304,256]{1,0:T(8,128)S(1)}, u32[]{:S(2)}, u32[]{:S(2)}) collective-permute-start(f32[2304,256]{1,0:T(8,128)} %get-tuple-element.10), channel_id=1, source_target_pairs={{0,2},{2,0},{1,3},{3,1},{4,6},{6,4},{5,7},{7,5},{8,10},{10,8},{9,1... | collective-permute-start | bytes 7077896 | tf_op jit(solution)/shard_map/ppermute | solution.py:281
  22.6 4.4 %collective-permute-done.recv = f32[2304,256]{1,0:T(8,128)S(1)} collective-permute-done((f32[2304,256]{1,0:T(8,128)}, f32[2304,256]{1,0:T(8,128)S(1)}, u32[]{:S(2)}, u32[]{:S(2)}) %collective-permute-start) | collective-permute-done | bytes 2359328 | tf_op jit(solution)/shard_map/ppermute | solution.py:281
  26.9 0.0 copy-start.1
  26.9 1.7 %copy-done.1 = f32[2304,256]{1,0:T(8,128)S(1)} copy-done((f32[2304,256]{1,0:T(8,128)S(1)}, f32[2304,256]{1,0:T(8,128)}, u32[]{:S(2)}) %copy-start.1) | copy-done | bytes 2359320
  28.6 0.5 shard_map.74
  29.1 21.6 %all_to_all.10.near = s16[16,160,256]{2,1,0:T(8,128)(2,1)S(1)} all-to-all(s16[16,160,256]{2,1,0:T(8,128)(2,1)S(1)} %shard_map.74), channel_id=1, replica_groups=mesh['y'=4,'xl'=2,'zh'=4,'zl'=2,'c'=2,'deg'=2] {'y','xl','zl'}, dimensions={0} | all-to-all | bytes 2621440 | tf_op jit(solution)/shard_map/all_to_all | solution.py:291
  50.8 0.4 shard_map.75
  51.2 6.1 %collective-permute-start.3 = (s16[160,256]{1,0:T(8,128)(2,1)S(1)}, s16[160,256]{1,0:T(8,128)(2,1)S(1)}, u32[]{:S(2)}, u32[]{:S(2)}) collective-permute-start(s16[160,256]{1,0:T(8,128)(2,1)S(1)} %get-tuple-element.12), channel_id=1, source_target_pairs={{0,16},{8,24},{16,0},{24,8},{1,17},{9,25},{17,1},{25,9},{2,18},{10... | collective-permute-start | bytes 245768 | tf_op jit(solution)/shard_map/ppermute | solution.py:301
  57.3 0.3 collective-permute-start.2
  57.5 2.1 %collective-permute-start.1 = (s16[160,256]{1,0:T(8,128)(2,1)S(1)}, s16[160,256]{1,0:T(8,128)(2,1)S(1)}, u32[]{:S(2)}, u32[]{:S(2)}) collective-permute-start(s16[160,256]{1,0:T(8,128)(2,1)S(1)} %get-tuple-element.12), channel_id=1, source_target_pairs={{0,8},{8,16},{16,24},{24,0},{1,9},{9,17},{17,25},{25,1},{2,10},{10... | collective-permute-start | bytes 245768 | tf_op jit(solution)/shard_map/ppermute | solution.py:301
  59.6 0.0 collective-permute-done.3.across
  59.6 4.5 %collective-permute-done.2.before = s16[160,256]{1,0:T(8,128)(2,1)S(1)} collective-permute-done((s16[160,256]{1,0:T(8,128)(2,1)S(1)}, s16[160,256]{1,0:T(8,128)(2,1)S(1)}, u32[]{:S(2)}, u32[]{:S(2)}) %collective-permute-start.2) | collective-permute-done | bytes 81952 | tf_op jit(solution)/shard_map/ppermute | solution.py:301
  64.1 0.0 collective-permute-done.1.after
  64.1 0.0 copy-start
  64.1 0.1 shard_map.76
  64.2 21.3 %all_to_all.11 = bf16[16,144,256]{2,1,0:T(8,128)(2,1)S(1)} all-to-all(bf16[16,144,256]{2,1,0:T(8,128)(2,1)S(1)} %shard_map.76), channel_id=1, replica_groups=mesh['y'=4,'xl'=2,'zh'=4,'zl'=2,'c'=2,'deg'=2] {'y','xl','zl'}, dimensions={0} | all-to-all | bytes 2359296 | tf_op jit(solution)/shard_map/all_to_all | solution.py:309
  85.6 3.1 %collective-permute-start.4 = (bf16[2304,256]{1,0:T(8,128)(2,1)S(1)}, bf16[2304,256]{1,0:T(8,128)(2,1)S(1)}, u32[]{:S(2)}, u32[]{:S(2)}) collective-permute-start(bf16[2304,256]{1,0:T(8,128)(2,1)S(1)} %bitcast.6), channel_id=1, source_target_pairs={{0,2},{2,0},{1,3},{3,1},{4,6},{6,4},{5,7},{7,5},{8,10},{10,8},{9,1... | collective-permute-start | bytes 3538952 | tf_op jit(solution)/shard_map/ppermute | solution.py:310
  88.7 2.5 %collective-permute-done.4.other = bf16[2304,256]{1,0:T(8,128)(2,1)S(1)} collective-permute-done((bf16[2304,256]{1,0:T(8,128)(2,1)S(1)}, bf16[2304,256]{1,0:T(8,128)(2,1)S(1)}, u32[]{:S(2)}, u32[]{:S(2)}) %collective-permute-start.4) | collective-permute-done | bytes 1179680 | tf_op jit(solution)/shard_map/ppermute | solution.py:310
  91.2 0.0 copy-done
  91.2 5.6 %shard_map.77 = f32[4,256]{1,0:T(4,128)S(1)} custom-call(s32[2]{0:T(128)S(1)} %pad_add_fusion.place, bf16[2304,256]{1,0:T(8,128)(2,1)S(1)} %bitcast.7, bf16[2304,256]{1,0:T(8,128)(2,1)S(1)} %collective-permute-done.4.other, bf16[4,26,128,128]{3,2,1,0:T(8,128)(2,1)S(1)} %copy-done), custom_call_target="tpu_custom_call" | custom-call | flops 872415232 | bytes 5767168 | tf_op jit(solution)/shard_map/pallas_call | solution.py:201
  96.7 2.5 %collective-permute-start.5 = (f32[4,256]{1,0:T(4,128)S(1)}, f32[4,256]{1,0:T(4,128)S(1)}, u32[]{:S(2)}, u32[]{:S(2)}) collective-permute-start(f32[4,256]{1,0:T(4,128)S(1)} %shard_map.77), channel_id=1, source_target_pairs={{0,1},{1,0},{2,3},{3,2},{4,5},{5,4},{6,7},{7,6},{8,9},{9,8},{10,11... | collective-permute-start | bytes 12296 | tf_op jit(solution)/shard_map/ppermute | solution.py:312
  99.3 1.5 %collective-permute-done.5 = f32[4,256]{1,0:T(4,128)S(1)} collective-permute-done((f32[4,256]{1,0:T(4,128)S(1)}, f32[4,256]{1,0:T(4,128)S(1)}, u32[]{:S(2)}, u32[]{:S(2)}) %collective-permute-start.5) | collective-permute-done | bytes 4128 | tf_op jit(solution)/shard_map/ppermute | solution.py:312
  100.8 0.6 add.11
Async XLA Ops:
  0.8 1.5 %copy-start.2 = (f32[64,26,256]{2,0,1:T(8,128)S(1)}, f32[64,26,256]{2,0,1:T(8,128)}, u32[]{:S(2)}) copy-start(f32[64,26,256]{2,0,1:T(8,128)} %param.12) | copy-start | bytes 5111812
  2.3 0.7 copy-start.3
  19.3 7.7 %collective-permute-start = (f32[2304,256]{1,0:T(8,128)}, f32[2304,256]{1,0:T(8,128)S(1)}, u32[]{:S(2)}, u32[]{:S(2)}) collective-permute-start(f32[2304,256]{1,0:T(8,128)} %get-tuple-element.10), channel_id=1, source_target_pairs={{0,2},{2,0},{1,3},{3,1},{4,6},{6,4},{5,7},{7,5},{8,10},{10,8},{9,1... | collective-permute-start | bytes 7077896 | tf_op jit(solution)/shard_map/ppermute | solution.py:281
  26.9 1.7 %copy-start.1 = (f32[2304,256]{1,0:T(8,128)S(1)}, f32[2304,256]{1,0:T(8,128)}, u32[]{:S(2)}) copy-start(f32[2304,256]{1,0:T(8,128)} %get-tuple-element.9.keep) | copy-start | bytes 7077892
  51.2 8.5 %collective-permute-start.3 = (s16[160,256]{1,0:T(8,128)(2,1)S(1)}, s16[160,256]{1,0:T(8,128)(2,1)S(1)}, u32[]{:S(2)}, u32[]{:S(2)}) collective-permute-start(s16[160,256]{1,0:T(8,128)(2,1)S(1)} %get-tuple-element.12), channel_id=1, source_target_pairs={{0,16},{8,24},{16,0},{24,8},{1,17},{9,25},{17,1},{25,9},{2,18},{10... | collective-permute-start | bytes 245768 | tf_op jit(solution)/shard_map/ppermute | solution.py:301
  57.3 6.9 %collective-permute-start.2 = (s16[160,256]{1,0:T(8,128)(2,1)S(1)}, s16[160,256]{1,0:T(8,128)(2,1)S(1)}, u32[]{:S(2)}, u32[]{:S(2)}) collective-permute-start(s16[160,256]{1,0:T(8,128)(2,1)S(1)} %get-tuple-element.12), channel_id=1, source_target_pairs={{0,24},{8,0},{16,8},{24,16},{1,25},{9,1},{17,9},{25,17},{2,26},{10... | collective-permute-start | bytes 245768 | tf_op jit(solution)/shard_map/ppermute | solution.py:301
  57.5 6.6 %collective-permute-start.1 = (s16[160,256]{1,0:T(8,128)(2,1)S(1)}, s16[160,256]{1,0:T(8,128)(2,1)S(1)}, u32[]{:S(2)}, u32[]{:S(2)}) collective-permute-start(s16[160,256]{1,0:T(8,128)(2,1)S(1)} %get-tuple-element.12), channel_id=1, source_target_pairs={{0,8},{8,16},{16,24},{24,0},{1,9},{9,17},{17,25},{25,1},{2,10},{10... | collective-permute-start | bytes 245768 | tf_op jit(solution)/shard_map/ppermute | solution.py:301
  64.1 27.0 %copy-start = (bf16[4,26,128,128]{3,2,1,0:T(8,128)(2,1)S(1)}, bf16[4,26,128,128]{3,2,1,0:T(8,128)(2,1)}, u32[]{:S(2)}) copy-start(bf16[4,26,128,128]{3,2,1,0:T(8,128)(2,1)} %wigner.1) | copy-start | bytes 10223620
  85.6 5.6 %collective-permute-start.4 = (bf16[2304,256]{1,0:T(8,128)(2,1)S(1)}, bf16[2304,256]{1,0:T(8,128)(2,1)S(1)}, u32[]{:S(2)}, u32[]{:S(2)}) collective-permute-start(bf16[2304,256]{1,0:T(8,128)(2,1)S(1)} %bitcast.6), channel_id=1, source_target_pairs={{0,2},{2,0},{1,3},{3,1},{4,6},{6,4},{5,7},{7,5},{8,10},{10,8},{9,1... | collective-permute-start | bytes 3538952 | tf_op jit(solution)/shard_map/ppermute | solution.py:310
  96.7 4.0 %collective-permute-start.5 = (f32[4,256]{1,0:T(4,128)S(1)}, f32[4,256]{1,0:T(4,128)S(1)}, u32[]{:S(2)}, u32[]{:S(2)}) collective-permute-start(f32[4,256]{1,0:T(4,128)S(1)} %shard_map.77), channel_id=1, source_target_pairs={{0,1},{1,0},{2,3},{3,2},{4,5},{5,4},{6,7},{7,6},{8,9},{9,8},{10,11... | collective-permute-start | bytes 12296 | tf_op jit(solution)/shard_map/ppermute | solution.py:312

commit v5 on v3

v5 whole, which is shorter than its diff:
```python
import functools
import jax
import jax.numpy as jnp
from jax import lax
from jax.experimental import pallas as pl
from jax.experimental.pallas import tpu as pltpu
from jax.sharding import Mesh, PartitionSpec as P

SHELLS = 64
TYPES = 8
BINS = SHELLS * TYPES
NEAR = ("y", "xl", "zl")
FAR = "zh"
PLANE = 16
LIMIT = 8
AMPLITUDE_MIB = 48
TURN_MIB = 16


def widths(local_deg, step):
    return [-(-(2 * (local_deg + j) + 1) // step) * step for j in range(local_deg)]


def starts(rows):
    return [sum(rows[:j]) for j in range(len(rows))]


def coded(x, spare):
    top = jnp.maximum(jnp.max(jnp.abs(x), axis=0, keepdims=True), 1e-30)
    power = jnp.floor(jnp.log2(top)) + 1.0
    steps = jnp.clip(jnp.round(x * jnp.exp2(15.0 - power)), -32767.0, 32767.0)
    tail = jnp.broadcast_to(power, (spare, x.shape[1]))
    return jnp.concatenate([steps, tail], axis=0).astype(jnp.int32).astype(jnp.int16)


def decoded(block, rows):
    wide = block.astype(jnp.int32).astype(jnp.float32)
    return wide[:rows] * jnp.exp2(wide[rows : rows + 1] - 15.0)


def amplitude_kernel(
    scale, rows, thin, place, keys, harmonic, bessel, form, keep, give,
    atoms, waves, forms, onehot, turned, high, low, away, atom_sems, wave_sem, form_sem,
):
    width = harmonic.shape[2]
    qcount = form.shape[1]
    degs = len(rows)
    fetch = [
        pltpu.make_async_copy(harmonic.at[j], atoms.at[j], atom_sems.at[j]) for j in range(degs)
    ]
    for copy in fetch:
        copy.start()
    wave_copy = pltpu.make_async_copy(bessel, waves, wave_sem)
    wave_copy.start()
    form_copy = pltpu.make_async_copy(form, forms, form_sem)
    form_copy.start()

    slots = lax.broadcasted_iota(jnp.int32, (width, 2 * BINS), 1).astype(jnp.float32)
    for i in range(atoms.shape[1] // width):
        line = keys[:, i * width : (i + 1) * width].astype(jnp.float32)
        tall = jnp.transpose(jnp.broadcast_to(line, (width, width)))
        same = slots == jnp.concatenate([tall] * (2 * BINS // width), axis=1)
        onehot[i * width : (i + 1) * width, :] = jnp.where(same, 1.0, 0.0).astype(jnp.bfloat16)
    used = sum(thin)
    blank = jnp.zeros((keep.shape[0] - used, qcount), jnp.float32)
    keep[used:, :] = blank
    away[used:, :] = blank

    wide_at, thin_at = starts(rows), starts(thin)

    def turn(j):
        fetch[j].wait()
        turned[wide_at[j] : wide_at[j] + rows[j], :] = jnp.transpose(atoms[j])[: rows[j]]

    def bin_rows(first, last):
        there = slice(wide_at[first], wide_at[last] + rows[last])
        binned = jnp.dot(turned[there, :], onehot[...], preferred_element_type=jnp.float32)
        top = binned.astype(jnp.bfloat16)
        high[there, :] = top
        low[there, :] = (binned - top.astype(jnp.float32)).astype(jnp.bfloat16)

    def mix(j):
        wide = rows[j]
        radial = (waves[j][:, None, :] * forms[...][None]).reshape(BINS, qcount)
        radial_hi = radial.astype(jnp.bfloat16)
        radial_lo = (radial - radial_hi.astype(jnp.float32)).astype(jnp.bfloat16)
        there = slice(wide_at[j], wide_at[j] + wide)
        tops = [high[there, :BINS], high[there, BINS:]]
        lows = [low[there, :BINS], low[there, BINS:]]
        main = jnp.dot(
            jnp.concatenate(tops + lows, axis=0), radial_hi, preferred_element_type=jnp.float32
        )
        rest = jnp.dot(
            jnp.concatenate(tops, axis=0), radial_lo, preferred_element_type=jnp.float32
        )
        out = (main[: 2 * wide] + (main[2 * wide :] + rest)) * scale
        live = 2 * (place[0] + j) + 1
        order = lax.broadcasted_iota(jnp.int32, (wide, qcount), 0)
        at = slice(thin_at[j], thin_at[j] + thin[j])
        keep[at, :] = jnp.where(order < live, out[:wide], 0.0)[: thin[j]]
        away[at, :] = jnp.where(order < live, out[wide:], 0.0)[: thin[j]]

    cuts = [(0, 5), (6, 13), (14, 21), (22, degs - 1)]
    for j in range(degs):
        turn(j)
    for first, last in cuts:
        bin_rows(first, last)
    wave_copy.wait()
    form_copy.wait()
    for j in range(degs):
        mix(j)
    height = keep.shape[0] // give.shape[0]
    for i in range(give.shape[0]):
        give[i] = coded(away[i * height : (i + 1) * height, :], give.shape[1] - height)


def local_amplitude(place, keys, harmonic, bessel, form, height, scale, rows, thin):
    degs, atoms, width = harmonic.shape
    qcount = form.shape[1]
    live_rows = sum(rows)
    outs = [
        jax.ShapeDtypeStruct((PLANE * height, qcount), jnp.float32),
        jax.ShapeDtypeStruct((PLANE, height + 8, qcount), jnp.int16),
    ]
    return pl.pallas_call(
        functools.partial(amplitude_kernel, scale, rows, thin),
        in_specs=[
            pl.BlockSpec(memory_space=pltpu.SMEM),
            pl.BlockSpec(memory_space=pltpu.VMEM),
            pl.BlockSpec(memory_space=pl.ANY),
            pl.BlockSpec(memory_space=pl.ANY),
            pl.BlockSpec(memory_space=pl.ANY),
        ],
        out_specs=[pl.BlockSpec(memory_space=pltpu.VMEM)] * 2,
        out_shape=outs,
        scratch_shapes=[
            pltpu.VMEM((degs, atoms, width), jnp.bfloat16),
            pltpu.VMEM(bessel.shape, jnp.float32),
            pltpu.VMEM(form.shape, jnp.float32),
            pltpu.VMEM((atoms, 2 * BINS), jnp.bfloat16),
            pltpu.VMEM((live_rows, atoms), jnp.bfloat16),
            pltpu.VMEM((live_rows, 2 * BINS), jnp.bfloat16),
            pltpu.VMEM((live_rows, 2 * BINS), jnp.bfloat16),
            pltpu.VMEM(outs[0].shape, jnp.float32),
            pltpu.SemaphoreType.DMA((degs,)),
            pltpu.SemaphoreType.DMA,
            pltpu.SemaphoreType.DMA,
        ],
        compiler_params=pltpu.CompilerParams(vmem_limit_bytes=AMPLITUDE_MIB * 2**20),
        cost_estimate=pl.CostEstimate(
            flops=2 * live_rows * (2 * BINS * atoms + 6 * BINS * qcount),
            bytes_accessed=harmonic.size * 2 + bessel.size * 4,
            transcendentals=0,
        ),
    )(place, keys, harmonic, bessel, form)


def turn_kernel(rows, thin, place, mine, other, wigner, out, first, second):
    rots, degs, width, _ = wigner.shape
    qcount = mine.shape[1]

    @pl.when(place[1] == 0)
    def _():
        first[...] = mine[...].astype(jnp.float32)
        second[...] = other[...].astype(jnp.float32)

    @pl.when(place[1] != 0)
    def _():
        first[...] = other[...].astype(jnp.float32)
        second[...] = mine[...].astype(jnp.float32)

    acc = [jnp.zeros((8, qcount), jnp.float32)] * rots
    thin_at = starts(thin)
    for j in range(degs):
        wide, some, at = rows[j], thin[j], thin_at[j]
        right = second[at : at + some, :]
        pad = jnp.zeros((width - some, qcount), jnp.float32)
        right = jnp.concatenate([right, pad], axis=0).astype(jnp.bfloat16)
        blocks = jnp.concatenate([wigner[r, j][:wide] for r in range(rots)], axis=0)
        turned = jnp.dot(blocks, right, preferred_element_type=jnp.float32)
        left = first[at : at + some, :]
        for r in range(rots):
            prod = turned[r * wide : r * wide + some] * left
            acc[r] = acc[r] + jnp.sum(prod.reshape(some // 8, 8, qcount), axis=0)
    for r in range(rots):
        out[r : r + 1, :] = jnp.sum(acc[r], axis=0, keepdims=True) * (0.5 / degs)


def local_intensity(place, mine, other, wigner, rows, thin):
    rots = wigner.shape[0]
    total, qcount = mine.shape
    vmem = pl.BlockSpec(memory_space=pltpu.VMEM)
    return pl.pallas_call(
        functools.partial(turn_kernel, rows, thin),
        in_specs=[pl.BlockSpec(memory_space=pltpu.SMEM), vmem, vmem, vmem],
        out_specs=vmem,
        out_shape=jax.ShapeDtypeStruct((rots, qcount), jnp.float32),
        scratch_shapes=[pltpu.VMEM((total, qcount), jnp.float32)] * 2,
        compiler_params=pltpu.CompilerParams(vmem_limit_bytes=TURN_MIB * 2**20),
        cost_estimate=pl.CostEstimate(
            flops=2 * wigner.size * qcount,
            bytes_accessed=wigner.size * 2 + mine.size * 4,
            transcendentals=0,
        ),
    )(place, mine, other, wigner)


def near_kernel(rows, keep, recv, out):
    for i in range(out.shape[0]):
        at = pl.ds(i * rows, rows)
        out[i] = coded(keep[at, :] + decoded(recv[i], rows), out.shape[1] - rows)


def plane_kernel(rows, near, total, code):
    acc = decoded(near[0], rows)
    for i in range(1, near.shape[0]):
        acc = acc + decoded(near[i], rows)
    total[...] = acc
    code[...] = coded(acc, code.shape[0] - rows)


def whole_kernel(total, after, before, across, out):
    rows = total.shape[0]
    acc = total[...] + decoded(across[...], rows)
    acc = acc + (decoded(after[...], rows) + decoded(before[...], rows))
    block = acc.astype(jnp.bfloat16)
    for i in range(out.shape[0]):
        out[i] = block


def whole_call(body, out_shape, limit, *args):
    spec = pl.BlockSpec(memory_space=pltpu.VMEM)
    return pl.pallas_call(
        body,
        in_specs=[spec] * len(args),
        out_specs=jax.tree.map(lambda _: spec, out_shape),
        out_shape=out_shape,
        compiler_params=pltpu.CompilerParams(vmem_limit_bytes=limit * 2**20),
    )(*args)


def per_device(harmonic, shell, atom_type, domain, form, bessel, wigner):
    atom_rows, local_deg, width = harmonic.shape
    qcount = form.shape[1]
    rows, thin = widths(local_deg, 16), widths(local_deg, 8)
    height = -(-sum(thin) // (8 * PLANE)) * 8
    total = height * PLANE
    core = lax.axis_index("c")
    swap = [(0, 1), (1, 0)]
    place = jnp.stack([lax.axis_index("deg") * local_deg, core]).astype(jnp.int32)
    side = jnp.where(core == 0, domain, 1 - domain)
    keys = ((side * SHELLS + shell) * TYPES + atom_type)[None]
    keep, give = local_amplitude(
        place,
        keys,
        harmonic.transpose(1, 0, 2),
        bessel.transpose(1, 0, 2),
        form,
        height,
        (atom_rows * 128) ** -0.5,
        rows,
        thin,
    )
    recv = lax.ppermute(give, "c", swap)
    coded_shape = (height + 8, qcount)
    near = whole_call(
        functools.partial(near_kernel, height),
        jax.ShapeDtypeStruct((PLANE,) + coded_shape, jnp.int16),
        LIMIT,
        keep,
        recv,
    )
    near = lax.all_to_all(near, NEAR, 0, 0)
    part, code = whole_call(
        functools.partial(plane_kernel, height),
        [
            jax.ShapeDtypeStruct((height, qcount), jnp.float32),
            jax.ShapeDtypeStruct(coded_shape, jnp.int16),
        ],
        LIMIT,
        near,
    )
    turns = [lax.ppermute(code, FAR, [(i, (i + k) % 4) for i in range(4)]) for k in (1, 3, 2)]
    spread = whole_call(
        whole_kernel,
        jax.ShapeDtypeStruct((PLANE, height, qcount), jnp.bfloat16),
        LIMIT,
        part,
        *turns,
    )
    mine = lax.all_to_all(spread, NEAR, 0, 0).reshape(total, qcount)
    other = lax.ppermute(mine, "c", swap)
    out = local_intensity(place, mine, other, wigner, rows, thin)
    return out + lax.ppermute(out, "deg", swap)


def solution(mesh):
    grid = Mesh(mesh.devices.reshape(4, 2, 4, 2, 2, 2), ("y", "xl", "zh", "zl", "c", "deg"))
    slab = ("y", "xl", "zh", "zl", "c")
    in_specs = (
        P(slab, "deg", None),
        P(slab),
        P(slab),
        P(slab),
        P(),
        P(None, "deg", None),
        P(slab, "deg", None, None),
    )
    return jax.shard_map(
        per_device, mesh=grid, in_specs=in_specs, out_specs=P(slab, None), check_vma=False
    )
```

time: 115 us -> 90.4 us (0.79)
  Pallas kernels: 37 us -> 17.4 us
  waiting for transfers between devices: 12.8 us -> 10.1 us
  other arithmetic: 2.56 us -> 1.4 us
    pallas_call x2, Pallas kernels: 36 us -> 16.3 us  [the longest x1 14 us: local_amplitude(): pl.pallas_call(functools.partial(amplitude_kernel, scale, rows, thin), in...]
    ppermute x1, waiting for transfers between devices: 4.37 us -> 2.47 us  [per_device(): recv = lax.ppermute(give, 'c', swap)]
where the time goes in v5:
time: 90.4 us; the launch traced here: 90.2 us
  blocking collectives  41.8 us (46%)
  Pallas kernels  17.4 us (19%)
  starting transfers between devices  17.3 us (19%)
  waiting for transfers between devices  10.1 us (11%)
  local copies, waits for them, and re-layouts  2.15 us (2%)
  other arithmetic  1.4 us (2%)
    all_to_all x1, blocking collectives, per_device(): near = lax.all_to_all(near, NEAR, 0, 0)  21.1 us
    all_to_all x1, blocking collectives, per_device(): mine = lax.all_to_all(spread, NEAR, 0, 0).reshape(total, qcount)  20.7 us
    pallas_call x1, Pallas kernels, local_amplitude(): pl.pallas_call(functools.partial(amplitude_kernel, scale, rows, thin), in...  14 us
    ppermute x3, starting transfers between devices, per_device(): lax.ppermute(code, FAR, [(i, (i + k) % 4) for i in range(4)])  8.64 us
    ppermute x3, waiting for transfers between devices, per_device(): lax.ppermute(code, FAR, [(i, (i + k) % 4) for i in range(4)])  3.71 us
    ppermute x1, starting transfers between devices, per_device(): recv = lax.ppermute(give, 'c', swap)  3.32 us
    ppermute x1, starting transfers between devices, per_device(): other = lax.ppermute(mine, 'c', swap)  2.83 us
    ppermute x1, starting transfers between devices, per_device(): return out + lax.ppermute(out, 'deg', swap)  2.52 us
  transfers between devices with their start and end apart: 6, of which 4 were waited for; matrix products, arithmetic and copies ran while one was open for 0% of the time, Pallas kernels for 0%

profile of v5, /device:TPU:1, one launch (start us, length us, event | category | flops | bytes accessed | tf_op | source)
XLA Modules:
  0.0 90.2 jit_solution(10526959840004297014)
XLA Ops:
  0.0 0.1 pad_add_fusion.place
  0.1 0.7 fusion.3
  0.8 0.0 copy-start.1
  0.8 1.5 %copy-done.1 = f32[64,26,256]{2,0,1:T(8,128)S(1)} copy-done((f32[64,26,256]{2,0,1:T(8,128)S(1)}, f32[64,26,256]{2,0,1:T(8,128)}, u32[]{:S(2)}) %copy-start.1) | copy-done | bytes 1703960
  2.3 0.0 copy-start.2
  2.3 0.7 copy-done.2
  3.0 14.0 %shard_map.73 = (f32[2176,256]{1,0:T(8,128)S(1)}, s16[16,144,256]{2,1,0:T(8,128)(2,1)S(1)}) custom-call(s32[2]{0:T(128)S(1)} %pad_add_fusion.place, s32[1,1024]{1,0:T(1,128)S(1)} %bitcast.8, bf16[26,1024,128]{2,1,0:T(8,128)(2,1)} %bitcast.10, f32[26,64,256]{2,1,0:T(8,128)S(1)} %bitcast.9, f32[8,256]{1,0:T(8,128)S(1)} %copy-done.2), custom_call_target="tpu_custom_call" | custom-call | flops 8220835840 | bytes 8519680 | tf_op jit(solution)/shard_map/pallas_call | solution.py:125
  17.0 3.3 %collective-permute-start = (s16[16,144,256]{2,1,0:T(8,128)(2,1)S(1)}, s16[16,144,256]{2,1,0:T(8,128)(2,1)S(1)}, u32[]{:S(2)}, u32[]{:S(2)}) collective-permute-start(s16[16,144,256]{2,1,0:T(8,128)(2,1)S(1)} %get-tuple-element.10), channel_id=1, source_target_pairs={{0,2},{2,0},{1,3},{3,1},{4,6},{6,4},{5,7},{7,5},{8,10},{10,8},{9,1... | collective-permute-start | bytes 3538952 | tf_op jit(solution)/shard_map/ppermute | solution.py:264
  20.3 2.5 %collective-permute-done.recv = s16[16,144,256]{2,1,0:T(8,128)(2,1)S(1)} collective-permute-done((s16[16,144,256]{2,1,0:T(8,128)(2,1)S(1)}, s16[16,144,256]{2,1,0:T(8,128)(2,1)S(1)}, u32[]{:S(2)}, u32[]{:S(2)}) %collective-permute-start) | collective-permute-done | bytes 1179680 | tf_op jit(solution)/shard_map/ppermute | solution.py:264
  22.8 0.7 shard_map.74
  23.5 21.1 %all_to_all.10.near = s16[16,144,256]{2,1,0:T(8,128)(2,1)S(1)} all-to-all(s16[16,144,256]{2,1,0:T(8,128)(2,1)S(1)} %shard_map.74), channel_id=1, replica_groups=mesh['y'=4,'xl'=2,'zh'=4,'zl'=2,'c'=2,'deg'=2] {'y','xl','zl'}, dimensions={0} | all-to-all | bytes 2359296 | tf_op jit(solution)/shard_map/all_to_all | solution.py:273
  44.6 0.4 shard_map.75
  45.0 6.3 %collective-permute-start.3 = (s16[144,256]{1,0:T(8,128)(2,1)S(1)}, s16[144,256]{1,0:T(8,128)(2,1)S(1)}, u32[]{:S(2)}, u32[]{:S(2)}) collective-permute-start(s16[144,256]{1,0:T(8,128)(2,1)S(1)} %get-tuple-element.12), channel_id=1, source_target_pairs={{0,16},{8,24},{16,0},{24,8},{1,17},{9,25},{17,1},{25,9},{2,18},{10... | collective-permute-start | bytes 221192 | tf_op jit(solution)/shard_map/ppermute | solution.py:283
  51.3 0.3 collective-permute-start.2
  51.5 2.1 %collective-permute-start.1 = (s16[144,256]{1,0:T(8,128)(2,1)S(1)}, s16[144,256]{1,0:T(8,128)(2,1)S(1)}, u32[]{:S(2)}, u32[]{:S(2)}) collective-permute-start(s16[144,256]{1,0:T(8,128)(2,1)S(1)} %get-tuple-element.12), channel_id=1, source_target_pairs={{0,8},{8,16},{16,24},{24,0},{1,9},{9,17},{17,25},{25,1},{2,10},{10... | collective-permute-start | bytes 221192 | tf_op jit(solution)/shard_map/ppermute | solution.py:283
  53.6 0.0 collective-permute-done.3.across
  53.6 3.7 %collective-permute-done.2.before = s16[144,256]{1,0:T(8,128)(2,1)S(1)} collective-permute-done((s16[144,256]{1,0:T(8,128)(2,1)S(1)}, s16[144,256]{1,0:T(8,128)(2,1)S(1)}, u32[]{:S(2)}, u32[]{:S(2)}) %collective-permute-start.2) | collective-permute-done | bytes 73760 | tf_op jit(solution)/shard_map/ppermute | solution.py:283
  57.3 0.0 collective-permute-done.1.after
  57.3 0.0 copy-start
  57.3 0.1 shard_map.76
  57.4 20.7 %all_to_all.11 = bf16[16,136,256]{2,1,0:T(8,128)(2,1)S(1)} all-to-all(bf16[16,136,256]{2,1,0:T(8,128)(2,1)S(1)} %shard_map.76), channel_id=1, replica_groups=mesh['y'=4,'xl'=2,'zh'=4,'zl'=2,'c'=2,'deg'=2] {'y','xl','zl'}, dimensions={0} | all-to-all | bytes 2228224 | tf_op jit(solution)/shard_map/all_to_all | solution.py:291
  78.1 2.8 %collective-permute-start.4 = (bf16[2176,256]{1,0:T(8,128)(2,1)S(1)}, bf16[2176,256]{1,0:T(8,128)(2,1)S(1)}, u32[]{:S(2)}, u32[]{:S(2)}) collective-permute-start(bf16[2176,256]{1,0:T(8,128)(2,1)S(1)} %bitcast.6), channel_id=1, source_target_pairs={{0,2},{2,0},{1,3},{3,1},{4,6},{6,4},{5,7},{7,5},{8,10},{10,8},{9,1... | collective-permute-start | bytes 3342344 | tf_op jit(solution)/shard_map/ppermute | solution.py:292
  80.9 2.4 %collective-permute-done.4.other = bf16[2176,256]{1,0:T(8,128)(2,1)S(1)} collective-permute-done((bf16[2176,256]{1,0:T(8,128)(2,1)S(1)}, bf16[2176,256]{1,0:T(8,128)(2,1)S(1)}, u32[]{:S(2)}, u32[]{:S(2)}) %collective-permute-start.4) | collective-permute-done | bytes 1114144 | tf_op jit(solution)/shard_map/ppermute | solution.py:292
  83.3 0.0 copy-done
  83.3 2.2 %shard_map.77 = f32[4,256]{1,0:T(4,128)S(1)} custom-call(s32[2]{0:T(128)S(1)} %pad_add_fusion.place, bf16[2176,256]{1,0:T(8,128)(2,1)S(1)} %bitcast.7, bf16[2176,256]{1,0:T(8,128)(2,1)S(1)} %collective-permute-done.4.other, bf16[4,26,128,128]{3,2,1,0:T(8,128)(2,1)S(1)} %copy-done), custom_call_target="tpu_custom_call" | custom-call | flops 872415232 | bytes 5636096 | tf_op jit(solution)/shard_map/pallas_call | solution.py:193
  85.5 2.5 %collective-permute-start.5 = (f32[4,256]{1,0:T(4,128)S(1)}, f32[4,256]{1,0:T(4,128)S(1)}, u32[]{:S(2)}, u32[]{:S(2)}) collective-permute-start(f32[4,256]{1,0:T(4,128)S(1)} %shard_map.77), channel_id=1, source_target_pairs={{0,1},{1,0},{2,3},{3,2},{4,5},{5,4},{6,7},{7,6},{8,9},{9,8},{10,11... | collective-permute-start | bytes 12296 | tf_op jit(solution)/shard_map/ppermute | solution.py:294
  88.1 1.5 %collective-permute-done.5 = f32[4,256]{1,0:T(4,128)S(1)} collective-permute-done((f32[4,256]{1,0:T(4,128)S(1)}, f32[4,256]{1,0:T(4,128)S(1)}, u32[]{:S(2)}, u32[]{:S(2)}) %collective-permute-start.5) | collective-permute-done | bytes 4128 | tf_op jit(solution)/shard_map/ppermute | solution.py:294
  89.6 0.6 add.11
Async XLA Ops:
  0.8 1.5 %copy-start.1 = (f32[64,26,256]{2,0,1:T(8,128)S(1)}, f32[64,26,256]{2,0,1:T(8,128)}, u32[]{:S(2)}) copy-start(f32[64,26,256]{2,0,1:T(8,128)} %param.12) | copy-start | bytes 5111812
  2.3 0.7 copy-start.2
  17.0 5.8 %collective-permute-start = (s16[16,144,256]{2,1,0:T(8,128)(2,1)S(1)}, s16[16,144,256]{2,1,0:T(8,128)(2,1)S(1)}, u32[]{:S(2)}, u32[]{:S(2)}) collective-permute-start(s16[16,144,256]{2,1,0:T(8,128)(2,1)S(1)} %get-tuple-element.10), channel_id=1, source_target_pairs={{0,2},{2,0},{1,3},{3,1},{4,6},{6,4},{5,7},{7,5},{8,10},{10,8},{9,1... | collective-permute-start | bytes 3538952 | tf_op jit(solution)/shard_map/ppermute | solution.py:264
  45.0 8.6 %collective-permute-start.3 = (s16[144,256]{1,0:T(8,128)(2,1)S(1)}, s16[144,256]{1,0:T(8,128)(2,1)S(1)}, u32[]{:S(2)}, u32[]{:S(2)}) collective-permute-start(s16[144,256]{1,0:T(8,128)(2,1)S(1)} %get-tuple-element.12), channel_id=1, source_target_pairs={{0,16},{8,24},{16,0},{24,8},{1,17},{9,25},{17,1},{25,9},{2,18},{10... | collective-permute-start | bytes 221192 | tf_op jit(solution)/shard_map/ppermute | solution.py:283
  51.3 6.1 %collective-permute-start.2 = (s16[144,256]{1,0:T(8,128)(2,1)S(1)}, s16[144,256]{1,0:T(8,128)(2,1)S(1)}, u32[]{:S(2)}, u32[]{:S(2)}) collective-permute-start(s16[144,256]{1,0:T(8,128)(2,1)S(1)} %get-tuple-element.12), channel_id=1, source_target_pairs={{0,24},{8,0},{16,8},{24,16},{1,25},{9,1},{17,9},{25,17},{2,26},{10... | collective-permute-start | bytes 221192 | tf_op jit(solution)/shard_map/ppermute | solution.py:283
  51.5 5.8 %collective-permute-start.1 = (s16[144,256]{1,0:T(8,128)(2,1)S(1)}, s16[144,256]{1,0:T(8,128)(2,1)S(1)}, u32[]{:S(2)}, u32[]{:S(2)}) collective-permute-start(s16[144,256]{1,0:T(8,128)(2,1)S(1)} %get-tuple-element.12), channel_id=1, source_target_pairs={{0,8},{8,16},{16,24},{24,0},{1,9},{9,17},{17,25},{25,1},{2,10},{10... | collective-permute-start | bytes 221192 | tf_op jit(solution)/shard_map/ppermute | solution.py:283
  57.3 26.0 %copy-start = (bf16[4,26,128,128]{3,2,1,0:T(8,128)(2,1)S(1)}, bf16[4,26,128,128]{3,2,1,0:T(8,128)(2,1)}, u32[]{:S(2)}) copy-start(bf16[4,26,128,128]{3,2,1,0:T(8,128)(2,1)} %wigner.1) | copy-start | bytes 10223620
  78.1 5.2 %collective-permute-start.4 = (bf16[2176,256]{1,0:T(8,128)(2,1)S(1)}, bf16[2176,256]{1,0:T(8,128)(2,1)S(1)}, u32[]{:S(2)}, u32[]{:S(2)}) collective-permute-start(bf16[2176,256]{1,0:T(8,128)(2,1)S(1)} %bitcast.6), channel_id=1, source_target_pairs={{0,2},{2,0},{1,3},{3,1},{4,6},{6,4},{5,7},{7,5},{8,10},{10,8},{9,1... | collective-permute-start | bytes 3342344 | tf_op jit(solution)/shard_map/ppermute | solution.py:292
  85.5 4.0 %collective-permute-start.5 = (f32[4,256]{1,0:T(4,128)S(1)}, f32[4,256]{1,0:T(4,128)S(1)}, u32[]{:S(2)}, u32[]{:S(2)}) collective-permute-start(f32[4,256]{1,0:T(4,128)S(1)} %shard_map.77), channel_id=1, source_target_pairs={{0,1},{1,0},{2,3},{3,2},{4,5},{5,4},{6,7},{7,6},{8,9},{9,8},{10,11... | collective-permute-start | bytes 12296 | tf_op jit(solution)/shard_map/ppermute | solution.py:294

commit v6 on v5

--- a/solution.py
+++ b/solution.py
@@ -25,17 +25,19 @@
     return [sum(rows[:j]) for j in range(len(rows))]
 
 
-def coded(x, spare):
-    top = jnp.maximum(jnp.max(jnp.abs(x), axis=0, keepdims=True), 1e-30)
+def coded(x):
+    last = x.shape[0] - 1
+    order = lax.broadcasted_iota(jnp.int32, x.shape, 0)
+    size = jnp.where(order < last, jnp.abs(x), 0.0)
+    top = jnp.maximum(jnp.max(size, axis=0, keepdims=True), 1e-30)
     power = jnp.floor(jnp.log2(top)) + 1.0
     steps = jnp.clip(jnp.round(x * jnp.exp2(15.0 - power)), -32767.0, 32767.0)
-    tail = jnp.broadcast_to(power, (spare, x.shape[1]))
-    return jnp.concatenate([steps, tail], axis=0).astype(jnp.int32).astype(jnp.int16)
-
-
-def decoded(block, rows):
+    return jnp.where(order < last, steps, power).astype(jnp.int32).astype(jnp.int16)
+
+
+def decoded(block):
     wide = block.astype(jnp.int32).astype(jnp.float32)
-    return wide[:rows] * jnp.exp2(wide[rows : rows + 1] - 15.0)
+    return wide * jnp.exp2(wide[block.shape[0] - 1 :] - 15.0)
 
 
 def amplitude_kernel(
@@ -62,9 +64,10 @@
         same = slots == jnp.concatenate([tall] * (2 * BINS // width), axis=1)
         onehot[i * width : (i + 1) * width, :] = jnp.where(same, 1.0, 0.0).astype(jnp.bfloat16)
     used = sum(thin)
-    blank = jnp.zeros((keep.shape[0] - used, qcount), jnp.float32)
-    keep[used:, :] = blank
-    away[used:, :] = blank
+    base = used // 8 * 8
+    blank = jnp.zeros((keep.shape[0] - base, qcount), jnp.float32)
+    keep[base:, :] = blank
+    away[base:, :] = blank
 
     wide_at, thin_at = starts(rows), starts(thin)
 
@@ -109,9 +112,10 @@
     form_copy.wait()
     for j in range(degs):
         mix(j)
-    height = keep.shape[0] // give.shape[0]
+    height = give.shape[1]
     for i in range(give.shape[0]):
-        give[i] = coded(away[i * height : (i + 1) * height, :], give.shape[1] - height)
+        at = i * (height - 1)
+        give[i] = coded(away[at : at + height, :])
 
 
 def local_amplitude(place, keys, harmonic, bessel, form, height, scale, rows, thin):
@@ -119,8 +123,8 @@
     qcount = form.shape[1]
     live_rows = sum(rows)
     outs = [
-        jax.ShapeDtypeStruct((PLANE * height, qcount), jnp.float32),
-        jax.ShapeDtypeStruct((PLANE, height + 8, qcount), jnp.int16),
+        jax.ShapeDtypeStruct((PLANE * (height - 1) + 8, qcount), jnp.float32),
+        jax.ShapeDtypeStruct((PLANE, height, qcount), jnp.int16),
     ]
     return pl.pallas_call(
         functools.partial(amplitude_kernel, scale, rows, thin),
@@ -157,38 +161,45 @@
 
 def turn_kernel(rows, thin, place, mine, other, wigner, out, first, second):
     rots, degs, width, _ = wigner.shape
-    qcount = mine.shape[1]
+    qcount = mine.shape[2]
+
+    height = mine.shape[1]
+
+    def unpack(block, into):
+        for i in range(block.shape[0]):
+            at = i * (height - 1)
+            into[at : at + height, :] = block[i].astype(jnp.float32)
 
     @pl.when(place[1] == 0)
     def _():
-        first[...] = mine[...].astype(jnp.float32)
-        second[...] = other[...].astype(jnp.float32)
+        unpack(mine, first)
+        unpack(other, second)
 
     @pl.when(place[1] != 0)
     def _():
-        first[...] = other[...].astype(jnp.float32)
-        second[...] = mine[...].astype(jnp.float32)
-
+        unpack(other, first)
+        unpack(mine, second)
+
+    order = lax.broadcasted_iota(jnp.int32, (width, qcount), 0)
     acc = [jnp.zeros((8, qcount), jnp.float32)] * rots
     thin_at = starts(thin)
     for j in range(degs):
         wide, some, at = rows[j], thin[j], thin_at[j]
-        right = second[at : at + some, :]
-        pad = jnp.zeros((width - some, qcount), jnp.float32)
-        right = jnp.concatenate([right, pad], axis=0).astype(jnp.bfloat16)
+        right = jnp.where(order < some, second[at : at + width, :], 0.0).astype(jnp.bfloat16)
         blocks = jnp.concatenate([wigner[r, j][:wide] for r in range(rots)], axis=0)
         turned = jnp.dot(blocks, right, preferred_element_type=jnp.float32)
-        left = first[at : at + some, :]
+        left = jnp.where(order[:wide] < some, first[at : at + wide, :], 0.0)
         for r in range(rots):
-            prod = turned[r * wide : r * wide + some] * left
-            acc[r] = acc[r] + jnp.sum(prod.reshape(some // 8, 8, qcount), axis=0)
+            prod = turned[r * wide : (r + 1) * wide] * left
+            acc[r] = acc[r] + jnp.sum(prod.reshape(wide // 8, 8, qcount), axis=0)
     for r in range(rots):
         out[r : r + 1, :] = jnp.sum(acc[r], axis=0, keepdims=True) * (0.5 / degs)
 
 
 def local_intensity(place, mine, other, wigner, rows, thin):
     rots = wigner.shape[0]
-    total, qcount = mine.shape
+    parts, height, qcount = mine.shape
+    total = -(-(parts * (height - 1) + wigner.shape[2]) // 8) * 8
     vmem = pl.BlockSpec(memory_space=pltpu.VMEM)
     return pl.pallas_call(
         functools.partial(turn_kernel, rows, thin),
@@ -205,24 +216,24 @@
     )(place, mine, other, wigner)
 
 
-def near_kernel(rows, keep, recv, out):
+def near_kernel(keep, recv, out):
+    height = out.shape[1]
     for i in range(out.shape[0]):
-        at = pl.ds(i * rows, rows)
-        out[i] = coded(keep[at, :] + decoded(recv[i], rows), out.shape[1] - rows)
-
-
-def plane_kernel(rows, near, total, code):
-    acc = decoded(near[0], rows)
+        at = i * (height - 1)
+        out[i] = coded(keep[at : at + height, :] + decoded(recv[i]))
+
+
+def plane_kernel(near, total, code):
+    acc = decoded(near[0])
     for i in range(1, near.shape[0]):
-        acc = acc + decoded(near[i], rows)
+        acc = acc + decoded(near[i])
     total[...] = acc
-    code[...] = coded(acc, code.shape[0] - rows)
+    code[...] = coded(acc)
 
 
 def whole_kernel(total, after, before, across, out):
-    rows = total.shape[0]
-    acc = total[...] + decoded(across[...], rows)
-    acc = acc + (decoded(after[...], rows) + decoded(before[...], rows))
+    acc = total[...] + decoded(across[...])
+    acc = acc + (decoded(after[...]) + decoded(before[...]))
     block = acc.astype(jnp.bfloat16)
     for i in range(out.shape[0]):
         out[i] = block
@@ -242,9 +253,8 @@
 def per_device(harmonic, shell, atom_type, domain, form, bessel, wigner):
     atom_rows, local_deg, width = harmonic.shape
     qcount = form.shape[1]
-    rows, thin = widths(local_deg, 16), widths(local_deg, 8)
-    height = -(-sum(thin) // (8 * PLANE)) * 8
-    total = height * PLANE
+    rows, thin = widths(local_deg, 16), widths(local_deg, 1)
+    height = -(-sum(thin) // PLANE) + 1
     core = lax.axis_index("c")
     swap = [(0, 1), (1, 0)]
     place = jnp.stack([lax.axis_index("deg") * local_deg, core]).astype(jnp.int32)
@@ -262,9 +272,9 @@
         thin,
     )
     recv = lax.ppermute(give, "c", swap)
-    coded_shape = (height + 8, qcount)
+    coded_shape = (height, qcount)
     near = whole_call(
-        functools.partial(near_kernel, height),
+        near_kernel,
         jax.ShapeDtypeStruct((PLANE,) + coded_shape, jnp.int16),
         LIMIT,
         keep,
@@ -272,7 +282,7 @@
     )
     near = lax.all_to_all(near, NEAR, 0, 0)
     part, code = whole_call(
-        functools.partial(plane_kernel, height),
+        plane_kernel,
         [
             jax.ShapeDtypeStruct((height, qcount), jnp.float32),
             jax.ShapeDtypeStruct(coded_shape, jnp.int16),
@@ -288,7 +298,7 @@
         part,
         *turns,
     )
-    mine = lax.all_to_all(spread, NEAR, 0, 0).reshape(total, qcount)
+    mine = lax.all_to_all(spread, NEAR, 0, 0)
     other = lax.ppermute(mine, "c", swap)
     out = local_intensity(place, mine, other, wigner, rows, thin)
     return out + lax.ppermute(out, "deg", swap)

time: 90.4 us -> 87.5 us (0.968)
  blocking collectives: 41.8 us -> 35.7 us
  starting transfers between devices: 17.3 us -> 19.7 us
  Pallas kernels: 17.4 us -> 18.9 us
    all_to_all x1, blocking collectives: 20.7 us -> 17.1 us  [per_device(): mine = lax.all_to_all(spread, NEAR, 0, 0)]
    all_to_all x1, blocking collectives: 21.1 us -> 18.6 us  [per_device(): near = lax.all_to_all(near, NEAR, 0, 0)]
    ppermute x1, starting transfers between devices: 2.83 us -> 5.19 us  [per_device(): other = lax.ppermute(mine, 'c', swap)]
  transfers between devices with their start and end apart: 6 -> 6, of which waited for: 4 -> 5; matrix products, arithmetic and copies ran while one was open for 0% -> 0% of each run, Pallas kernels for 0% -> 0%
where the time goes in v6:
time: 87.5 us; the launch traced here: 87.2 us
  blocking collectives  35.7 us (41%)
  starting transfers between devices  19.7 us (23%)
  Pallas kernels  18.9 us (22%)
  waiting for transfers between devices  9.25 us (11%)
  local copies, waits for them, and re-layouts  2.16 us (2%)
  other arithmetic  1.4 us (2%)
    all_to_all x1, blocking collectives, per_device(): near = lax.all_to_all(near, NEAR, 0, 0)  18.6 us
    all_to_all x1, blocking collectives, per_device(): mine = lax.all_to_all(spread, NEAR, 0, 0)  17.1 us
    pallas_call x1, Pallas kernels, local_amplitude(): pl.pallas_call(functools.partial(amplitude_kernel, scale, rows, thin), in...  14.9 us
    ppermute x3, starting transfers between devices, per_device(): lax.ppermute(code, FAR, [(i, (i + k) % 4) for i in range(4)])  8.46 us
    ppermute x1, starting transfers between devices, per_device(): other = lax.ppermute(mine, 'c', swap)  5.19 us
    ppermute x1, starting transfers between devices, per_device(): recv = lax.ppermute(give, 'c', swap)  3.5 us
    ppermute x3, waiting for transfers between devices, per_device(): lax.ppermute(code, FAR, [(i, (i + k) % 4) for i in range(4)])  3.18 us
    ppermute x1, starting transfers between devices, per_device(): return out + lax.ppermute(out, 'deg', swap)  2.55 us
  transfers between devices with their start and end apart: 6, of which 5 were waited for; matrix products, arithmetic and copies ran while one was open for 0% of the time, Pallas kernels for 0%

profile of v6, /device:TPU:1, one launch (start us, length us, event | category | flops | bytes accessed | tf_op | source)
XLA Modules:
  0.0 87.2 jit_solution(3274693849328701314)
XLA Ops:
  0.0 0.1 pad_add_fusion.place
  0.1 0.7 fusion.3
  0.8 0.0 copy-start.1
  0.8 1.5 %copy-done.1 = f32[64,26,256]{2,0,1:T(8,128)S(1)} copy-done((f32[64,26,256]{2,0,1:T(8,128)S(1)}, f32[64,26,256]{2,0,1:T(8,128)}, u32[]{:S(2)}) %copy-start.1) | copy-done | bytes 1703960
  2.3 0.0 copy-start.2
  2.3 0.7 copy-done.2
  3.0 14.9 %shard_map.73 = (f32[2040,256]{1,0:T(8,128)S(1)}, s16[16,128,256]{2,1,0:T(8,128)(2,1)S(1)}) custom-call(s32[2]{0:T(128)S(1)} %pad_add_fusion.place, s32[1,1024]{1,0:T(1,128)S(1)} %bitcast.5, bf16[26,1024,128]{2,1,0:T(8,128)(2,1)} %bitcast.7, f32[26,64,256]{2,1,0:T(8,128)S(1)} %bitcast.6, f32[8,256]{1,0:T(8,128)S(1)} %copy-done.2), custom_call_target="tpu_custom_call" | custom-call | flops 8220835840 | bytes 8519680 | tf_op jit(solution)/shard_map/pallas_call | solution.py:129
  17.8 3.5 %collective-permute-start = (s16[16,128,256]{2,1,0:T(8,128)(2,1)S(1)}, s16[16,128,256]{2,1,0:T(8,128)(2,1)S(1)}, u32[]{:S(2)}, u32[]{:S(2)}) collective-permute-start(s16[16,128,256]{2,1,0:T(8,128)(2,1)S(1)} %get-tuple-element.10), channel_id=1, source_target_pairs={{0,2},{2,0},{1,3},{3,1},{4,6},{6,4},{5,7},{7,5},{8,10},{10,8},{9,1... | collective-permute-start | bytes 3145736 | tf_op jit(solution)/shard_map/ppermute | solution.py:274
  21.3 2.3 %collective-permute-done.recv = s16[16,128,256]{2,1,0:T(8,128)(2,1)S(1)} collective-permute-done((s16[16,128,256]{2,1,0:T(8,128)(2,1)S(1)}, s16[16,128,256]{2,1,0:T(8,128)(2,1)S(1)}, u32[]{:S(2)}, u32[]{:S(2)}) %collective-permute-start) | collective-permute-done | bytes 1048608 | tf_op jit(solution)/shard_map/ppermute | solution.py:274
  23.6 1.3 %shard_map.74 = s16[16,128,256]{2,1,0:T(8,128)(2,1)S(1)} custom-call(f32[2040,256]{1,0:T(8,128)S(1)} %get-tuple-element.9.keep, s16[16,128,256]{2,1,0:T(8,128)(2,1)S(1)} %collective-permute-done.recv), custom_call_target="tpu_custom_call" | custom-call | tf_op jit(solution)/shard_map/pallas_call | solution.py:244
  25.0 0.0 copy-start
  25.0 18.6 %all_to_all.10.near = s16[16,128,256]{2,1,0:T(8,128)(2,1)S(1)} all-to-all(s16[16,128,256]{2,1,0:T(8,128)(2,1)S(1)} %shard_map.74), channel_id=1, replica_groups=mesh['y'=4,'xl'=2,'zh'=4,'zl'=2,'c'=2,'deg'=2] {'y','xl','zl'}, dimensions={0} | all-to-all | bytes 2097152 | tf_op jit(solution)/shard_map/all_to_all | solution.py:283
  43.5 0.3 shard_map.75
  43.9 6.1 %collective-permute-start.3 = (s16[128,256]{1,0:T(8,128)(2,1)S(1)}, s16[128,256]{1,0:T(8,128)(2,1)S(1)}, u32[]{:S(2)}, u32[]{:S(2)}) collective-permute-start(s16[128,256]{1,0:T(8,128)(2,1)S(1)} %get-tuple-element.12), channel_id=1, source_target_pairs={{0,16},{8,24},{16,0},{24,8},{1,17},{9,25},{17,1},{25,9},{2,18},{10... | collective-permute-start | bytes 196616 | tf_op jit(solution)/shard_map/ppermute | solution.py:293
  50.0 0.3 collective-permute-start.2
  50.2 2.1 %collective-permute-start.1 = (s16[128,256]{1,0:T(8,128)(2,1)S(1)}, s16[128,256]{1,0:T(8,128)(2,1)S(1)}, u32[]{:S(2)}, u32[]{:S(2)}) collective-permute-start(s16[128,256]{1,0:T(8,128)(2,1)S(1)} %get-tuple-element.12), channel_id=1, source_target_pairs={{0,8},{8,16},{16,24},{24,0},{1,9},{9,17},{17,25},{25,1},{2,10},{10... | collective-permute-start | bytes 196616 | tf_op jit(solution)/shard_map/ppermute | solution.py:293
  52.3 0.0 collective-permute-done.3.across
  52.3 2.4 %collective-permute-done.2.before = s16[128,256]{1,0:T(8,128)(2,1)S(1)} collective-permute-done((s16[128,256]{1,0:T(8,128)(2,1)S(1)}, s16[128,256]{1,0:T(8,128)(2,1)S(1)}, u32[]{:S(2)}, u32[]{:S(2)}) %collective-permute-start.2) | collective-permute-done | bytes 65568 | tf_op jit(solution)/shard_map/ppermute | solution.py:293
  54.8 0.7 collective-permute-done.1.after
  55.5 0.1 shard_map.76
  55.6 17.1 %all_to_all.11.mine = bf16[16,128,256]{2,1,0:T(8,128)(2,1)S(1)} all-to-all(bf16[16,128,256]{2,1,0:T(8,128)(2,1)S(1)} %shard_map.76), channel_id=1, replica_groups=mesh['y'=4,'xl'=2,'zh'=4,'zl'=2,'c'=2,'deg'=2] {'y','xl','zl'}, dimensions={0} | all-to-all | bytes 2097152 | tf_op jit(solution)/shard_map/all_to_all | solution.py:301
  72.8 5.2 %collective-permute-start.4 = (bf16[16,128,256]{2,1,0:T(8,128)(2,1)S(1)}, bf16[16,128,256]{2,1,0:T(8,128)(2,1)S(1)}, u32[]{:S(2)}, u32[]{:S(2)}) collective-permute-start(bf16[16,128,256]{2,1,0:T(8,128)(2,1)S(1)} %all_to_all.11.mine), channel_id=1, source_target_pairs={{0,2},{2,0},{1,3},{3,1},{4,6},{6,4},{5,7},{7,5},{8,10},{10,8},{9,1... | collective-permute-start | bytes 3145736 | tf_op jit(solution)/shard_map/ppermute | solution.py:302
  78.0 2.3 %collective-permute-done.4.other = bf16[16,128,256]{2,1,0:T(8,128)(2,1)S(1)} collective-permute-done((bf16[16,128,256]{2,1,0:T(8,128)(2,1)S(1)}, bf16[16,128,256]{2,1,0:T(8,128)(2,1)S(1)}, u32[]{:S(2)}, u32[]{:S(2)}) %collective-permute-start.4) | collective-permute-done | bytes 1048608 | tf_op jit(solution)/shard_map/ppermute | solution.py:302
  80.3 0.0 copy-done
  80.3 2.3 %shard_map.77 = f32[4,256]{1,0:T(4,128)S(1)} custom-call(s32[2]{0:T(128)S(1)} %pad_add_fusion.place, bf16[16,128,256]{2,1,0:T(8,128)(2,1)S(1)} %all_to_all.11.mine, bf16[16,128,256]{2,1,0:T(8,128)(2,1)S(1)} %collective-permute-done.4.other, bf16[4,26,128,128]{3,2,1,0:T(8,128)(2,1)S(1)} %copy-done), custom_call_target="tpu_custom_call" | custom-call | flops 872415232 | bytes 5505024 | tf_op jit(solution)/shard_map/pallas_call | solution.py:204
  82.6 2.6 %collective-permute-start.5 = (f32[4,256]{1,0:T(4,128)S(1)}, f32[4,256]{1,0:T(4,128)S(1)}, u32[]{:S(2)}, u32[]{:S(2)}) collective-permute-start(f32[4,256]{1,0:T(4,128)S(1)} %shard_map.77), channel_id=1, source_target_pairs={{0,1},{1,0},{2,3},{3,2},{4,5},{5,4},{6,7},{7,6},{8,9},{9,8},{10,11... | collective-permute-start | bytes 12296 | tf_op jit(solution)/shard_map/ppermute | solution.py:304
  85.1 1.5 %collective-permute-done.5 = f32[4,256]{1,0:T(4,128)S(1)} collective-permute-done((f32[4,256]{1,0:T(4,128)S(1)}, f32[4,256]{1,0:T(4,128)S(1)}, u32[]{:S(2)}, u32[]{:S(2)}) %collective-permute-start.5) | collective-permute-done | bytes 4128 | tf_op jit(solution)/shard_map/ppermute | solution.py:304
  86.6 0.6 add.11
Async XLA Ops:
  0.8 1.5 %copy-start.1 = (f32[64,26,256]{2,0,1:T(8,128)S(1)}, f32[64,26,256]{2,0,1:T(8,128)}, u32[]{:S(2)}) copy-start(f32[64,26,256]{2,0,1:T(8,128)} %param.12) | copy-start | bytes 5111812
  2.3 0.7 copy-start.2
  17.8 5.8 %collective-permute-start = (s16[16,128,256]{2,1,0:T(8,128)(2,1)S(1)}, s16[16,128,256]{2,1,0:T(8,128)(2,1)S(1)}, u32[]{:S(2)}, u32[]{:S(2)}) collective-permute-start(s16[16,128,256]{2,1,0:T(8,128)(2,1)S(1)} %get-tuple-element.10), channel_id=1, source_target_pairs={{0,2},{2,0},{1,3},{3,1},{4,6},{6,4},{5,7},{7,5},{8,10},{10,8},{9,1... | collective-permute-start | bytes 3145736 | tf_op jit(solution)/shard_map/ppermute | solution.py:274
  25.0 55.3 %copy-start = (bf16[4,26,128,128]{3,2,1,0:T(8,128)(2,1)S(1)}, bf16[4,26,128,128]{3,2,1,0:T(8,128)(2,1)}, u32[]{:S(2)}) copy-start(bf16[4,26,128,128]{3,2,1,0:T(8,128)(2,1)} %wigner.1) | copy-start | bytes 10223620
  43.9 8.5 %collective-permute-start.3 = (s16[128,256]{1,0:T(8,128)(2,1)S(1)}, s16[128,256]{1,0:T(8,128)(2,1)S(1)}, u32[]{:S(2)}, u32[]{:S(2)}) collective-permute-start(s16[128,256]{1,0:T(8,128)(2,1)S(1)} %get-tuple-element.12), channel_id=1, source_target_pairs={{0,16},{8,24},{16,0},{24,8},{1,17},{9,25},{17,1},{25,9},{2,18},{10... | collective-permute-start | bytes 196616 | tf_op jit(solution)/shard_map/ppermute | solution.py:293
  50.0 4.8 %collective-permute-start.2 = (s16[128,256]{1,0:T(8,128)(2,1)S(1)}, s16[128,256]{1,0:T(8,128)(2,1)S(1)}, u32[]{:S(2)}, u32[]{:S(2)}) collective-permute-start(s16[128,256]{1,0:T(8,128)(2,1)S(1)} %get-tuple-element.12), channel_id=1, source_target_pairs={{0,24},{8,0},{16,8},{24,16},{1,25},{9,1},{17,9},{25,17},{2,26},{10... | collective-permute-start | bytes 196616 | tf_op jit(solution)/shard_map/ppermute | solution.py:293
  50.2 5.3 %collective-permute-start.1 = (s16[128,256]{1,0:T(8,128)(2,1)S(1)}, s16[128,256]{1,0:T(8,128)(2,1)S(1)}, u32[]{:S(2)}, u32[]{:S(2)}) collective-permute-start(s16[128,256]{1,0:T(8,128)(2,1)S(1)} %get-tuple-element.12), channel_id=1, source_target_pairs={{0,8},{8,16},{16,24},{24,0},{1,9},{9,17},{17,25},{25,1},{2,10},{10... | collective-permute-start | bytes 196616 | tf_op jit(solution)/shard_map/ppermute | solution.py:293
  72.8 7.5 %collective-permute-start.4 = (bf16[16,128,256]{2,1,0:T(8,128)(2,1)S(1)}, bf16[16,128,256]{2,1,0:T(8,128)(2,1)S(1)}, u32[]{:S(2)}, u32[]{:S(2)}) collective-permute-start(bf16[16,128,256]{2,1,0:T(8,128)(2,1)S(1)} %all_to_all.11.mine), channel_id=1, source_target_pairs={{0,2},{2,0},{1,3},{3,1},{4,6},{6,4},{5,7},{7,5},{8,10},{10,8},{9,1... | collective-permute-start | bytes 3145736 | tf_op jit(solution)/shard_map/ppermute | solution.py:302
  82.6 4.0 %collective-permute-start.5 = (f32[4,256]{1,0:T(4,128)S(1)}, f32[4,256]{1,0:T(4,128)S(1)}, u32[]{:S(2)}, u32[]{:S(2)}) collective-permute-start(f32[4,256]{1,0:T(4,128)S(1)} %shard_map.77), channel_id=1, source_target_pairs={{0,1},{1,0},{2,3},{3,2},{4,5},{5,4},{6,7},{7,6},{8,9},{9,8},{10,11... | collective-permute-start | bytes 12296 | tf_op jit(solution)/shard_map/ppermute | solution.py:304

commit v7 on v6

--- a/solution.py
+++ b/solution.py
@@ -63,16 +63,14 @@
         tall = jnp.transpose(jnp.broadcast_to(line, (width, width)))
         same = slots == jnp.concatenate([tall] * (2 * BINS // width), axis=1)
         onehot[i * width : (i + 1) * width, :] = jnp.where(same, 1.0, 0.0).astype(jnp.bfloat16)
-    used = sum(thin)
-    base = used // 8 * 8
-    blank = jnp.zeros((keep.shape[0] - base, qcount), jnp.float32)
-    keep[base:, :] = blank
-    away[base:, :] = blank
+    height = give.shape[1]
+    blank = jnp.zeros((8, qcount), jnp.float32)
+    keep[keep.shape[0] - 8 :, :] = blank
+    away[keep.shape[0] - 8 :, :] = blank
 
     wide_at, thin_at = starts(rows), starts(thin)
 
     def turn(j):
-        fetch[j].wait()
         turned[wide_at[j] : wide_at[j] + rows[j], :] = jnp.transpose(atoms[j])[: rows[j]]
 
     def bin_rows(first, last):
@@ -99,23 +97,28 @@
         out = (main[: 2 * wide] + (main[2 * wide :] + rest)) * scale
         live = 2 * (place[0] + j) + 1
         order = lax.broadcasted_iota(jnp.int32, (wide, qcount), 0)
-        at = slice(thin_at[j], thin_at[j] + thin[j])
-        keep[at, :] = jnp.where(order < live, out[:wide], 0.0)[: thin[j]]
-        away[at, :] = jnp.where(order < live, out[wide:], 0.0)[: thin[j]]
+        mine = jnp.where(order < live, out[:wide], 0.0)
+        other = jnp.where(order < live, out[wide:], 0.0)
+        done = 0
+        while done < thin[j]:
+            part, row = divmod(thin_at[j] + done, height - 1)
+            count = min(thin[j] - done, height - 1 - row)
+            at = slice(part * height + row, part * height + row + count)
+            keep[at, :] = mine[done : done + count]
+            away[at, :] = other[done : done + count]
+            done += count
 
     cuts = [(0, 5), (6, 13), (14, 21), (22, degs - 1)]
+    for copy in fetch + [wave_copy, form_copy]:
+        copy.wait()
     for j in range(degs):
         turn(j)
     for first, last in cuts:
         bin_rows(first, last)
-    wave_copy.wait()
-    form_copy.wait()
     for j in range(degs):
         mix(j)
-    height = give.shape[1]
     for i in range(give.shape[0]):
-        at = i * (height - 1)
-        give[i] = coded(away[at : at + height, :])
+        give[i] = coded(away[i * height : (i + 1) * height, :])
 
 
 def local_amplitude(place, keys, harmonic, bessel, form, height, scale, rows, thin):
@@ -123,7 +126,7 @@
     qcount = form.shape[1]
     live_rows = sum(rows)
     outs = [
-        jax.ShapeDtypeStruct((PLANE * (height - 1) + 8, qcount), jnp.float32),
+        jax.ShapeDtypeStruct((PLANE * height, qcount), jnp.float32),
         jax.ShapeDtypeStruct((PLANE, height, qcount), jnp.int16),
     ]
     return pl.pallas_call(
@@ -219,8 +222,7 @@
 def near_kernel(keep, recv, out):
     height = out.shape[1]
     for i in range(out.shape[0]):
-        at = i * (height - 1)
-        out[i] = coded(keep[at : at + height, :] + decoded(recv[i]))
+        out[i] = coded(keep[i * height : (i + 1) * height, :] + decoded(recv[i]))
 
 
 def plane_kernel(near, total, code):

time: 87.5 us -> 85.1 us (0.973)
  Pallas kernels: 18.9 us -> 16.8 us
    pallas_call x1, Pallas kernels: 14.9 us -> 13.3 us  [local_amplitude(): pl.pallas_call(functools.partial(amplitude_kernel, scale, rows, thin), in...]
where the time goes in v7:
time: 85.1 us; the launch traced here: 84.9 us
  blocking collectives  36.2 us (43%)
  starting transfers between devices  19 us (22%)
  Pallas kernels  16.8 us (20%)
  waiting for transfers between devices  9.27 us (11%)
  local copies, waits for them, and re-layouts  2.16 us (3%)
  other arithmetic  1.4 us (2%)
    all_to_all x1, blocking collectives, per_device(): near = lax.all_to_all(near, NEAR, 0, 0)  18.6 us
    all_to_all x1, blocking collectives, per_device(): mine = lax.all_to_all(spread, NEAR, 0, 0)  17.7 us
    pallas_call x1, Pallas kernels, local_amplitude(): pl.pallas_call(functools.partial(amplitude_kernel, scale, rows, thin), in...  13.3 us
    ppermute x3, starting transfers between devices, per_device(): lax.ppermute(code, FAR, [(i, (i + k) % 4) for i in range(4)])  8.47 us
    ppermute x1, starting transfers between devices, per_device(): other = lax.ppermute(mine, 'c', swap)  4.65 us
    ppermute x1, starting transfers between devices, per_device(): recv = lax.ppermute(give, 'c', swap)  3.33 us
    ppermute x3, waiting for transfers between devices, per_device(): lax.ppermute(code, FAR, [(i, (i + k) % 4) for i in range(4)])  3.18 us
    ppermute x1, starting transfers between devices, per_device(): return out + lax.ppermute(out, 'deg', swap)  2.54 us
  transfers between devices with their start and end apart: 6, of which 5 were waited for; matrix products, arithmetic and copies ran while one was open for 0% of the time, Pallas kernels for 0%

profile of v7, /device:TPU:1, one launch (start us, length us, event | category | flops | bytes accessed | tf_op | source)
XLA Modules:
  0.0 84.9 jit_solution(12142316675431507858)
XLA Ops:
  0.0 0.1 pad_add_fusion.place
  0.1 0.7 fusion.3
  0.8 0.0 copy-start.1
  0.8 1.5 %copy-done.1 = f32[64,26,256]{2,0,1:T(8,128)S(1)} copy-done((f32[64,26,256]{2,0,1:T(8,128)S(1)}, f32[64,26,256]{2,0,1:T(8,128)}, u32[]{:S(2)}) %copy-start.1) | copy-done | bytes 1703960
  2.3 0.0 copy-start.2
  2.3 0.7 copy-done.2
  3.0 13.3 %shard_map.73 = (f32[2048,256]{1,0:T(8,128)S(1)}, s16[16,128,256]{2,1,0:T(8,128)(2,1)S(1)}) custom-call(s32[2]{0:T(128)S(1)} %pad_add_fusion.place, s32[1,1024]{1,0:T(1,128)S(1)} %bitcast.5, bf16[26,1024,128]{2,1,0:T(8,128)(2,1)} %bitcast.7, f32[26,64,256]{2,1,0:T(8,128)S(1)} %bitcast.6, f32[8,256]{1,0:T(8,128)S(1)} %copy-done.2), custom_call_target="tpu_custom_call" | custom-call | flops 8220835840 | bytes 8519680 | tf_op jit(solution)/shard_map/pallas_call | solution.py:132
  16.3 3.3 %collective-permute-start = (s16[16,128,256]{2,1,0:T(8,128)(2,1)S(1)}, s16[16,128,256]{2,1,0:T(8,128)(2,1)S(1)}, u32[]{:S(2)}, u32[]{:S(2)}) collective-permute-start(s16[16,128,256]{2,1,0:T(8,128)(2,1)S(1)} %get-tuple-element.10), channel_id=1, source_target_pairs={{0,2},{2,0},{1,3},{3,1},{4,6},{6,4},{5,7},{7,5},{8,10},{10,8},{9,1... | collective-permute-start | bytes 3145736 | tf_op jit(solution)/shard_map/ppermute | solution.py:276
  19.6 2.3 %collective-permute-done.recv = s16[16,128,256]{2,1,0:T(8,128)(2,1)S(1)} collective-permute-done((s16[16,128,256]{2,1,0:T(8,128)(2,1)S(1)}, s16[16,128,256]{2,1,0:T(8,128)(2,1)S(1)}, u32[]{:S(2)}, u32[]{:S(2)}) %collective-permute-start) | collective-permute-done | bytes 1048608 | tf_op jit(solution)/shard_map/ppermute | solution.py:276
  21.9 0.7 shard_map.74
  22.6 0.0 copy-start
  22.6 18.6 %all_to_all.10.near = s16[16,128,256]{2,1,0:T(8,128)(2,1)S(1)} all-to-all(s16[16,128,256]{2,1,0:T(8,128)(2,1)S(1)} %shard_map.74), channel_id=1, replica_groups=mesh['y'=4,'xl'=2,'zh'=4,'zl'=2,'c'=2,'deg'=2] {'y','xl','zl'}, dimensions={0} | all-to-all | bytes 2097152 | tf_op jit(solution)/shard_map/all_to_all | solution.py:285
  41.2 0.3 shard_map.75
  41.5 6.1 %collective-permute-start.3 = (s16[128,256]{1,0:T(8,128)(2,1)S(1)}, s16[128,256]{1,0:T(8,128)(2,1)S(1)}, u32[]{:S(2)}, u32[]{:S(2)}) collective-permute-start(s16[128,256]{1,0:T(8,128)(2,1)S(1)} %get-tuple-element.12), channel_id=1, source_target_pairs={{0,16},{8,24},{16,0},{24,8},{1,17},{9,25},{17,1},{25,9},{2,18},{10... | collective-permute-start | bytes 196616 | tf_op jit(solution)/shard_map/ppermute | solution.py:295
  47.6 0.3 collective-permute-start.2
  47.9 2.1 %collective-permute-start.1 = (s16[128,256]{1,0:T(8,128)(2,1)S(1)}, s16[128,256]{1,0:T(8,128)(2,1)S(1)}, u32[]{:S(2)}, u32[]{:S(2)}) collective-permute-start(s16[128,256]{1,0:T(8,128)(2,1)S(1)} %get-tuple-element.12), channel_id=1, source_target_pairs={{0,8},{8,16},{16,24},{24,0},{1,9},{9,17},{17,25},{25,1},{2,10},{10... | collective-permute-start | bytes 196616 | tf_op jit(solution)/shard_map/ppermute | solution.py:295
  50.0 0.0 collective-permute-done.3.across
  50.0 2.4 %collective-permute-done.2.before = s16[128,256]{1,0:T(8,128)(2,1)S(1)} collective-permute-done((s16[128,256]{1,0:T(8,128)(2,1)S(1)}, s16[128,256]{1,0:T(8,128)(2,1)S(1)}, u32[]{:S(2)}, u32[]{:S(2)}) %collective-permute-start.2) | collective-permute-done | bytes 65568 | tf_op jit(solution)/shard_map/ppermute | solution.py:295
  52.4 0.7 collective-permute-done.1.after
  53.1 0.1 shard_map.76
  53.3 17.7 %all_to_all.11.mine = bf16[16,128,256]{2,1,0:T(8,128)(2,1)S(1)} all-to-all(bf16[16,128,256]{2,1,0:T(8,128)(2,1)S(1)} %shard_map.76), channel_id=1, replica_groups=mesh['y'=4,'xl'=2,'zh'=4,'zl'=2,'c'=2,'deg'=2] {'y','xl','zl'}, dimensions={0} | all-to-all | bytes 2097152 | tf_op jit(solution)/shard_map/all_to_all | solution.py:303
  71.0 4.7 %collective-permute-start.4 = (bf16[16,128,256]{2,1,0:T(8,128)(2,1)S(1)}, bf16[16,128,256]{2,1,0:T(8,128)(2,1)S(1)}, u32[]{:S(2)}, u32[]{:S(2)}) collective-permute-start(bf16[16,128,256]{2,1,0:T(8,128)(2,1)S(1)} %all_to_all.11.mine), channel_id=1, source_target_pairs={{0,2},{2,0},{1,3},{3,1},{4,6},{6,4},{5,7},{7,5},{8,10},{10,8},{9,1... | collective-permute-start | bytes 3145736 | tf_op jit(solution)/shard_map/ppermute | solution.py:304
  75.6 2.3 %collective-permute-done.4.other = bf16[16,128,256]{2,1,0:T(8,128)(2,1)S(1)} collective-permute-done((bf16[16,128,256]{2,1,0:T(8,128)(2,1)S(1)}, bf16[16,128,256]{2,1,0:T(8,128)(2,1)S(1)}, u32[]{:S(2)}, u32[]{:S(2)}) %collective-permute-start.4) | collective-permute-done | bytes 1048608 | tf_op jit(solution)/shard_map/ppermute | solution.py:304
  77.9 0.0 copy-done
  77.9 2.3 %shard_map.77 = f32[4,256]{1,0:T(4,128)S(1)} custom-call(s32[2]{0:T(128)S(1)} %pad_add_fusion.place, bf16[16,128,256]{2,1,0:T(8,128)(2,1)S(1)} %all_to_all.11.mine, bf16[16,128,256]{2,1,0:T(8,128)(2,1)S(1)} %collective-permute-done.4.other, bf16[4,26,128,128]{3,2,1,0:T(8,128)(2,1)S(1)} %copy-done), custom_call_target="tpu_custom_call" | custom-call | flops 872415232 | bytes 5505024 | tf_op jit(solution)/shard_map/pallas_call | solution.py:207
  80.2 2.5 %collective-permute-start.5 = (f32[4,256]{1,0:T(4,128)S(1)}, f32[4,256]{1,0:T(4,128)S(1)}, u32[]{:S(2)}, u32[]{:S(2)}) collective-permute-start(f32[4,256]{1,0:T(4,128)S(1)} %shard_map.77), channel_id=1, source_target_pairs={{0,1},{1,0},{2,3},{3,2},{4,5},{5,4},{6,7},{7,6},{8,9},{9,8},{10,11... | collective-permute-start | bytes 12296 | tf_op jit(solution)/shard_map/ppermute | solution.py:306
  82.8 1.5 %collective-permute-done.5 = f32[4,256]{1,0:T(4,128)S(1)} collective-permute-done((f32[4,256]{1,0:T(4,128)S(1)}, f32[4,256]{1,0:T(4,128)S(1)}, u32[]{:S(2)}, u32[]{:S(2)}) %collective-permute-start.5) | collective-permute-done | bytes 4128 | tf_op jit(solution)/shard_map/ppermute | solution.py:306
  84.3 0.6 add.11
Async XLA Ops:
  0.8 1.5 %copy-start.1 = (f32[64,26,256]{2,0,1:T(8,128)S(1)}, f32[64,26,256]{2,0,1:T(8,128)}, u32[]{:S(2)}) copy-start(f32[64,26,256]{2,0,1:T(8,128)} %param.12) | copy-start | bytes 5111812
  2.3 0.7 copy-start.2
  16.3 5.6 %collective-permute-start = (s16[16,128,256]{2,1,0:T(8,128)(2,1)S(1)}, s16[16,128,256]{2,1,0:T(8,128)(2,1)S(1)}, u32[]{:S(2)}, u32[]{:S(2)}) collective-permute-start(s16[16,128,256]{2,1,0:T(8,128)(2,1)S(1)} %get-tuple-element.10), channel_id=1, source_target_pairs={{0,2},{2,0},{1,3},{3,1},{4,6},{6,4},{5,7},{7,5},{8,10},{10,8},{9,1... | collective-permute-start | bytes 3145736 | tf_op jit(solution)/shard_map/ppermute | solution.py:276
  22.6 55.3 %copy-start = (bf16[4,26,128,128]{3,2,1,0:T(8,128)(2,1)S(1)}, bf16[4,26,128,128]{3,2,1,0:T(8,128)(2,1)}, u32[]{:S(2)}) copy-start(bf16[4,26,128,128]{3,2,1,0:T(8,128)(2,1)} %wigner.1) | copy-start | bytes 10223620
  41.5 8.5 %collective-permute-start.3 = (s16[128,256]{1,0:T(8,128)(2,1)S(1)}, s16[128,256]{1,0:T(8,128)(2,1)S(1)}, u32[]{:S(2)}, u32[]{:S(2)}) collective-permute-start(s16[128,256]{1,0:T(8,128)(2,1)S(1)} %get-tuple-element.12), channel_id=1, source_target_pairs={{0,16},{8,24},{16,0},{24,8},{1,17},{9,25},{17,1},{25,9},{2,18},{10... | collective-permute-start | bytes 196616 | tf_op jit(solution)/shard_map/ppermute | solution.py:295
  47.6 4.8 %collective-permute-start.2 = (s16[128,256]{1,0:T(8,128)(2,1)S(1)}, s16[128,256]{1,0:T(8,128)(2,1)S(1)}, u32[]{:S(2)}, u32[]{:S(2)}) collective-permute-start(s16[128,256]{1,0:T(8,128)(2,1)S(1)} %get-tuple-element.12), channel_id=1, source_target_pairs={{0,24},{8,0},{16,8},{24,16},{1,25},{9,1},{17,9},{25,17},{2,26},{10... | collective-permute-start | bytes 196616 | tf_op jit(solution)/shard_map/ppermute | solution.py:295
  47.9 5.3 %collective-permute-start.1 = (s16[128,256]{1,0:T(8,128)(2,1)S(1)}, s16[128,256]{1,0:T(8,128)(2,1)S(1)}, u32[]{:S(2)}, u32[]{:S(2)}) collective-permute-start(s16[128,256]{1,0:T(8,128)(2,1)S(1)} %get-tuple-element.12), channel_id=1, source_target_pairs={{0,8},{8,16},{16,24},{24,0},{1,9},{9,17},{17,25},{25,1},{2,10},{10... | collective-permute-start | bytes 196616 | tf_op jit(solution)/shard_map/ppermute | solution.py:295
  71.0 6.9 %collective-permute-start.4 = (bf16[16,128,256]{2,1,0:T(8,128)(2,1)S(1)}, bf16[16,128,256]{2,1,0:T(8,128)(2,1)S(1)}, u32[]{:S(2)}, u32[]{:S(2)}) collective-permute-start(bf16[16,128,256]{2,1,0:T(8,128)(2,1)S(1)} %all_to_all.11.mine), channel_id=1, source_target_pairs={{0,2},{2,0},{1,3},{3,1},{4,6},{6,4},{5,7},{7,5},{8,10},{10,8},{9,1... | collective-permute-start | bytes 3145736 | tf_op jit(solution)/shard_map/ppermute | solution.py:304
  80.2 4.0 %collective-permute-start.5 = (f32[4,256]{1,0:T(4,128)S(1)}, f32[4,256]{1,0:T(4,128)S(1)}, u32[]{:S(2)}, u32[]{:S(2)}) collective-permute-start(f32[4,256]{1,0:T(4,128)S(1)} %shard_map.77), channel_id=1, source_target_pairs={{0,1},{1,0},{2,3},{3,2},{4,5},{5,4},{6,7},{7,6},{8,9},{9,8},{10,11... | collective-permute-start | bytes 12296 | tf_op jit(solution)/shard_map/ppermute | solution.py:306

commit v8 on v7

--- a/solution.py
+++ b/solution.py
@@ -82,7 +82,7 @@
 
     def mix(j):
         wide = rows[j]
-        radial = (waves[j][:, None, :] * forms[...][None]).reshape(BINS, qcount)
+        radial = (waves[j][:, None, :] * scaled[None]).reshape(BINS, qcount)
         radial_hi = radial.astype(jnp.bfloat16)
         radial_lo = (radial - radial_hi.astype(jnp.float32)).astype(jnp.bfloat16)
         there = slice(wide_at[j], wide_at[j] + wide)
@@ -94,7 +94,7 @@
         rest = jnp.dot(
             jnp.concatenate(tops, axis=0), radial_lo, preferred_element_type=jnp.float32
         )
-        out = (main[: 2 * wide] + (main[2 * wide :] + rest)) * scale
+        out = (main[: 2 * wide] + (main[2 * wide :] + rest))
         live = 2 * (place[0] + j) + 1
         order = lax.broadcasted_iota(jnp.int32, (wide, qcount), 0)
         mine = jnp.where(order < live, out[:wide], 0.0)
@@ -109,12 +109,15 @@
             done += count
 
     cuts = [(0, 5), (6, 13), (14, 21), (22, degs - 1)]
-    for copy in fetch + [wave_copy, form_copy]:
-        copy.wait()
-    for j in range(degs):
-        turn(j)
     for first, last in cuts:
+        for copy in fetch[first : last + 1]:
+            copy.wait()
+        for j in range(first, last + 1):
+            turn(j)
         bin_rows(first, last)
+    wave_copy.wait()
+    form_copy.wait()
+    scaled = forms[...] * scale
     for j in range(degs):
         mix(j)
     for i in range(give.shape[0]):

time: 85.1 us -> 84 us (0.987)
  Pallas kernels: 16.8 us -> 15.6 us
    pallas_call x1, Pallas kernels: 13.3 us -> 12.2 us  [local_amplitude(): pl.pallas_call(functools.partial(amplitude_kernel, scale, rows, thin), in...]
where the time goes in v8:
time: 84 us; the launch traced here: 83.8 us
  blocking collectives  36.2 us (43%)
  starting transfers between devices  19 us (23%)
  Pallas kernels  15.6 us (19%)
  waiting for transfers between devices  9.27 us (11%)
  local copies, waits for them, and re-layouts  2.16 us (3%)
  other arithmetic  1.4 us (2%)
    all_to_all x1, blocking collectives, per_device(): near = lax.all_to_all(near, NEAR, 0, 0)  18.5 us
    all_to_all x1, blocking collectives, per_device(): mine = lax.all_to_all(spread, NEAR, 0, 0)  17.7 us
    pallas_call x1, Pallas kernels, local_amplitude(): pl.pallas_call(functools.partial(amplitude_kernel, scale, rows, thin), in...  12.2 us
    ppermute x3, starting transfers between devices, per_device(): lax.ppermute(code, FAR, [(i, (i + k) % 4) for i in range(4)])  8.47 us
    ppermute x1, starting transfers between devices, per_device(): other = lax.ppermute(mine, 'c', swap)  4.65 us
    ppermute x1, starting transfers between devices, per_device(): recv = lax.ppermute(give, 'c', swap)  3.33 us
    ppermute x3, waiting for transfers between devices, per_device(): lax.ppermute(code, FAR, [(i, (i + k) % 4) for i in range(4)])  3.18 us
    ppermute x1, starting transfers between devices, per_device(): return out + lax.ppermute(out, 'deg', swap)  2.53 us
  transfers between devices with their start and end apart: 6, of which 5 were waited for; matrix products, arithmetic and copies ran while one was open for 0% of the time, Pallas kernels for 0%

profile of v8, /device:TPU:1, one launch (start us, length us, event | category | flops | bytes accessed | tf_op | source)
XLA Modules:
  0.0 83.8 jit_solution(816368917011440805)
XLA Ops:
  0.0 0.1 pad_add_fusion.place
  0.1 0.7 fusion.3
  0.8 0.0 copy-start.1
  0.8 1.5 %copy-done.1 = f32[64,26,256]{2,0,1:T(8,128)S(1)} copy-done((f32[64,26,256]{2,0,1:T(8,128)S(1)}, f32[64,26,256]{2,0,1:T(8,128)}, u32[]{:S(2)}) %copy-start.1) | copy-done | bytes 1703960
  2.3 0.0 copy-start.2
  2.3 0.7 copy-done.2
  3.0 12.2 %shard_map.73 = (f32[2048,256]{1,0:T(8,128)S(1)}, s16[16,128,256]{2,1,0:T(8,128)(2,1)S(1)}) custom-call(s32[2]{0:T(128)S(1)} %pad_add_fusion.place, s32[1,1024]{1,0:T(1,128)S(1)} %bitcast.5, bf16[26,1024,128]{2,1,0:T(8,128)(2,1)} %bitcast.7, f32[26,64,256]{2,1,0:T(8,128)S(1)} %bitcast.6, f32[8,256]{1,0:T(8,128)S(1)} %copy-done.2), custom_call_target="tpu_custom_call" | custom-call | flops 8220835840 | bytes 8519680 | tf_op jit(solution)/shard_map/pallas_call | solution.py:135
  15.2 3.3 %collective-permute-start = (s16[16,128,256]{2,1,0:T(8,128)(2,1)S(1)}, s16[16,128,256]{2,1,0:T(8,128)(2,1)S(1)}, u32[]{:S(2)}, u32[]{:S(2)}) collective-permute-start(s16[16,128,256]{2,1,0:T(8,128)(2,1)S(1)} %get-tuple-element.10), channel_id=1, source_target_pairs={{0,2},{2,0},{1,3},{3,1},{4,6},{6,4},{5,7},{7,5},{8,10},{10,8},{9,1... | collective-permute-start | bytes 3145736 | tf_op jit(solution)/shard_map/ppermute | solution.py:279
  18.5 2.3 %collective-permute-done.recv = s16[16,128,256]{2,1,0:T(8,128)(2,1)S(1)} collective-permute-done((s16[16,128,256]{2,1,0:T(8,128)(2,1)S(1)}, s16[16,128,256]{2,1,0:T(8,128)(2,1)S(1)}, u32[]{:S(2)}, u32[]{:S(2)}) %collective-permute-start) | collective-permute-done | bytes 1048608 | tf_op jit(solution)/shard_map/ppermute | solution.py:279
  20.8 0.7 shard_map.74
  21.5 0.0 copy-start
  21.5 18.5 %all_to_all.10.near = s16[16,128,256]{2,1,0:T(8,128)(2,1)S(1)} all-to-all(s16[16,128,256]{2,1,0:T(8,128)(2,1)S(1)} %shard_map.74), channel_id=1, replica_groups=mesh['y'=4,'xl'=2,'zh'=4,'zl'=2,'c'=2,'deg'=2] {'y','xl','zl'}, dimensions={0} | all-to-all | bytes 2097152 | tf_op jit(solution)/shard_map/all_to_all | solution.py:288
  40.0 0.3 shard_map.75
  40.4 6.1 %collective-permute-start.3 = (s16[128,256]{1,0:T(8,128)(2,1)S(1)}, s16[128,256]{1,0:T(8,128)(2,1)S(1)}, u32[]{:S(2)}, u32[]{:S(2)}) collective-permute-start(s16[128,256]{1,0:T(8,128)(2,1)S(1)} %get-tuple-element.12), channel_id=1, source_target_pairs={{0,16},{8,24},{16,0},{24,8},{1,17},{9,25},{17,1},{25,9},{2,18},{10... | collective-permute-start | bytes 196616 | tf_op jit(solution)/shard_map/ppermute | solution.py:298
  46.5 0.3 collective-permute-start.2
  46.8 2.1 %collective-permute-start.1 = (s16[128,256]{1,0:T(8,128)(2,1)S(1)}, s16[128,256]{1,0:T(8,128)(2,1)S(1)}, u32[]{:S(2)}, u32[]{:S(2)}) collective-permute-start(s16[128,256]{1,0:T(8,128)(2,1)S(1)} %get-tuple-element.12), channel_id=1, source_target_pairs={{0,8},{8,16},{16,24},{24,0},{1,9},{9,17},{17,25},{25,1},{2,10},{10... | collective-permute-start | bytes 196616 | tf_op jit(solution)/shard_map/ppermute | solution.py:298
  48.9 0.0 collective-permute-done.3.across
  48.9 2.4 %collective-permute-done.2.before = s16[128,256]{1,0:T(8,128)(2,1)S(1)} collective-permute-done((s16[128,256]{1,0:T(8,128)(2,1)S(1)}, s16[128,256]{1,0:T(8,128)(2,1)S(1)}, u32[]{:S(2)}, u32[]{:S(2)}) %collective-permute-start.2) | collective-permute-done | bytes 65568 | tf_op jit(solution)/shard_map/ppermute | solution.py:298
  51.3 0.7 collective-permute-done.1.after
  52.0 0.1 shard_map.76
  52.2 17.7 %all_to_all.11.mine = bf16[16,128,256]{2,1,0:T(8,128)(2,1)S(1)} all-to-all(bf16[16,128,256]{2,1,0:T(8,128)(2,1)S(1)} %shard_map.76), channel_id=1, replica_groups=mesh['y'=4,'xl'=2,'zh'=4,'zl'=2,'c'=2,'deg'=2] {'y','xl','zl'}, dimensions={0} | all-to-all | bytes 2097152 | tf_op jit(solution)/shard_map/all_to_all | solution.py:306
  69.9 4.6 %collective-permute-start.4 = (bf16[16,128,256]{2,1,0:T(8,128)(2,1)S(1)}, bf16[16,128,256]{2,1,0:T(8,128)(2,1)S(1)}, u32[]{:S(2)}, u32[]{:S(2)}) collective-permute-start(bf16[16,128,256]{2,1,0:T(8,128)(2,1)S(1)} %all_to_all.11.mine), channel_id=1, source_target_pairs={{0,2},{2,0},{1,3},{3,1},{4,6},{6,4},{5,7},{7,5},{8,10},{10,8},{9,1... | collective-permute-start | bytes 3145736 | tf_op jit(solution)/shard_map/ppermute | solution.py:307
  74.5 2.3 %collective-permute-done.4.other = bf16[16,128,256]{2,1,0:T(8,128)(2,1)S(1)} collective-permute-done((bf16[16,128,256]{2,1,0:T(8,128)(2,1)S(1)}, bf16[16,128,256]{2,1,0:T(8,128)(2,1)S(1)}, u32[]{:S(2)}, u32[]{:S(2)}) %collective-permute-start.4) | collective-permute-done | bytes 1048608 | tf_op jit(solution)/shard_map/ppermute | solution.py:307
  76.8 0.0 copy-done
  76.8 2.3 %shard_map.77 = f32[4,256]{1,0:T(4,128)S(1)} custom-call(s32[2]{0:T(128)S(1)} %pad_add_fusion.place, bf16[16,128,256]{2,1,0:T(8,128)(2,1)S(1)} %all_to_all.11.mine, bf16[16,128,256]{2,1,0:T(8,128)(2,1)S(1)} %collective-permute-done.4.other, bf16[4,26,128,128]{3,2,1,0:T(8,128)(2,1)S(1)} %copy-done), custom_call_target="tpu_custom_call" | custom-call | flops 872415232 | bytes 5505024 | tf_op jit(solution)/shard_map/pallas_call | solution.py:210
  79.1 2.5 %collective-permute-start.5 = (f32[4,256]{1,0:T(4,128)S(1)}, f32[4,256]{1,0:T(4,128)S(1)}, u32[]{:S(2)}, u32[]{:S(2)}) collective-permute-start(f32[4,256]{1,0:T(4,128)S(1)} %shard_map.77), channel_id=1, source_target_pairs={{0,1},{1,0},{2,3},{3,2},{4,5},{5,4},{6,7},{7,6},{8,9},{9,8},{10,11... | collective-permute-start | bytes 12296 | tf_op jit(solution)/shard_map/ppermute | solution.py:309
  81.6 1.5 %collective-permute-done.5 = f32[4,256]{1,0:T(4,128)S(1)} collective-permute-done((f32[4,256]{1,0:T(4,128)S(1)}, f32[4,256]{1,0:T(4,128)S(1)}, u32[]{:S(2)}, u32[]{:S(2)}) %collective-permute-start.5) | collective-permute-done | bytes 4128 | tf_op jit(solution)/shard_map/ppermute | solution.py:309
  83.2 0.6 add.11
Async XLA Ops:
  0.8 1.5 %copy-start.1 = (f32[64,26,256]{2,0,1:T(8,128)S(1)}, f32[64,26,256]{2,0,1:T(8,128)}, u32[]{:S(2)}) copy-start(f32[64,26,256]{2,0,1:T(8,128)} %param.12) | copy-start | bytes 5111812
  2.3 0.7 copy-start.2
  15.2 5.6 %collective-permute-start = (s16[16,128,256]{2,1,0:T(8,128)(2,1)S(1)}, s16[16,128,256]{2,1,0:T(8,128)(2,1)S(1)}, u32[]{:S(2)}, u32[]{:S(2)}) collective-permute-start(s16[16,128,256]{2,1,0:T(8,128)(2,1)S(1)} %get-tuple-element.10), channel_id=1, source_target_pairs={{0,2},{2,0},{1,3},{3,1},{4,6},{6,4},{5,7},{7,5},{8,10},{10,8},{9,1... | collective-permute-start | bytes 3145736 | tf_op jit(solution)/shard_map/ppermute | solution.py:279
  21.5 55.3 %copy-start = (bf16[4,26,128,128]{3,2,1,0:T(8,128)(2,1)S(1)}, bf16[4,26,128,128]{3,2,1,0:T(8,128)(2,1)}, u32[]{:S(2)}) copy-start(bf16[4,26,128,128]{3,2,1,0:T(8,128)(2,1)} %wigner.1) | copy-start | bytes 10223620
  40.4 8.5 %collective-permute-start.3 = (s16[128,256]{1,0:T(8,128)(2,1)S(1)}, s16[128,256]{1,0:T(8,128)(2,1)S(1)}, u32[]{:S(2)}, u32[]{:S(2)}) collective-permute-start(s16[128,256]{1,0:T(8,128)(2,1)S(1)} %get-tuple-element.12), channel_id=1, source_target_pairs={{0,16},{8,24},{16,0},{24,8},{1,17},{9,25},{17,1},{25,9},{2,18},{10... | collective-permute-start | bytes 196616 | tf_op jit(solution)/shard_map/ppermute | solution.py:298
  46.5 4.8 %collective-permute-start.2 = (s16[128,256]{1,0:T(8,128)(2,1)S(1)}, s16[128,256]{1,0:T(8,128)(2,1)S(1)}, u32[]{:S(2)}, u32[]{:S(2)}) collective-permute-start(s16[128,256]{1,0:T(8,128)(2,1)S(1)} %get-tuple-element.12), channel_id=1, source_target_pairs={{0,24},{8,0},{16,8},{24,16},{1,25},{9,1},{17,9},{25,17},{2,26},{10... | collective-permute-start | bytes 196616 | tf_op jit(solution)/shard_map/ppermute | solution.py:298
  46.8 5.3 %collective-permute-start.1 = (s16[128,256]{1,0:T(8,128)(2,1)S(1)}, s16[128,256]{1,0:T(8,128)(2,1)S(1)}, u32[]{:S(2)}, u32[]{:S(2)}) collective-permute-start(s16[128,256]{1,0:T(8,128)(2,1)S(1)} %get-tuple-element.12), channel_id=1, source_target_pairs={{0,8},{8,16},{16,24},{24,0},{1,9},{9,17},{17,25},{25,1},{2,10},{10... | collective-permute-start | bytes 196616 | tf_op jit(solution)/shard_map/ppermute | solution.py:298
  69.9 6.9 %collective-permute-start.4 = (bf16[16,128,256]{2,1,0:T(8,128)(2,1)S(1)}, bf16[16,128,256]{2,1,0:T(8,128)(2,1)S(1)}, u32[]{:S(2)}, u32[]{:S(2)}) collective-permute-start(bf16[16,128,256]{2,1,0:T(8,128)(2,1)S(1)} %all_to_all.11.mine), channel_id=1, source_target_pairs={{0,2},{2,0},{1,3},{3,1},{4,6},{6,4},{5,7},{7,5},{8,10},{10,8},{9,1... | collective-permute-start | bytes 3145736 | tf_op jit(solution)/shard_map/ppermute | solution.py:307
  79.1 4.0 %collective-permute-start.5 = (f32[4,256]{1,0:T(4,128)S(1)}, f32[4,256]{1,0:T(4,128)S(1)}, u32[]{:S(2)}, u32[]{:S(2)}) collective-permute-start(f32[4,256]{1,0:T(4,128)S(1)} %shard_map.77), channel_id=1, source_target_pairs={{0,1},{1,0},{2,3},{3,2},{4,5},{5,4},{6,7},{7,6},{8,9},{9,8},{10,11... | collective-permute-start | bytes 12296 | tf_op jit(solution)/shard_map/ppermute | solution.py:309

commit v9 on v8

--- a/solution.py
+++ b/solution.py
@@ -236,10 +236,14 @@
     code[...] = coded(acc)
 
 
-def whole_kernel(total, after, before, across, out):
-    acc = total[...] + decoded(across[...])
-    acc = acc + (decoded(after[...]) + decoded(before[...]))
-    block = acc.astype(jnp.bfloat16)
+def pair_kernel(part, recv, total, code):
+    acc = part[...] + decoded(recv[...])
+    total[...] = acc
+    code[...] = coded(acc)
+
+
+def whole_kernel(part, recv, out):
+    block = (part[...] + decoded(recv[...])).astype(jnp.bfloat16)
     for i in range(out.shape[0]):
         out[i] = block
 
@@ -286,22 +290,20 @@
         recv,
     )
     near = lax.all_to_all(near, NEAR, 0, 0)
-    part, code = whole_call(
-        plane_kernel,
-        [
-            jax.ShapeDtypeStruct((height, qcount), jnp.float32),
-            jax.ShapeDtypeStruct(coded_shape, jnp.int16),
-        ],
-        LIMIT,
-        near,
-    )
-    turns = [lax.ppermute(code, FAR, [(i, (i + k) % 4) for i in range(4)]) for k in (1, 3, 2)]
+    shapes = [
+        jax.ShapeDtypeStruct((height, qcount), jnp.float32),
+        jax.ShapeDtypeStruct(coded_shape, jnp.int16),
+    ]
+    part, code = whole_call(plane_kernel, shapes, LIMIT, near)
+    code = lax.ppermute(code, FAR, [(0, 1), (1, 0), (2, 3), (3, 2)])
+    part, code = whole_call(pair_kernel, shapes, LIMIT, part, code)
+    code = lax.ppermute(code, FAR, [(1, 2), (2, 1), (3, 0), (0, 3)])
     spread = whole_call(
         whole_kernel,
         jax.ShapeDtypeStruct((PLANE, height, qcount), jnp.bfloat16),
         LIMIT,
         part,
-        *turns,
+        code,
     )
     mine = lax.all_to_all(spread, NEAR, 0, 0)
     other = lax.ppermute(mine, "c", swap)

time: 84 us -> 83.2 us (level)
  blocking collectives: 36.2 us -> 34.4 us
    all_to_all x1, blocking collectives: 17.7 us -> 15.8 us  [per_device(): mine = lax.all_to_all(spread, NEAR, 0, 0)]
    ppermute x1, starting transfers between devices: 4.65 us -> 6.27 us  [per_device(): other = lax.ppermute(mine, 'c', swap)]
    ppermute x3 -> x2, starting transfers between devices: 8.47 us -> 7.67 us  [the longest x1 4.58 us: per_device(): code = lax.ppermute(code, FAR, [(1, 2), (2, 1), (3, 0), (0, 3)])]
    ppermute x3 -> x2, waiting for transfers between devices: 3.18 us -> 3.31 us  [the longest x1 1.66 us: per_device(): code = lax.ppermute(code, FAR, [(0, 1), (1, 0), (2, 3), (3, 2)])]
  transfers between devices with their start and end apart: 6 -> 5, of which waited for: 5 -> 5; matrix products, arithmetic and copies ran while one was open for 0% -> 0% of each run, Pallas kernels for 0% -> 0%
where the time goes in v9:
time: 83.2 us; the launch traced here: 82.9 us
  blocking collectives  34.4 us (41%)
  starting transfers between devices  19.8 us (24%)
  Pallas kernels  15.7 us (19%)
  waiting for transfers between devices  9.4 us (11%)
  local copies, waits for them, and re-layouts  2.16 us (3%)
  other arithmetic  1.4 us (2%)
    all_to_all x1, blocking collectives, per_device(): near = lax.all_to_all(near, NEAR, 0, 0)  18.5 us
    all_to_all x1, blocking collectives, per_device(): mine = lax.all_to_all(spread, NEAR, 0, 0)  15.8 us
    pallas_call x1, Pallas kernels, local_amplitude(): pl.pallas_call(functools.partial(amplitude_kernel, scale, rows, thin), in...  12.2 us
    ppermute x1, starting transfers between devices, per_device(): other = lax.ppermute(mine, 'c', swap)  6.27 us
    ppermute x1, starting transfers between devices, per_device(): code = lax.ppermute(code, FAR, [(1, 2), (2, 1), (3, 0), (0, 3)])  4.58 us
    ppermute x1, starting transfers between devices, per_device(): recv = lax.ppermute(give, 'c', swap)  3.33 us
    ppermute x1, starting transfers between devices, per_device(): code = lax.ppermute(code, FAR, [(0, 1), (1, 0), (2, 3), (3, 2)])  3.09 us
    ppermute x1, starting transfers between devices, per_device(): return out + lax.ppermute(out, 'deg', swap)  2.53 us
  transfers between devices with their start and end apart: 5, of which 5 were waited for; matrix products, arithmetic and copies ran while one was open for 0% of the time, Pallas kernels for 0%

profile of v9, /device:TPU:1, one launch (start us, length us, event | category | flops | bytes accessed | tf_op | source)
XLA Modules:
  0.0 82.9 jit_solution(10215418820060555518)
XLA Ops:
  0.0 0.1 pad_add_fusion.place
  0.1 0.7 fusion.3
  0.8 0.0 copy-start.1
  0.8 1.5 %copy-done.1 = f32[64,26,256]{2,0,1:T(8,128)S(1)} copy-done((f32[64,26,256]{2,0,1:T(8,128)S(1)}, f32[64,26,256]{2,0,1:T(8,128)}, u32[]{:S(2)}) %copy-start.1) | copy-done | bytes 1703960
  2.3 0.0 copy-start.2
  2.3 0.7 copy-done.2
  3.0 12.2 %shard_map.73 = (f32[2048,256]{1,0:T(8,128)S(1)}, s16[16,128,256]{2,1,0:T(8,128)(2,1)S(1)}) custom-call(s32[2]{0:T(128)S(1)} %pad_add_fusion.place, s32[1,1024]{1,0:T(1,128)S(1)} %bitcast.5, bf16[26,1024,128]{2,1,0:T(8,128)(2,1)} %bitcast.7, f32[26,64,256]{2,1,0:T(8,128)S(1)} %bitcast.6, f32[8,256]{1,0:T(8,128)S(1)} %copy-done.2), custom_call_target="tpu_custom_call" | custom-call | flops 8220835840 | bytes 8519680 | tf_op jit(solution)/shard_map/pallas_call | solution.py:135
  15.2 3.3 %collective-permute-start = (s16[16,128,256]{2,1,0:T(8,128)(2,1)S(1)}, s16[16,128,256]{2,1,0:T(8,128)(2,1)S(1)}, u32[]{:S(2)}, u32[]{:S(2)}) collective-permute-start(s16[16,128,256]{2,1,0:T(8,128)(2,1)S(1)} %get-tuple-element.12), channel_id=1, source_target_pairs={{0,2},{2,0},{1,3},{3,1},{4,6},{6,4},{5,7},{7,5},{8,10},{10,8},{9,1... | collective-permute-start | bytes 3145736 | tf_op jit(solution)/shard_map/ppermute | solution.py:283
  18.5 2.3 %collective-permute-done.recv = s16[16,128,256]{2,1,0:T(8,128)(2,1)S(1)} collective-permute-done((s16[16,128,256]{2,1,0:T(8,128)(2,1)S(1)}, s16[16,128,256]{2,1,0:T(8,128)(2,1)S(1)}, u32[]{:S(2)}, u32[]{:S(2)}) %collective-permute-start) | collective-permute-done | bytes 1048608 | tf_op jit(solution)/shard_map/ppermute | solution.py:283
  20.8 0.7 shard_map.74
  21.5 0.0 copy-start
  21.5 18.5 %all_to_all.10.near = s16[16,128,256]{2,1,0:T(8,128)(2,1)S(1)} all-to-all(s16[16,128,256]{2,1,0:T(8,128)(2,1)S(1)} %shard_map.74), channel_id=1, replica_groups=mesh['y'=4,'xl'=2,'zh'=4,'zl'=2,'c'=2,'deg'=2] {'y','xl','zl'}, dimensions={0} | all-to-all | bytes 2097152 | tf_op jit(solution)/shard_map/all_to_all | solution.py:292
  40.0 0.3 shard_map.75
  40.4 3.1 %collective-permute-start.1 = (s16[128,256]{1,0:T(8,128)(2,1)S(1)}, s16[128,256]{1,0:T(8,128)(2,1)S(1)}, u32[]{:S(2)}, u32[]{:S(2)}) collective-permute-start(s16[128,256]{1,0:T(8,128)(2,1)S(1)} %get-tuple-element.14), channel_id=1, source_target_pairs={{0,8},{8,0},{16,24},{24,16},{1,9},{9,1},{17,25},{25,17},{2,10},{10... | collective-permute-start | bytes 196616 | tf_op jit(solution)/shard_map/ppermute | solution.py:298
  43.5 1.7 %collective-permute-done.1.recv = s16[128,256]{1,0:T(8,128)(2,1)S(1)} collective-permute-done((s16[128,256]{1,0:T(8,128)(2,1)S(1)}, s16[128,256]{1,0:T(8,128)(2,1)S(1)}, u32[]{:S(2)}, u32[]{:S(2)}) %collective-permute-start.1) | collective-permute-done | bytes 65568 | tf_op jit(solution)/shard_map/ppermute | solution.py:298
  45.1 0.1 shard_map.76
  45.2 4.6 %collective-permute-start.2 = (s16[128,256]{1,0:T(8,128)(2,1)S(1)}, s16[128,256]{1,0:T(8,128)(2,1)S(1)}, u32[]{:S(2)}, u32[]{:S(2)}) collective-permute-start(s16[128,256]{1,0:T(8,128)(2,1)S(1)} %get-tuple-element.16), channel_id=1, source_target_pairs={{8,16},{16,8},{24,0},{0,24},{9,17},{17,9},{25,1},{1,25},{10,18},{1... | collective-permute-start | bytes 196616 | tf_op jit(solution)/shard_map/ppermute | solution.py:300
  49.8 1.7 %collective-permute-done.2.recv = s16[128,256]{1,0:T(8,128)(2,1)S(1)} collective-permute-done((s16[128,256]{1,0:T(8,128)(2,1)S(1)}, s16[128,256]{1,0:T(8,128)(2,1)S(1)}, u32[]{:S(2)}, u32[]{:S(2)}) %collective-permute-start.2) | collective-permute-done | bytes 65568 | tf_op jit(solution)/shard_map/ppermute | solution.py:300
  51.4 0.1 shard_map.77
  51.5 15.8 %all_to_all.11.mine = bf16[16,128,256]{2,1,0:T(8,128)(2,1)S(1)} all-to-all(bf16[16,128,256]{2,1,0:T(8,128)(2,1)S(1)} %shard_map.77), channel_id=1, replica_groups=mesh['y'=4,'xl'=2,'zh'=4,'zl'=2,'c'=2,'deg'=2] {'y','xl','zl'}, dimensions={0} | all-to-all | bytes 2097152 | tf_op jit(solution)/shard_map/all_to_all | solution.py:308
  67.4 6.3 %collective-permute-start.3 = (bf16[16,128,256]{2,1,0:T(8,128)(2,1)S(1)}, bf16[16,128,256]{2,1,0:T(8,128)(2,1)S(1)}, u32[]{:S(2)}, u32[]{:S(2)}) collective-permute-start(bf16[16,128,256]{2,1,0:T(8,128)(2,1)S(1)} %all_to_all.11.mine), channel_id=1, source_target_pairs={{0,2},{2,0},{1,3},{3,1},{4,6},{6,4},{5,7},{7,5},{8,10},{10,8},{9,1... | collective-permute-start | bytes 3145736 | tf_op jit(solution)/shard_map/ppermute | solution.py:309
  73.6 2.3 %collective-permute-done.3.other = bf16[16,128,256]{2,1,0:T(8,128)(2,1)S(1)} collective-permute-done((bf16[16,128,256]{2,1,0:T(8,128)(2,1)S(1)}, bf16[16,128,256]{2,1,0:T(8,128)(2,1)S(1)}, u32[]{:S(2)}, u32[]{:S(2)}) %collective-permute-start.3) | collective-permute-done | bytes 1048608 | tf_op jit(solution)/shard_map/ppermute | solution.py:309
  75.9 0.0 copy-done
  75.9 2.3 %shard_map.78 = f32[4,256]{1,0:T(4,128)S(1)} custom-call(s32[2]{0:T(128)S(1)} %pad_add_fusion.place, bf16[16,128,256]{2,1,0:T(8,128)(2,1)S(1)} %all_to_all.11.mine, bf16[16,128,256]{2,1,0:T(8,128)(2,1)S(1)} %collective-permute-done.3.other, bf16[4,26,128,128]{3,2,1,0:T(8,128)(2,1)S(1)} %copy-done), custom_call_target="tpu_custom_call" | custom-call | flops 872415232 | bytes 5505024 | tf_op jit(solution)/shard_map/pallas_call | solution.py:210
  78.2 2.5 %collective-permute-start.4 = (f32[4,256]{1,0:T(4,128)S(1)}, f32[4,256]{1,0:T(4,128)S(1)}, u32[]{:S(2)}, u32[]{:S(2)}) collective-permute-start(f32[4,256]{1,0:T(4,128)S(1)} %shard_map.78), channel_id=1, source_target_pairs={{0,1},{1,0},{2,3},{3,2},{4,5},{5,4},{6,7},{7,6},{8,9},{9,8},{10,11... | collective-permute-start | bytes 12296 | tf_op jit(solution)/shard_map/ppermute | solution.py:311
  80.8 1.5 %collective-permute-done.4 = f32[4,256]{1,0:T(4,128)S(1)} collective-permute-done((f32[4,256]{1,0:T(4,128)S(1)}, f32[4,256]{1,0:T(4,128)S(1)}, u32[]{:S(2)}, u32[]{:S(2)}) %collective-permute-start.4) | collective-permute-done | bytes 4128 | tf_op jit(solution)/shard_map/ppermute | solution.py:311
  82.3 0.6 add.11
Async XLA Ops:
  0.8 1.5 %copy-start.1 = (f32[64,26,256]{2,0,1:T(8,128)S(1)}, f32[64,26,256]{2,0,1:T(8,128)}, u32[]{:S(2)}) copy-start(f32[64,26,256]{2,0,1:T(8,128)} %param.12) | copy-start | bytes 5111812
  2.3 0.7 copy-start.2
  15.2 5.6 %collective-permute-start = (s16[16,128,256]{2,1,0:T(8,128)(2,1)S(1)}, s16[16,128,256]{2,1,0:T(8,128)(2,1)S(1)}, u32[]{:S(2)}, u32[]{:S(2)}) collective-permute-start(s16[16,128,256]{2,1,0:T(8,128)(2,1)S(1)} %get-tuple-element.12), channel_id=1, source_target_pairs={{0,2},{2,0},{1,3},{3,1},{4,6},{6,4},{5,7},{7,5},{8,10},{10,8},{9,1... | collective-permute-start | bytes 3145736 | tf_op jit(solution)/shard_map/ppermute | solution.py:283
  21.5 54.4 %copy-start = (bf16[4,26,128,128]{3,2,1,0:T(8,128)(2,1)S(1)}, bf16[4,26,128,128]{3,2,1,0:T(8,128)(2,1)}, u32[]{:S(2)}) copy-start(bf16[4,26,128,128]{3,2,1,0:T(8,128)(2,1)} %wigner.1) | copy-start | bytes 10223620
  40.4 4.7 %collective-permute-start.1 = (s16[128,256]{1,0:T(8,128)(2,1)S(1)}, s16[128,256]{1,0:T(8,128)(2,1)S(1)}, u32[]{:S(2)}, u32[]{:S(2)}) collective-permute-start(s16[128,256]{1,0:T(8,128)(2,1)S(1)} %get-tuple-element.14), channel_id=1, source_target_pairs={{0,8},{8,0},{16,24},{24,16},{1,9},{9,1},{17,25},{25,17},{2,10},{10... | collective-permute-start | bytes 196616 | tf_op jit(solution)/shard_map/ppermute | solution.py:298
  45.2 6.2 %collective-permute-start.2 = (s16[128,256]{1,0:T(8,128)(2,1)S(1)}, s16[128,256]{1,0:T(8,128)(2,1)S(1)}, u32[]{:S(2)}, u32[]{:S(2)}) collective-permute-start(s16[128,256]{1,0:T(8,128)(2,1)S(1)} %get-tuple-element.16), channel_id=1, source_target_pairs={{8,16},{16,8},{24,0},{0,24},{9,17},{17,9},{25,1},{1,25},{10,18},{1... | collective-permute-start | bytes 196616 | tf_op jit(solution)/shard_map/ppermute | solution.py:300
  67.4 8.6 %collective-permute-start.3 = (bf16[16,128,256]{2,1,0:T(8,128)(2,1)S(1)}, bf16[16,128,256]{2,1,0:T(8,128)(2,1)S(1)}, u32[]{:S(2)}, u32[]{:S(2)}) collective-permute-start(bf16[16,128,256]{2,1,0:T(8,128)(2,1)S(1)} %all_to_all.11.mine), channel_id=1, source_target_pairs={{0,2},{2,0},{1,3},{3,1},{4,6},{6,4},{5,7},{7,5},{8,10},{10,8},{9,1... | collective-permute-start | bytes 3145736 | tf_op jit(solution)/shard_map/ppermute | solution.py:309
  78.2 4.0 %collective-permute-start.4 = (f32[4,256]{1,0:T(4,128)S(1)}, f32[4,256]{1,0:T(4,128)S(1)}, u32[]{:S(2)}, u32[]{:S(2)}) collective-permute-start(f32[4,256]{1,0:T(4,128)S(1)} %shard_map.78), channel_id=1, source_target_pairs={{0,1},{1,0},{2,3},{3,2},{4,5},{5,4},{6,7},{7,6},{8,9},{9,8},{10,11... | collective-permute-start | bytes 12296 | tf_op jit(solution)/shard_map/ppermute | solution.py:311

commit v10 on v9

--- a/solution.py
+++ b/solution.py
@@ -108,7 +108,7 @@
             away[at, :] = other[done : done + count]
             done += count
 
-    cuts = [(0, 5), (6, 13), (14, 21), (22, degs - 1)]
+    cuts = [(0, 2), (3, 9), (10, 17), (18, degs - 1)]
     for first, last in cuts:
         for copy in fetch[first : last + 1]:
             copy.wait()

time: 83.2 us -> 82.9 us (level)
  no operation moved by 1% of the time
where the time goes in v10:
time: 82.9 us; the launch traced here: 82.7 us
  blocking collectives  34.4 us (41%)
  starting transfers between devices  19.8 us (24%)
  Pallas kernels  15.5 us (19%)
  waiting for transfers between devices  9.39 us (11%)
  local copies, waits for them, and re-layouts  2.16 us (3%)
  other arithmetic  1.4 us (2%)
    all_to_all x1, blocking collectives, per_device(): near = lax.all_to_all(near, NEAR, 0, 0)  18.5 us
    all_to_all x1, blocking collectives, per_device(): mine = lax.all_to_all(spread, NEAR, 0, 0)  15.8 us
    pallas_call x1, Pallas kernels, local_amplitude(): pl.pallas_call(functools.partial(amplitude_kernel, scale, rows, thin), in...  12 us
    ppermute x1, starting transfers between devices, per_device(): other = lax.ppermute(mine, 'c', swap)  6.27 us
    ppermute x1, starting transfers between devices, per_device(): code = lax.ppermute(code, FAR, [(1, 2), (2, 1), (3, 0), (0, 3)])  4.58 us
    ppermute x1, starting transfers between devices, per_device(): recv = lax.ppermute(give, 'c', swap)  3.33 us
    ppermute x1, starting transfers between devices, per_device(): code = lax.ppermute(code, FAR, [(0, 1), (1, 0), (2, 3), (3, 2)])  3.08 us
    ppermute x1, starting transfers between devices, per_device(): return out + lax.ppermute(out, 'deg', swap)  2.54 us
  transfers between devices with their start and end apart: 5, of which 5 were waited for; matrix products, arithmetic and copies ran while one was open for 0% of the time, Pallas kernels for 0%

profile of v10, /device:TPU:1, one launch (start us, length us, event | category | flops | bytes accessed | tf_op | source)
XLA Modules:
  0.0 82.7 jit_solution(5436060042675330793)
XLA Ops:
  0.0 0.1 pad_add_fusion.place
  0.1 0.7 fusion.3
  0.8 0.0 copy-start.1
  0.8 1.5 %copy-done.1 = f32[64,26,256]{2,0,1:T(8,128)S(1)} copy-done((f32[64,26,256]{2,0,1:T(8,128)S(1)}, f32[64,26,256]{2,0,1:T(8,128)}, u32[]{:S(2)}) %copy-start.1) | copy-done | bytes 1703960
  2.3 0.0 copy-start.2
  2.3 0.7 copy-done.2
  3.0 12.0 %shard_map.73 = (f32[2048,256]{1,0:T(8,128)S(1)}, s16[16,128,256]{2,1,0:T(8,128)(2,1)S(1)}) custom-call(s32[2]{0:T(128)S(1)} %pad_add_fusion.place, s32[1,1024]{1,0:T(1,128)S(1)} %bitcast.5, bf16[26,1024,128]{2,1,0:T(8,128)(2,1)} %bitcast.7, f32[26,64,256]{2,1,0:T(8,128)S(1)} %bitcast.6, f32[8,256]{1,0:T(8,128)S(1)} %copy-done.2), custom_call_target="tpu_custom_call" | custom-call | flops 8220835840 | bytes 8519680 | tf_op jit(solution)/shard_map/pallas_call | solution.py:135
  15.0 3.3 %collective-permute-start = (s16[16,128,256]{2,1,0:T(8,128)(2,1)S(1)}, s16[16,128,256]{2,1,0:T(8,128)(2,1)S(1)}, u32[]{:S(2)}, u32[]{:S(2)}) collective-permute-start(s16[16,128,256]{2,1,0:T(8,128)(2,1)S(1)} %get-tuple-element.12), channel_id=1, source_target_pairs={{0,2},{2,0},{1,3},{3,1},{4,6},{6,4},{5,7},{7,5},{8,10},{10,8},{9,1... | collective-permute-start | bytes 3145736 | tf_op jit(solution)/shard_map/ppermute | solution.py:283
  18.3 2.3 %collective-permute-done.recv = s16[16,128,256]{2,1,0:T(8,128)(2,1)S(1)} collective-permute-done((s16[16,128,256]{2,1,0:T(8,128)(2,1)S(1)}, s16[16,128,256]{2,1,0:T(8,128)(2,1)S(1)}, u32[]{:S(2)}, u32[]{:S(2)}) %collective-permute-start) | collective-permute-done | bytes 1048608 | tf_op jit(solution)/shard_map/ppermute | solution.py:283
  20.6 0.7 shard_map.74
  21.3 0.0 copy-start
  21.3 18.5 %all_to_all.10.near = s16[16,128,256]{2,1,0:T(8,128)(2,1)S(1)} all-to-all(s16[16,128,256]{2,1,0:T(8,128)(2,1)S(1)} %shard_map.74), channel_id=1, replica_groups=mesh['y'=4,'xl'=2,'zh'=4,'zl'=2,'c'=2,'deg'=2] {'y','xl','zl'}, dimensions={0} | all-to-all | bytes 2097152 | tf_op jit(solution)/shard_map/all_to_all | solution.py:292
  39.8 0.3 shard_map.75
  40.2 3.1 %collective-permute-start.1 = (s16[128,256]{1,0:T(8,128)(2,1)S(1)}, s16[128,256]{1,0:T(8,128)(2,1)S(1)}, u32[]{:S(2)}, u32[]{:S(2)}) collective-permute-start(s16[128,256]{1,0:T(8,128)(2,1)S(1)} %get-tuple-element.14), channel_id=1, source_target_pairs={{0,8},{8,0},{16,24},{24,16},{1,9},{9,1},{17,25},{25,17},{2,10},{10... | collective-permute-start | bytes 196616 | tf_op jit(solution)/shard_map/ppermute | solution.py:298
  43.2 1.7 %collective-permute-done.1.recv = s16[128,256]{1,0:T(8,128)(2,1)S(1)} collective-permute-done((s16[128,256]{1,0:T(8,128)(2,1)S(1)}, s16[128,256]{1,0:T(8,128)(2,1)S(1)}, u32[]{:S(2)}, u32[]{:S(2)}) %collective-permute-start.1) | collective-permute-done | bytes 65568 | tf_op jit(solution)/shard_map/ppermute | solution.py:298
  44.9 0.1 shard_map.76
  45.0 4.6 %collective-permute-start.2 = (s16[128,256]{1,0:T(8,128)(2,1)S(1)}, s16[128,256]{1,0:T(8,128)(2,1)S(1)}, u32[]{:S(2)}, u32[]{:S(2)}) collective-permute-start(s16[128,256]{1,0:T(8,128)(2,1)S(1)} %get-tuple-element.16), channel_id=1, source_target_pairs={{8,16},{16,8},{24,0},{0,24},{9,17},{17,9},{25,1},{1,25},{10,18},{1... | collective-permute-start | bytes 196616 | tf_op jit(solution)/shard_map/ppermute | solution.py:300
  49.5 1.7 %collective-permute-done.2.recv = s16[128,256]{1,0:T(8,128)(2,1)S(1)} collective-permute-done((s16[128,256]{1,0:T(8,128)(2,1)S(1)}, s16[128,256]{1,0:T(8,128)(2,1)S(1)}, u32[]{:S(2)}, u32[]{:S(2)}) %collective-permute-start.2) | collective-permute-done | bytes 65568 | tf_op jit(solution)/shard_map/ppermute | solution.py:300
  51.2 0.1 shard_map.77
  51.3 15.8 %all_to_all.11.mine = bf16[16,128,256]{2,1,0:T(8,128)(2,1)S(1)} all-to-all(bf16[16,128,256]{2,1,0:T(8,128)(2,1)S(1)} %shard_map.77), channel_id=1, replica_groups=mesh['y'=4,'xl'=2,'zh'=4,'zl'=2,'c'=2,'deg'=2] {'y','xl','zl'}, dimensions={0} | all-to-all | bytes 2097152 | tf_op jit(solution)/shard_map/all_to_all | solution.py:308
  67.1 6.3 %collective-permute-start.3 = (bf16[16,128,256]{2,1,0:T(8,128)(2,1)S(1)}, bf16[16,128,256]{2,1,0:T(8,128)(2,1)S(1)}, u32[]{:S(2)}, u32[]{:S(2)}) collective-permute-start(bf16[16,128,256]{2,1,0:T(8,128)(2,1)S(1)} %all_to_all.11.mine), channel_id=1, source_target_pairs={{0,2},{2,0},{1,3},{3,1},{4,6},{6,4},{5,7},{7,5},{8,10},{10,8},{9,1... | collective-permute-start | bytes 3145736 | tf_op jit(solution)/shard_map/ppermute | solution.py:309
  73.4 2.3 %collective-permute-done.3.other = bf16[16,128,256]{2,1,0:T(8,128)(2,1)S(1)} collective-permute-done((bf16[16,128,256]{2,1,0:T(8,128)(2,1)S(1)}, bf16[16,128,256]{2,1,0:T(8,128)(2,1)S(1)}, u32[]{:S(2)}, u32[]{:S(2)}) %collective-permute-start.3) | collective-permute-done | bytes 1048608 | tf_op jit(solution)/shard_map/ppermute | solution.py:309
  75.7 0.0 copy-done
  75.7 2.3 %shard_map.78 = f32[4,256]{1,0:T(4,128)S(1)} custom-call(s32[2]{0:T(128)S(1)} %pad_add_fusion.place, bf16[16,128,256]{2,1,0:T(8,128)(2,1)S(1)} %all_to_all.11.mine, bf16[16,128,256]{2,1,0:T(8,128)(2,1)S(1)} %collective-permute-done.3.other, bf16[4,26,128,128]{3,2,1,0:T(8,128)(2,1)S(1)} %copy-done), custom_call_target="tpu_custom_call" | custom-call | flops 872415232 | bytes 5505024 | tf_op jit(solution)/shard_map/pallas_call | solution.py:210
  78.0 2.5 %collective-permute-start.4 = (f32[4,256]{1,0:T(4,128)S(1)}, f32[4,256]{1,0:T(4,128)S(1)}, u32[]{:S(2)}, u32[]{:S(2)}) collective-permute-start(f32[4,256]{1,0:T(4,128)S(1)} %shard_map.78), channel_id=1, source_target_pairs={{0,1},{1,0},{2,3},{3,2},{4,5},{5,4},{6,7},{7,6},{8,9},{9,8},{10,11... | collective-permute-start | bytes 12296 | tf_op jit(solution)/shard_map/ppermute | solution.py:311
  80.5 1.5 %collective-permute-done.4 = f32[4,256]{1,0:T(4,128)S(1)} collective-permute-done((f32[4,256]{1,0:T(4,128)S(1)}, f32[4,256]{1,0:T(4,128)S(1)}, u32[]{:S(2)}, u32[]{:S(2)}) %collective-permute-start.4) | collective-permute-done | bytes 4128 | tf_op jit(solution)/shard_map/ppermute | solution.py:311
  82.1 0.6 add.11
Async XLA Ops:
  0.8 1.5 %copy-start.1 = (f32[64,26,256]{2,0,1:T(8,128)S(1)}, f32[64,26,256]{2,0,1:T(8,128)}, u32[]{:S(2)}) copy-start(f32[64,26,256]{2,0,1:T(8,128)} %param.12) | copy-start | bytes 5111812
  2.3 0.7 copy-start.2
  15.0 5.6 %collective-permute-start = (s16[16,128,256]{2,1,0:T(8,128)(2,1)S(1)}, s16[16,128,256]{2,1,0:T(8,128)(2,1)S(1)}, u32[]{:S(2)}, u32[]{:S(2)}) collective-permute-start(s16[16,128,256]{2,1,0:T(8,128)(2,1)S(1)} %get-tuple-element.12), channel_id=1, source_target_pairs={{0,2},{2,0},{1,3},{3,1},{4,6},{6,4},{5,7},{7,5},{8,10},{10,8},{9,1... | collective-permute-start | bytes 3145736 | tf_op jit(solution)/shard_map/ppermute | solution.py:283
  21.3 54.4 %copy-start = (bf16[4,26,128,128]{3,2,1,0:T(8,128)(2,1)S(1)}, bf16[4,26,128,128]{3,2,1,0:T(8,128)(2,1)}, u32[]{:S(2)}) copy-start(bf16[4,26,128,128]{3,2,1,0:T(8,128)(2,1)} %wigner.1) | copy-start | bytes 10223620
  40.2 4.7 %collective-permute-start.1 = (s16[128,256]{1,0:T(8,128)(2,1)S(1)}, s16[128,256]{1,0:T(8,128)(2,1)S(1)}, u32[]{:S(2)}, u32[]{:S(2)}) collective-permute-start(s16[128,256]{1,0:T(8,128)(2,1)S(1)} %get-tuple-element.14), channel_id=1, source_target_pairs={{0,8},{8,0},{16,24},{24,16},{1,9},{9,1},{17,25},{25,17},{2,10},{10... | collective-permute-start | bytes 196616 | tf_op jit(solution)/shard_map/ppermute | solution.py:298
  45.0 6.2 %collective-permute-start.2 = (s16[128,256]{1,0:T(8,128)(2,1)S(1)}, s16[128,256]{1,0:T(8,128)(2,1)S(1)}, u32[]{:S(2)}, u32[]{:S(2)}) collective-permute-start(s16[128,256]{1,0:T(8,128)(2,1)S(1)} %get-tuple-element.16), channel_id=1, source_target_pairs={{8,16},{16,8},{24,0},{0,24},{9,17},{17,9},{25,1},{1,25},{10,18},{1... | collective-permute-start | bytes 196616 | tf_op jit(solution)/shard_map/ppermute | solution.py:300
  67.1 8.6 %collective-permute-start.3 = (bf16[16,128,256]{2,1,0:T(8,128)(2,1)S(1)}, bf16[16,128,256]{2,1,0:T(8,128)(2,1)S(1)}, u32[]{:S(2)}, u32[]{:S(2)}) collective-permute-start(bf16[16,128,256]{2,1,0:T(8,128)(2,1)S(1)} %all_to_all.11.mine), channel_id=1, source_target_pairs={{0,2},{2,0},{1,3},{3,1},{4,6},{6,4},{5,7},{7,5},{8,10},{10,8},{9,1... | collective-permute-start | bytes 3145736 | tf_op jit(solution)/shard_map/ppermute | solution.py:309
  78.0 4.0 %collective-permute-start.4 = (f32[4,256]{1,0:T(4,128)S(1)}, f32[4,256]{1,0:T(4,128)S(1)}, u32[]{:S(2)}, u32[]{:S(2)}) collective-permute-start(f32[4,256]{1,0:T(4,128)S(1)} %shard_map.78), channel_id=1, source_target_pairs={{0,1},{1,0},{2,3},{3,2},{4,5},{5,4},{6,7},{7,6},{8,9},{9,8},{10,11... | collective-permute-start | bytes 12296 | tf_op jit(solution)/shard_map/ppermute | solution.py:311
